TPU v7x, 128 devices: a whole 4x4x4 slice. The times are simulated.
128 devices in a mesh: dp: 4 (over y_hi, core), seq: 32 (over y_lo, x, z).
Axes of the slice: x: 4, y: 4 (y_hi: 2, y_lo: 2; y = y_hi * 2 + y_lo), z: 4, core: 2. Of those that a mesh axis runs over, the one named last changes fastest.
Arguments:
- conv_input: bfloat16 [4, 24576, 768], P('dp', 'seq'), may hold values from -6 to 6
- skip_grad: bfloat16 [4, 24576, 768], P('dp', 'seq'), may hold values from -3 to 3
- conv_weight: bfloat16 [5, 768, 768], replicated, may hold values from -0.09375 to 0.09375
- proj_weight: bfloat16 [768, 4608], replicated, may hold values from -1.75 to 1.75
- saved_query: bfloat16 [4, 1536, 1536], P('dp', 'seq'), may hold values from -6 to 6
- saved_key: bfloat16 [4, 1536, 1536], P('dp', 'seq'), may hold values from -6 to 6
- saved_value: bfloat16 [4, 1536, 1536], P('dp', 'seq'), may hold values from -6 to 6
- attn_grad: bfloat16 [4, 1536, 1536], P('dp', 'seq'), may hold values from -144 to 144
Outputs:
- input_grad: bfloat16 [4, 24576, 768], P('dp', 'seq')
- conv_grad: float32 [5, 768, 768], P(None, 'seq')
- proj_grad: float32 [768, 4608], P('seq')
All inputs are finite; a program needn't handle non-finite values.
Results may differ from a plain program's by a relative error of at most 0.0084.
Values may be sent and summed in bfloat16 or wider, within the bound.
No kernel may reach another device: no remote copies, remote signals or barrier semaphores. Data moves between devices by JAX's collectives and lax.ppermute only.
A program may use at most 192 MiB of HBM per device.

v0:
```python
import jax
import jax.numpy as jnp
from jax import lax
from jax.sharding import PartitionSpec as P

HEADS = 8
TAPS = 5
LOSS_SCALE = 32


SQRT_HALF = 0.7071067811865476
INV_ROOT_TWO_PI = 0.3989422804014327


def extended(x, sides, width):
    for axis, dim in sides:
        devices, length = (lax.axis_size(axis), x.shape[dim])
        up = [(i, (i + 1) % devices) for i in range(devices - 1)]
        down = [(j, i) for i, j in up]
        last = lax.slice_in_dim(x, length - width, length, axis=dim)
        leading = lax.slice_in_dim(x, 0, width, axis=dim)
        before = lax.ppermute(last, axis, up)
        after = lax.ppermute(leading, axis, down)
        x = jnp.concatenate([before, x, after], axis=dim)
    return x


def gelu_pair(preact):
    cumul = 0.5 * (1.0 + lax.erf(preact * SQRT_HALF))
    return (preact * cumul, cumul + preact * INV_ROOT_TWO_PI * jnp.exp(-0.5 * preact * preact))


def conv_apply(padded, weights, count):
    total = jnp.dot(padded[0:count], weights[0], preferred_element_type=jnp.float32)
    for offset in range(1, weights.shape[0]):
        total = total + jnp.dot(
            padded[offset : offset + count], weights[offset], preferred_element_type=jnp.float32
        )
    return total


def conv_adjoint(padded, weights, count, total):
    last_tap = weights.shape[0] - 1
    for offset in range(weights.shape[0]):
        start = last_tap - offset
        total = total + jnp.einsum(
            "ro,co->rc",
            padded[start : start + count],
            weights[offset],
            preferred_element_type=jnp.float32,
        )
    return total


def weight_terms(padded, grad_rows, count):
    return jnp.stack(
        [
            jnp.einsum(
                "rc,ro->co",
                padded[offset : offset + count],
                grad_rows,
                preferred_element_type=jnp.float32,
            )
            for offset in range(TAPS)
        ]
    )


def spread_columns(matrix, seq_count, dp_count):
    lead = matrix.shape[0]
    return matrix.reshape(lead, seq_count, dp_count, -1).swapaxes(1, 2).reshape(lead, -1)


def head_gradients(query, keyset, valueset, grad_out, score_scale):
    scores = (
        jnp.einsum("qd,kd->qk", query, keyset, preferred_element_type=jnp.float32) * score_scale
    )
    top = jnp.max(scores, axis=1, keepdims=True)
    powers = jnp.exp(scores - top)
    probs = powers / jnp.sum(powers, axis=1, keepdims=True)
    probs_low = probs.astype(jnp.bfloat16)
    output = jnp.dot(probs_low, valueset, preferred_element_type=jnp.float32)
    row_delta = jnp.sum(grad_out.astype(jnp.float32) * output, axis=1, keepdims=True)
    prob_grad = jnp.einsum("qd,kd->qk", grad_out, valueset, preferred_element_type=jnp.float32)
    score_grad = (probs * (prob_grad - row_delta)).astype(jnp.bfloat16)
    query_grad = jnp.dot(score_grad, keyset, preferred_element_type=jnp.float32) * score_scale
    key_grad = (
        jnp.einsum("qk,qd->kd", score_grad, query, preferred_element_type=jnp.float32) * score_scale
    )
    value_grad = jnp.einsum("qk,qd->kd", probs_low, grad_out, preferred_element_type=jnp.float32)
    return (query_grad, key_grad, value_grad)


def local(
    conv_input, skip_grad, conv_weight, proj_weight, saved_query, saved_key, saved_value, attn_grad
):
    seq_count = lax.axis_size("seq")
    dp_count = lax.axis_size("dp")
    rim_width = conv_weight.shape[0] // 2
    conv_rows = conv_input.shape[1]
    channels = conv_input.shape[2]
    att_rows = saved_query.shape[1]
    width = saved_query.shape[2]
    head_dim = width // HEADS
    groups = seq_count // HEADS
    sub_rows = att_rows // groups
    factor = conv_rows // att_rows
    score_scale = head_dim ** (-0.5)
    inputs = conv_input[0]
    padded = extended(inputs, (("seq", 0),), rim_width)
    preact = conv_apply(padded, conv_weight, conv_rows)
    act, slope = gelu_pair(preact)
    block_out = (inputs.astype(jnp.float32) + act).astype(jnp.bfloat16)
    pooled = jnp.mean(
        block_out.astype(jnp.float32).reshape(att_rows, factor, channels), axis=1
    ).astype(jnp.bfloat16)
    query_part = saved_query[0].reshape(att_rows, HEADS, head_dim)
    grad_part = attn_grad[0].reshape(att_rows, HEADS, head_dim)
    paired = jnp.concatenate([query_part, grad_part], axis=2)
    paired = (
        paired.reshape(groups, sub_rows, HEADS, 2 * head_dim)
        .transpose(2, 0, 1, 3)
        .reshape(seq_count, sub_rows * 2 * head_dim)
    )
    key_part = saved_key[0].reshape(att_rows, HEADS, head_dim)
    value_part = saved_value[0].reshape(att_rows, HEADS, head_dim)
    key_value = jnp.concatenate([key_part, value_part], axis=2).transpose(1, 0, 2)
    key_value = jnp.broadcast_to(
        key_value[:, None], (HEADS, groups, att_rows, 2 * head_dim)
    ).reshape(seq_count, att_rows, 2 * head_dim)
    got_rows, got_keys = (
        lax.all_to_all(paired, "seq", split_axis=0, concat_axis=0, tiled=True),
        lax.all_to_all(key_value, "seq", split_axis=0, concat_axis=0, tiled=True),
    )
    query_block = got_rows.reshape(seq_count * sub_rows, 2 * head_dim)
    key_block = got_keys.reshape(seq_count * att_rows, 2 * head_dim)
    query_grad, key_grad, value_grad = head_gradients(
        query_block[:, :head_dim],
        key_block[:, :head_dim],
        key_block[:, head_dim:],
        query_block[:, head_dim:],
        score_scale,
    )
    back_rows = query_grad.reshape(seq_count, sub_rows * head_dim)
    back_keys = jnp.concatenate([key_grad, value_grad], axis=1).reshape(
        seq_count, att_rows, 2 * head_dim
    )
    got_query, got_pairs = (
        lax.all_to_all(back_rows, "seq", split_axis=0, concat_axis=0, tiled=True),
        lax.all_to_all(back_keys, "seq", split_axis=0, concat_axis=0, tiled=True),
    )
    query_rows = (
        got_query.reshape(HEADS, groups, sub_rows, head_dim)
        .transpose(1, 2, 0, 3)
        .reshape(att_rows, width)
    )
    pair_sums = jnp.sum(got_pairs.reshape(HEADS, groups, att_rows, 2 * head_dim), axis=1)
    key_rows = pair_sums[:, :, :head_dim].transpose(1, 0, 2).reshape(att_rows, width)
    value_rows = pair_sums[:, :, head_dim:].transpose(1, 0, 2).reshape(att_rows, width)
    qkv_grad = jnp.concatenate([query_rows, key_rows, value_rows], axis=1).astype(jnp.bfloat16)
    pool_grad = jnp.einsum("rk,ck->rc", qkv_grad, proj_weight, preferred_element_type=jnp.float32)
    spread = jnp.broadcast_to(
        (pool_grad / factor)[:, None, :], (att_rows, factor, channels)
    ).reshape(conv_rows, channels)
    row_grad = skip_grad[0].astype(jnp.float32) + spread
    pre_grad = (row_grad * slope).astype(jnp.bfloat16)
    grad_pad = extended(pre_grad, (("seq", 0),), rim_width)
    input_grad = conv_adjoint(grad_pad, conv_weight, conv_rows, row_grad).astype(jnp.bfloat16)
    conv_term = weight_terms(spread_columns(padded, seq_count, dp_count), pre_grad, conv_rows)
    proj_term = jnp.einsum(
        "rc,rk->ck",
        spread_columns(pooled, seq_count, dp_count),
        qkv_grad,
        preferred_element_type=jnp.float32,
    )[None]
    shards = (
        lax.psum_scatter(conv_term, ("dp", "seq"), scatter_dimension=1, tiled=True),
        lax.psum_scatter(proj_term, ("dp", "seq"), scatter_dimension=1, tiled=True),
    )
    conv_part, proj_part = (
        lax.all_gather(shards[0], "dp", axis=1, tiled=True),
        lax.all_gather(shards[1], "dp", axis=1, tiled=True),
    )
    return (input_grad[None], conv_part / LOSS_SCALE, proj_part[0] / LOSS_SCALE)


def solution(mesh):
    placed = (
        P("dp", "seq", None),
        P("dp", "seq", None),
        P(),
        P(),
        P("dp", "seq", None),
        P("dp", "seq", None),
        P("dp", "seq", None),
        P("dp", "seq", None),
    )
    return jax.shard_map(
        local,
        mesh=mesh,
        in_specs=placed,
        out_specs=(P("dp", "seq", None), P(None, "seq", None), P("seq", None)),
        check_vma=False,
    )
```

profile of v0, /device:TPU:7, one launch (start us, length us, event | category | flops | bytes accessed | tf_op | source)
XLA Modules:
  0.0 497.6 jit_solution(18434963979330735548)
XLA Ops:
  10.4 2.4 reduce.3
  13.6 8.9 %all-to-all-start = ((bf16[32,2,2304]{2,1,0:T(2,128)(2,1)}), bf16[32,2,2304]{2,1,0:T(2,128)(2,1)S(1)}, u32[]{:S(2)}, u32[]{:S(2)}) async-start(bf16[32,2,2304]{2,1,0:T(2,128)(2,1)} %reshape.111), calls=%async_computation | async-start | bytes 589824 | tf_op jit(solution)/shard_map/all_to_all | solution.py:132
  23.0 6.6 %all-to-all-done = bf16[32,2,2304]{2,1,0:T(2,128)(2,1)S(1)} async-done(((bf16[32,2,2304]{2,1,0:T(2,128)(2,1)}), bf16[32,2,2304]{2,1,0:T(2,128)(2,1)S(1)}, u32[]{:S(2)}, u32[]{:S(2)}) %all-to-all-start) | async-done | bytes 294944 | tf_op jit(solution)/shard_map/all_to_all | solution.py:132
  30.8 5.1 %all-to-all-start.1 = ((bf16[32,48,384]{2,1,0:T(8,128)(2,1)}), bf16[32,48,384]{2,1,0:T(8,128)(2,1)S(1)}, u32[]{:S(2)}, u32[]{:S(2)}) async-start(bf16[32,48,384]{2,1,0:T(8,128)(2,1)} %bitcast.3), calls=%async_computation.1 | async-start | bytes 2359296 | tf_op jit(solution)/shard_map/all_to_all | solution.py:133
  35.9 4.6 collective-permute-start.1
  40.5 2.4 collective-permute-start
  45.6 5.9 %all-to-all-done.1 = bf16[32,48,384]{2,1,0:T(8,128)(2,1)S(1)} async-done(((bf16[32,48,384]{2,1,0:T(8,128)(2,1)}), bf16[32,48,384]{2,1,0:T(8,128)(2,1)S(1)}, u32[]{:S(2)}, u32[]{:S(2)}) %all-to-all-start.1) | async-done | bytes 1179680 | tf_op jit(solution)/shard_map/all_to_all | solution.py:133
  61.2 6.3 %all-to-all-start.2 = ((bf16[32,2,1152]{2,1,0:T(2,128)(2,1)}), bf16[32,2,1152]{2,1,0:T(2,128)(2,1)}, u32[]{:S(2)}, u32[]{:S(2)}) async-start(bf16[32,2,1152]{2,1,0:T(2,128)(2,1)} %reshape.113), calls=%async_computation.2 | async-start | bytes 294912 | tf_op jit(solution)/shard_map/all_to_all | solution.py:149
  71.3 2.4 all-to-all-done.2
  73.7 5.4 %all-to-all-start.3 = ((f32[32,48,384]{2,1,0:T(8,128)}), f32[32,48,384]{2,1,0:T(8,128)S(1)}, u32[]{:S(2)}, u32[]{:S(2)}) async-start(f32[32,48,384]{2,1,0:T(8,128)} %bitcast.6), calls=%async_computation.3 | async-start | bytes 4718592 | tf_op jit(solution)/shard_map/all_to_all | solution.py:150
  79.1 3.8 fusion.41
  84.5 3.2 concatenate.56
  88.5 2.4 copy.64
  91.7 2.4 copy.63
  94.1 2.5 maximum_bitcast_fusion
  96.6 4.0 fusion.82
  101.9 3.2 slice.146
  105.1 2.7 copy.66
  107.8 3.2 slice.148
  111.0 2.7 copy.67
  113.6 3.2 slice.150
  116.8 2.8 copy.68
  119.6 3.2 slice.152
  122.8 2.7 copy.69
  125.5 3.2 slice.154
  128.7 3.8 fusion.33
  132.5 3.8 fusion.22
  136.3 3.9 fusion.25
  140.1 2.0 reshape.114
  142.1 2.4 convert_reduce_fusion.1
  153.5 5.3 %convolution_multiply_fusion.4 = f32[48,768]{1,0:T(8,128)S(1)} fusion(bf16[48,4608]{1,0:T(8,128)(2,1)S(1)} %constant_dynamic-update-slice_fusion, bf16[768,4608]{1,0:T(8,128)(2,1)} %param.11), kind=kOutput, calls=%fused_computation.77 | convolution fusion | flops 339775488 | bytes 7667712 | tf_op jit(solution)/shard_map/rk,ck->rc/dot_general | solution.py:161
  158.8 4.8 add_convert_fusion
  166.7 53.4 %copy.73 = f32[1,768,4608]{2,0,1:T(1,128)} copy(f32[1,768,4608]{2,1,0:T(8,128)S(1)} %convolution_bitcast_fusion) | data formatting | bytes 28311552 | tf_op jit(solution)/shard_map/broadcast_in_dim | solution.py:170
  220.1 2.5 bitcast_dynamic-update-slice_fusion.4
  222.7 2.5 bitcast_dynamic-update-slice_fusion.3
  225.2 2.5 bitcast_dynamic-update-slice_fusion.2
  227.7 2.5 bitcast_dynamic-update-slice_fusion.1
  230.2 2.5 bitcast_dynamic-update-slice_fusion
  232.7 4.6 collective-permute-start.2
  237.3 2.4 fusion.39
  239.7 2.2 collective-permute-start.3
  241.9 2.4 fusion.19
  244.3 2.7 fusion.29
  247.1 2.5 fusion.16
  249.5 3.9 fusion.12
  253.4 215.0 %all-reduce.5.cloned.1.call-done = (f32[5,768,768]{2,1,0:T(8,128)}, f32[1,768,4608]{2,0,1:T(1,128)}) async-done(((f32[5,768,768]{2,1,0:T(8,128)}, f32[1,768,4608]{2,0,1:T(1,128)}), (f32[5,768,768]{2,1,0:T(8,128)}, f32[1,768,4608]{2,0,1:T(1,128)})) %all-reduce.5.cloned.1.call-update) | async-done | bytes 25952272
  469.4 9.7 %all_gather.6 = f32[5,24,768]{2,0,1:T(8,128)S(1)} all-gather(f32[5,6,768]{2,0,1:T(8,128)S(1)} %copy.70), channel_id=1, replica_groups=mesh['dp'=4,'seq'=32] {'dp'}, dimensions={1}, use_global_device_ids=true | all-gather | bytes 460800 | tf_op jit(solution)/shard_map/all_gather | solution.py:181
  481.0 8.4 %all_gather.7 = f32[1,24,4608]{2,0,1:T(1,128)S(1)} all-gather(f32[1,6,4608]{2,0,1:T(1,128)S(1)} %constant_dynamic-slice_fusion), channel_id=1, replica_groups=mesh['dp'=4,'seq'=32] {'dp'}, dimensions={1}, use_global_device_ids=true | all-gather | bytes 552960 | tf_op jit(solution)/shard_map/all_gather | solution.py:182
  (104 shorter events, 42.0 us)
Async XLA Ops:
  9.5 12.9 %copy-start.15 = (bf16[1,48,1536]{2,1,0:T(8,128)(2,1)S(1)}, bf16[1,48,1536]{2,1,0:T(8,128)(2,1)}, u32[]{:S(2)}) copy-start(bf16[1,48,1536]{2,1,0:T(8,128)(2,1)} %param.14) | copy-start | bytes 442372
  9.7 13.0 %copy-start.16 = (bf16[1,48,1536]{2,1,0:T(8,128)(2,1)S(1)}, bf16[1,48,1536]{2,1,0:T(8,128)(2,1)}, u32[]{:S(2)}) copy-start(bf16[1,48,1536]{2,1,0:T(8,128)(2,1)} %param.13) | copy-start | bytes 442372
  13.6 16.1 %all-to-all-start = ((bf16[32,2,2304]{2,1,0:T(2,128)(2,1)}), bf16[32,2,2304]{2,1,0:T(2,128)(2,1)S(1)}, u32[]{:S(2)}, u32[]{:S(2)}) async-start(bf16[32,2,2304]{2,1,0:T(2,128)(2,1)} %reshape.111), calls=%async_computation | async-start | bytes 589824 | tf_op jit(solution)/shard_map/all_to_all | solution.py:132
  23.0 12.9 %copy-start = (bf16[1,768,768]{2,1,0:T(8,128)(2,1)S(1)}, bf16[1,768,768]{2,1,0:T(8,128)(2,1)}, u32[]{:S(2)}) copy-start(bf16[1,768,768]{2,1,0:T(8,128)(2,1)} %param.8) | copy-start | bytes 3538948
  30.8 20.7 %all-to-all-start.1 = ((bf16[32,48,384]{2,1,0:T(8,128)(2,1)}), bf16[32,48,384]{2,1,0:T(8,128)(2,1)S(1)}, u32[]{:S(2)}, u32[]{:S(2)}) async-start(bf16[32,48,384]{2,1,0:T(8,128)(2,1)} %bitcast.3), calls=%async_computation.1 | async-start | bytes 2359296 | tf_op jit(solution)/shard_map/all_to_all | solution.py:133
  35.9 51.8 %collective-permute-start.1 = (bf16[2,768]{1,0:T(2,128)(2,1)S(1)}, bf16[2,768]{1,0:T(2,128)(2,1)S(1)}, u32[]{:S(2)}, u32[]{:S(2)}) collective-permute-start(bf16[2,768]{1,0:T(2,128)(2,1)S(1)} %get-tuple-element.21), channel_id=1, source_target_pairs={{1,0},{2,1},{3,2},{4,3},{5,4},{6,5},{7,6},{8,7},{9,8},{10,9},{11,1... | collective-permute-start | bytes 9224 | tf_op jit(solution)/shard_map/ppermute | solution.py:23
  40.5 50.4 %collective-permute-start = (bf16[2,768]{1,0:T(2,128)(2,1)S(1)}, bf16[2,768]{1,0:T(2,128)(2,1)S(1)}, u32[]{:S(2)}, u32[]{:S(2)}) collective-permute-start(bf16[2,768]{1,0:T(2,128)(2,1)S(1)} %get-tuple-element.20), channel_id=1, source_target_pairs={{0,1},{1,2},{2,3},{3,4},{4,5},{5,6},{6,7},{7,8},{8,9},{9,10},{10,1... | collective-permute-start | bytes 9224 | tf_op jit(solution)/shard_map/ppermute | solution.py:22
  61.2 12.4 %all-to-all-start.2 = ((bf16[32,2,1152]{2,1,0:T(2,128)(2,1)}), bf16[32,2,1152]{2,1,0:T(2,128)(2,1)}, u32[]{:S(2)}, u32[]{:S(2)}) async-start(bf16[32,2,1152]{2,1,0:T(2,128)(2,1)} %reshape.113), calls=%async_computation.2 | async-start | bytes 294912 | tf_op jit(solution)/shard_map/all_to_all | solution.py:149
  73.7 77.9 %all-to-all-start.3 = ((f32[32,48,384]{2,1,0:T(8,128)}), f32[32,48,384]{2,1,0:T(8,128)S(1)}, u32[]{:S(2)}, u32[]{:S(2)}) async-start(f32[32,48,384]{2,1,0:T(8,128)} %bitcast.6), calls=%async_computation.3 | async-start | bytes 4718592 | tf_op jit(solution)/shard_map/all_to_all | solution.py:150
  79.1 389.3 %all-reduce.5.cloned.1.call-start = ((), (), s32[]{:S(2)}) async-start(), calls=%async_computation.4 | async-start | bytes 51904512
  151.7 1.0 copy-start.2
  152.7 6.1 %copy-start.7 = (f32[768,768]{1,0:T(8,128)S(1)}, f32[768,768]{1,0:T(8,128)}, u32[]{:S(2)}) copy-start(f32[768,768]{1,0:T(8,128)} %fusion.22) | copy-start | bytes 7077892
  152.7 0.8 copy-start.3
  153.5 5.3 %copy-start.1 = (bf16[1,768,768]{2,1,0:T(8,128)(2,1)S(1)}, bf16[1,768,768]{2,1,0:T(8,128)(2,1)}, u32[]{:S(2)}) copy-start(bf16[1,768,768]{2,1,0:T(8,128)(2,1)} %param.9) | copy-start | bytes 3538948
  153.5 5.3 %copy-start.5 = (f32[768,768]{1,0:T(8,128)S(1)}, f32[768,768]{1,0:T(8,128)}, u32[]{:S(2)}) copy-start(f32[768,768]{1,0:T(8,128)} %fusion.41) | copy-start | bytes 7077892
  153.5 5.3 %copy-start.6 = (f32[768,768]{1,0:T(8,128)S(1)}, f32[768,768]{1,0:T(8,128)}, u32[]{:S(2)}) copy-start(f32[768,768]{1,0:T(8,128)} %fusion.33) | copy-start | bytes 7077892
  158.8 4.9 copy-start.8
  163.7 1.0 copy-start.4
  166.7 53.4 %copy-start.10 = (bf16[768,768]{0,1:T(8,128)(2,1)S(1)}, bf16[768,768]{0,1:T(8,128)(2,1)}, u32[]{:S(2)}) copy-start(bf16[768,768]{0,1:T(8,128)(2,1)} %slice.146) | copy-start | bytes 3538948
  220.1 2.6 copy-start.11
  222.7 2.5 copy-start.12
  225.2 2.6 copy-start.13
  227.7 2.5 copy-start.14
  232.7 9.2 %collective-permute-start.2 = (bf16[2,768]{1,0:T(2,128)(2,1)S(1)}, bf16[2,768]{1,0:T(2,128)(2,1)S(1)}, u32[]{:S(2)}, u32[]{:S(2)}) collective-permute-start(bf16[2,768]{1,0:T(2,128)(2,1)S(1)} %get-tuple-element.18), channel_id=1, source_target_pairs={{1,0},{2,1},{3,2},{4,3},{5,4},{6,5},{7,6},{8,7},{9,8},{10,9},{11,1... | collective-permute-start | bytes 9224 | tf_op jit(solution)/shard_map/ppermute | solution.py:23
  239.7 7.3 %collective-permute-start.3 = (bf16[2,768]{1,0:T(2,128)(2,1)S(1)}, bf16[2,768]{1,0:T(2,128)(2,1)S(1)}, u32[]{:S(2)}, u32[]{:S(2)}) collective-permute-start(bf16[2,768]{1,0:T(2,128)(2,1)S(1)} %get-tuple-element.19), channel_id=1, source_target_pairs={{0,1},{1,2},{2,3},{3,4},{4,5},{5,6},{6,7},{7,8},{8,9},{9,10},{10,1... | collective-permute-start | bytes 9224 | tf_op jit(solution)/shard_map/ppermute | solution.py:22
  247.0 2.5 copy-start.9
Sparse Core Ops, SparseCore 0:
  232.8 235.5 all-reduce.4
where the time goes:
time: 505 us; the launch traced here: 498 us
  waiting for transfers between devices  230 us (46%)
  local copies, waits for them, and re-layouts  123 us (24%)
  matrix products  60.3 us (12%)
  starting transfers between devices  39.5 us (8%)
  blocking collectives  18.1 us (4%)
  between operations  14.9 us (3%)
  other arithmetic  11.7 us (2%)
    unnamed x2, waiting for transfers between devices  215 us
    broadcast_in_dim x1, local copies, waits for them, and re-layouts, local(): jnp.einsum('rc,rk->ck', spread_columns(pooled, seq_count, dp_count), qkv_...  53.4 us
    slice x11, local copies, waits for them, and re-layouts, weight_terms(): padded[offset:offset + count]  32.1 us
    dot_general x4, matrix products, conv_apply(): jnp.dot(padded[offset:offset + count], weights[offset], preferred_element...  16.2 us
    dot_general x5, matrix products, conv_adjoint(): jnp.einsum('ro,co->rc', padded[start:start + count], weights[offset], pre...  13.9 us
    dot_general x5, matrix products, weight_terms(): jnp.einsum('rc,ro->co', padded[offset:offset + count], grad_rows, preferr...  12.5 us
    unnamed x47, local copies, waits for them, and re-layouts  12 us
  transfers between devices with their start and end apart: 9, of which 4 were waited for; matrix products, arithmetic and copies ran while one was open for 21% of the time, Pallas kernels for 0%

commit v1 on v0

v1 whole, which is shorter than its diff:
```python
import jax
import jax.numpy as jnp
from jax import lax
from jax.experimental import pallas as pl
from jax.experimental.pallas import tpu as pltpu
from jax.sharding import Mesh, PartitionSpec as P

HEADS = 8
TAPS = 5
LOSS_SCALE = 32
HD = 192
C = 768
ROWS = 768
ATT = 48
BLK = 384
FACTOR = 16
HALF = 384
QH = 288
SCALE = HD ** (-0.5)
SQRT_HALF = 0.7071067811865476
INV_ROOT_TWO_PI = 0.3989422804014327

BF = jnp.bfloat16
F32 = jnp.float32
DP = ("yh", "core")
SEQ = ("yl", "x", "z")
HAX = ("yl", "x")

NT = (((1,), (1,)), ((), ()))
TN = (((0,), (0,)), ((), ()))

A_PAIR = [(0, 1), (1, 0), (2, 3), (3, 2)]
B_PAIR = [(0, 3), (3, 0), (1, 2), (2, 1)]
SWAP = [(0, 1), (1, 0)]


def sds(shape, dtype):
    return jax.ShapeDtypeStruct(shape, dtype)


def params(mib):
    return pltpu.CompilerParams(vmem_limit_bytes=mib * 1024 * 1024)


def cost(flops, nbytes, trans=0):
    return pl.CostEstimate(flops=flops, bytes_accessed=nbytes, transcendentals=trans)


VM = pl.BlockSpec(memory_space=pltpu.VMEM)
SM = pl.BlockSpec(memory_space=pltpu.SMEM)


def nt(a, b):
    return lax.dot_general(a, b, NT, preferred_element_type=F32)


def tn(a, b):
    return lax.dot_general(a, b, TN, preferred_element_type=F32)


def mm(a, b):
    return jnp.dot(a, b, preferred_element_type=F32)


def pack_kernel(q, k, v, g, out):
    for h in range(HEADS):
        cols = slice(h * HD, (h + 1) * HD)
        for slot, ref in enumerate((q, g, k, v)):
            out[h, :, slot * HD : (slot + 1) * HD] = ref[:, cols]


def pack_heads(q, k, v, g):
    return pl.pallas_call(
        pack_kernel,
        out_shape=sds((HEADS, ATT, 4 * HD), BF),
        in_specs=[VM] * 4,
        out_specs=VM,
        name="pack_heads",
        cost_estimate=cost(0, 1200000),
    )(q, k, v, g)


def att_parts(own, qg, kv):
    query = jnp.concatenate([own[:, 0:HD], qg[:, 0:HD]], axis=0)
    grads = jnp.concatenate([own[:, HD : 2 * HD], qg[:, HD : 2 * HD]], axis=0)
    keys = jnp.concatenate([own[:, 2 * HD : 3 * HD], kv[:, 0:HD]], axis=0)
    values = jnp.concatenate([own[:, 3 * HD : 4 * HD], kv[:, HD : 2 * HD]], axis=0)
    return query, grads, keys, values


def stats_kernel(own, qg, kv, out):
    query, grads, keys, values = att_parts(own, qg, kv)
    out[...] = jnp.zeros_like(out)
    for i in range(2):
        rows = slice(i * BLK, (i + 1) * BLK)
        scores = nt(keys, query[rows]) * SCALE
        top = jnp.max(scores, axis=0, keepdims=True)
        powers = jnp.exp(scores - top)
        pgrad = nt(values, grads[rows])
        out[0:1, rows] = top
        out[1:2, rows] = jnp.sum(powers, axis=0, keepdims=True)
        out[2:3, rows] = jnp.sum(powers * pgrad, axis=0, keepdims=True)


def att_stats(own, qg, kv):
    return pl.pallas_call(
        stats_kernel,
        out_shape=sds((8, 2 * BLK), F32),
        in_specs=[VM] * 3,
        out_specs=VM,
        name="att_stats",
        compiler_params=params(32),
        cost_estimate=cost(2 * 768 * 768 * 192 * 2, 1200000, 768 * 768),
    )(own, qg, kv)


def grads_kernel(own, qg, kv, st, st2, dq_own, dq_send, dkv_own, dkv_send):
    query, grads, keys, values = att_parts(own, qg, kv)
    dk = jnp.zeros((2 * BLK, HD), F32)
    dv = jnp.zeros((2 * BLK, HD), F32)
    for i in range(2):
        rows = slice(i * BLK, (i + 1) * BLK)
        other = slice((1 - i) * BLK, (2 - i) * BLK)
        m0, m1 = st[0:1, rows], st2[0:1, other]
        top = jnp.maximum(m0, m1)
        e0, e1 = jnp.exp(m0 - top), jnp.exp(m1 - top)
        inv = 1.0 / (st[1:2, rows] * e0 + st2[1:2, other] * e1)
        delta = (st[2:3, rows] * e0 + st2[2:3, other] * e1) * inv
        scores = nt(keys, query[rows]) * SCALE
        probs = jnp.exp(scores - top) * inv
        pgrad = nt(values, grads[rows])
        sgrad = (probs * (pgrad - delta)).astype(BF)
        dq = tn(sgrad, keys) * SCALE
        dk = dk + mm(sgrad, query[rows])
        dv = dv + mm(probs.astype(BF), grads[rows])
        if i == 0:
            dq_own[...] = dq
        else:
            dq_send[:, 0:HD] = dq[0 : BLK // 2].astype(BF)
            dq_send[:, HD : 2 * HD] = dq[BLK // 2 : BLK].astype(BF)
    dk = dk * SCALE
    dkv_own[:, 0:HD] = dk[0:BLK]
    dkv_own[:, HD : 2 * HD] = dv[0:BLK]
    dkv_send[:, 0:HD] = dk[BLK:].astype(BF)
    dkv_send[:, HD : 2 * HD] = dv[BLK:].astype(BF)


def att_grads(own, qg, kv, st, st2):
    return pl.pallas_call(
        grads_kernel,
        out_shape=(
            sds((BLK, HD), F32),
            sds((BLK // 2, 2 * HD), BF),
            sds((BLK, 2 * HD), F32),
            sds((BLK, 2 * HD), BF),
        ),
        in_specs=[VM] * 5,
        out_specs=(VM,) * 4,
        name="att_grads",
        compiler_params=params(40),
        cost_estimate=cost(5 * 768 * 768 * 192 * 2, 3000000, 768 * 768),
    )(own, qg, kv, st, st2)


def join_kernel(core, dq_own, dkv_own, dq_in, dkv_in, wh, pool, keep, send):
    dq_got = jnp.concatenate([dq_in[:, 0:HD], dq_in[:, HD : 2 * HD]], axis=0).astype(F32)
    dq = (dq_own[...] + dq_got).astype(BF)
    dkv = (dkv_own[...] + dkv_in[...].astype(F32)).astype(BF)
    qkv = jnp.concatenate([dq, dkv], axis=1)
    pool[...] = nt(qkv, wh[...]).astype(BF)

    @pl.when(core[0] == 0)
    def _():
        keep[...] = qkv[:, 0:QH]
        send[...] = qkv[:, QH : 2 * QH]

    @pl.when(core[0] != 0)
    def _():
        keep[...] = qkv[:, QH : 2 * QH]
        send[...] = qkv[:, 0:QH]


def att_join(core, dq_own, dkv_own, dq_in, dkv_in, wh):
    return pl.pallas_call(
        join_kernel,
        out_shape=(sds((BLK, C), BF), sds((BLK, QH), BF), sds((BLK, QH), BF)),
        in_specs=[SM] + [VM] * 5,
        out_specs=(VM,) * 3,
        name="att_join",
        compiler_params=params(24),
        cost_estimate=cost(2 * 384 * 576 * 768, 3500000),
    )(core, dq_own, dkv_own, dq_in, dkv_in, wh)


def forward_kernel(xp, w, slope, pooled, xf, acc):
    tap = pl.program_id(0)

    @pl.when(tap == 0)
    def _():
        xf[...] = xp[...].astype(F32)

    for t in range(TAPS):

        @pl.when(tap == t)
        def _(t=t):
            for r in range(0, ROWS, 256):
                rows = xf[6 + t + r : 6 + t + r + 256, :].astype(BF)
                got = mm(rows, w[0])
                if t == 0:
                    acc[r : r + 256, :] = got
                else:
                    acc[r : r + 256, :] += got

    @pl.when(tap == TAPS - 1)
    def _():
        @pl.loop(0, ROWS // 64)
        def _(i):
            at = pl.multiple_of(i * 64, 64)
            pre = acc[pl.ds(at, 64), :]
            cumul = 0.5 * (1.0 + lax.erf(pre * SQRT_HALF))
            slope[pl.ds(at, 64), :] = (
                cumul + pre * INV_ROOT_TWO_PI * jnp.exp(-0.5 * pre * pre)
            ).astype(BF)
            rows = xf[pl.ds(pl.multiple_of(at + 8, 8), 64), :]
            block = (rows + pre * cumul).astype(BF).astype(F32)
            acc[pl.ds(pl.multiple_of(i * 8, 8), 8), :] = jnp.concatenate(
                [jnp.mean(block.reshape(4, FACTOR, C), axis=1), jnp.zeros((4, C), F32)], axis=0
            )

        for i in range(ROWS // 64):
            pooled[4 * i : 4 * i + 4, :] = acc[8 * i : 8 * i + 4, :]


def conv_forward(xp, w):
    return pl.pallas_call(
        forward_kernel,
        grid=(TAPS,),
        out_shape=(sds((ROWS, C), BF), sds((ATT, C), F32)),
        in_specs=[
            pl.BlockSpec((ROWS + 16, C), lambda t: (0, 0)),
            pl.BlockSpec((1, C, C), lambda t: (t, 0, 0)),
        ],
        out_specs=(
            pl.BlockSpec((ROWS, C), lambda t: (0, 0)),
            pl.BlockSpec((ATT, C), lambda t: (0, 0)),
        ),
        scratch_shapes=[pltpu.VMEM((ROWS + 16, C), F32), pltpu.VMEM((ROWS, C), F32)],
        name="conv_forward",
        compiler_params=params(32),
        cost_estimate=cost(2 * 5 * 768**3, 9500000, 2 * 768 * 768),
    )(xp, w)


def turn_kernel(xp, xt, alts, edge):
    for r in range(0, ROWS, 128):
        xt[:, r : r + 128] = xp[8 + r : 8 + r + 128, :].T
    last = xp[8 + ROWS - 128 : 8 + ROWS, :].astype(F32)
    first = xp[8 : 8 + 128, :].astype(F32)
    top = xp[0:16, :].astype(F32)[0:8]
    bottom = xp[ROWS : ROWS + 16, :].astype(F32)[8:16]
    edge[...] = last
    edge[126:128, :] = top[6:8]
    alts[:, 0:128] = edge[...].astype(BF).T
    edge[126:127, :] = last[126:127]
    alts[:, 128:256] = edge[...].astype(BF).T
    edge[...] = first
    edge[0:1, :] = bottom[0:1]
    alts[:, 256:384] = edge[...].astype(BF).T
    edge[1:2, :] = bottom[1:2]
    alts[:, 384:512] = edge[...].astype(BF).T


def turn_input(xp):
    return pl.pallas_call(
        turn_kernel,
        out_shape=(sds((C, ROWS), BF), sds((C, 512), BF)),
        in_specs=[VM],
        out_specs=(VM, VM),
        scratch_shapes=[pltpu.VMEM((128, C), F32)],
        name="turn_input",
        compiler_params=params(24),
        cost_estimate=cost(10 * 768 * 768, 3200000),
    )(xp)


def slope_kernel(core, parts, skip, slope, pre, send, keep, pool):
    total = jnp.sum(parts[...].astype(F32), axis=0) * (1.0 / FACTOR)
    pool[...] = total
    for r in range(0, ATT, 8):
        piece = jnp.broadcast_to(total[r : r + 8, None, :], (8, FACTOR, C)).reshape(128, C)
        rows = slice(r * FACTOR, r * FACTOR + 128)
        grad = (skip[rows, :].astype(F32) + piece) * slope[rows, :].astype(F32)
        pre[rows, :] = grad.astype(BF)

    @pl.when(core[0] == 0)
    def _():
        keep[...] = pre[:, 0:HALF]
        send[...] = pre[:, HALF:]

    @pl.when(core[0] != 0)
    def _():
        keep[...] = pre[:, HALF:]
        send[...] = pre[:, 0:HALF]


def pre_grads(core, parts, skip, slope):
    return pl.pallas_call(
        slope_kernel,
        out_shape=(
            sds((ROWS, C), BF),
            sds((ROWS, HALF), BF),
            sds((ROWS, HALF), BF),
            sds((ATT, C), F32),
        ),
        in_specs=[SM] + [VM] * 3,
        out_specs=(VM,) * 4,
        name="pre_grads",
        compiler_params=params(24),
        cost_estimate=cost(5 * 768 * 768, 6000000),
    )(core, parts, skip, slope)


def weights_kernel(xt0, al0, xt1, al1, y0, y1, p0, p1, s0, s1, out, yf, yt):
    step = pl.program_id(0)

    @pl.when(step == 0)
    def _():
        for i, ref in enumerate((y0, y1)):
            got = ref[...].astype(F32)
            yf[8 : 8 + ROWS, :] = got
            yf[0:8, :] = got[ROWS - 8 :]
            yf[8 + ROWS : 16 + ROWS, :] = got[0:8]
            for t in range(TAPS):
                yt[t, i * ROWS : (i + 1) * ROWS, :] = yf[10 - t : 10 - t + ROWS, :].astype(BF)

    def shifted(xt, al, t):
        if t < 2:
            return jnp.concatenate([xt[:, : ROWS - 128], al[:, t * 128 : t * 128 + 128]], axis=1)
        if t > 2:
            return jnp.concatenate([al[:, (t - 1) * 128 : t * 128], xt[:, 128:]], axis=1)
        return xt[...]

    for t in range(TAPS):
        left = jnp.concatenate([shifted(xt0, al0, t), shifted(xt1, al1, t)], axis=1)
        out[:, t * HALF : (t + 1) * HALF] = mm(left, yt[t]).astype(BF)
    out[:, TAPS * HALF : TAPS * HALF + QH] = (tn(p0[...], s0[...]) + tn(p1[...], s1[...])).astype(BF)
    out[:, TAPS * HALF + QH :] = jnp.zeros((256, 2304 - TAPS * HALF - QH), BF)


def weight_grads(xt0, al0, xt1, al1, y0, y1, p0, p1, s0, s1):
    rows = lambda n: pl.BlockSpec((256, n), lambda i: (i, 0))
    whole = lambda a, b: pl.BlockSpec((a, b), lambda i: (0, 0))
    cols = pl.BlockSpec((BLK, 256), lambda i: (0, i))
    return pl.pallas_call(
        weights_kernel,
        grid=(3,),
        out_shape=sds((C, 2304), BF),
        in_specs=[
            rows(ROWS),
            rows(512),
            rows(ROWS),
            rows(512),
            whole(ROWS, HALF),
            whole(ROWS, HALF),
            cols,
            cols,
            whole(BLK, QH),
            whole(BLK, QH),
        ],
        out_specs=rows(2304),
        scratch_shapes=[
            pltpu.VMEM((ROWS + 16, HALF), F32),
            pltpu.VMEM((TAPS, 2 * ROWS, HALF), BF),
        ],
        name="weight_grads",
        compiler_params=params(40),
        cost_estimate=cost(2 * 5 * 768 * 1536 * 384, 10000000),
    )(xt0, al0, xt1, al1, y0, y1, p0, p1, s0, s1)


def adjoint_kernel(pre, top, bottom, w, skip, pool, out, yf, acc):
    tap = pl.program_id(0)

    @pl.when(tap == 0)
    def _():
        yf[8 : 8 + ROWS, :] = pre[...].astype(F32)
        yf[6:8, :] = top[...].astype(F32)
        yf[8 + ROWS : 10 + ROWS, :] = bottom[...].astype(F32)
        for r in range(0, ATT, 8):
            piece = jnp.broadcast_to(pool[r : r + 8, :][:, None, :], (8, FACTOR, C)).reshape(128, C)
            rows = slice(r * FACTOR, r * FACTOR + 128)
            acc[rows, :] = skip[rows, :].astype(F32) + piece

    for t in range(TAPS):

        @pl.when(tap == t)
        def _(t=t):
            for r in range(0, ROWS, 256):
                rows = yf[10 - t + r : 10 - t + r + 256, :].astype(BF)
                got = acc[r : r + 256, :] + nt(rows, w[0])
                if t == TAPS - 1:
                    out[r : r + 256, :] = got.astype(BF)
                else:
                    acc[r : r + 256, :] = got


def conv_adjoint(pre, top, bottom, w, skip, pool):
    whole = lambda a, b: pl.BlockSpec((a, b), lambda t: (0, 0))
    return pl.pallas_call(
        adjoint_kernel,
        grid=(TAPS,),
        out_shape=sds((ROWS, C), BF),
        in_specs=[
            whole(ROWS, C),
            whole(2, C),
            whole(2, C),
            pl.BlockSpec((1, C, C), lambda t: (t, 0, 0)),
            whole(ROWS, C),
            whole(ATT, C),
        ],
        out_specs=whole(ROWS, C),
        scratch_shapes=[pltpu.VMEM((ROWS + 16, C), F32), pltpu.VMEM((ROWS, C), F32)],
        name="conv_adjoint",
        compiler_params=params(32),
        cost_estimate=cost(2 * 5 * 768**3, 9500000),
    )(pre, top, bottom, w, skip, pool)


def sum_conv_kernel(parts, out):
    total = parts[0].astype(F32)
    for s in range(1, 32):
        total = total + parts[s].astype(F32)
    out[0] = total.astype(BF)


def sum_proj_kernel(parts, out):
    for h in range(HEADS):
        total = parts[4 * h].astype(F32)
        for s in range(4 * h + 1, 4 * h + 4):
            total = total + parts[s].astype(F32)
        out[h] = total.astype(BF)


def sum_partials(parts):
    conv = pl.pallas_call(
        sum_conv_kernel,
        grid=(TAPS,),
        out_shape=sds((TAPS, 24, HALF), BF),
        in_specs=[pl.BlockSpec((32, 24, HALF), lambda t: (0, 0, t))],
        out_specs=pl.BlockSpec((1, 24, HALF), lambda t: (t, 0, 0)),
        name="sum_conv",
        cost_estimate=cost(32 * 24 * 1920, 3000000),
    )(parts)
    proj = pl.pallas_call(
        sum_proj_kernel,
        grid=(1,),
        out_shape=sds((HEADS, 24, HALF), BF),
        in_specs=[pl.BlockSpec((32, 24, HALF), lambda t: (0, 0, TAPS))],
        out_specs=pl.BlockSpec((HEADS, 24, HALF), lambda t: (0, 0, 0)),
        name="sum_proj",
        cost_estimate=cost(32 * 24 * 384, 700000),
    )(parts)
    return conv, proj


def add_kernel(a, b, c, d, out):
    out[0:TAPS] = (a[...].astype(F32) + b[...].astype(F32)) * (1.0 / LOSS_SCALE)
    out[TAPS:] = (c[...].astype(F32) + d[...].astype(F32)) * (1.0 / LOSS_SCALE)


def add_pair(a, b, c, d):
    return pl.pallas_call(
        add_kernel,
        out_shape=sds((TAPS + HEADS, 24, HALF), F32),
        in_specs=[VM] * 4,
        out_specs=VM,
        name="add_pair",
        cost_estimate=cost(300000, 1500000),
    )(a, b, c, d)


def place_kernel(core, mine, other, conv, proj):
    def put(low, high):
        conv[:, :, 0:HALF] = low[0:TAPS]
        conv[:, :, HALF:] = high[0:TAPS]
        for h in range(HEADS):
            at = h * HD
            proj[:, at : at + HD] = low[TAPS + h, :, 0:HD]
            proj[:, 1536 + at : 1536 + at + HD] = jnp.concatenate(
                [low[TAPS + h, :, HD:QH], high[TAPS + h, :, 0 : HD // 2]], axis=1
            )
            proj[:, 3072 + at : 3072 + at + HD] = high[TAPS + h, :, HD // 2 : QH]

    @pl.when(core[0] == 0)
    def _():
        put(mine, other)

    @pl.when(core[0] != 0)
    def _():
        put(other, mine)


def place(core, mine, other):
    return pl.pallas_call(
        place_kernel,
        out_shape=(sds((TAPS, 24, C), F32), sds((24, 4608), F32)),
        in_specs=[SM, VM, VM],
        out_specs=(VM, VM),
        name="place",
        cost_estimate=cost(0, 2500000),
    )(core, mine, other)


def halo(x):
    up = [(i, i + 1) for i in range(31)]
    down = [(i + 1, i) for i in range(31)]
    return lax.ppermute(x[ROWS - 2 :], SEQ, up), lax.ppermute(x[0:2], SEQ, down)


def local(conv_input, skip_grad, conv_weight, proj_weight, query, key, value, grad):
    core = lax.axis_index("core").astype(jnp.int32).reshape(1)
    head = lax.axis_index("yl") * 4 + lax.axis_index("x")
    x, skip = conv_input[0], skip_grad[0]

    packed = pack_heads(query[0], key[0], value[0], grad[0])
    own = lax.all_to_all(packed, HAX, 0, 0, tiled=True).reshape(BLK, 4 * HD)
    qg = lax.ppermute(own[:, : 2 * HD], "z", A_PAIR)
    kv = lax.ppermute(own[:, 2 * HD :], "z", B_PAIR)

    top, bottom = halo(x)
    edge = jnp.zeros((6, C), BF)
    xp = jnp.concatenate([edge, top, x, bottom, edge], axis=0)
    xp_sib = lax.ppermute(xp, "core", SWAP)
    slope, pooled = conv_forward(xp, conv_weight)
    pooled_blk = lax.all_gather(pooled.astype(BF), HAX, axis=0, tiled=True)
    pooled_sib = lax.ppermute(pooled_blk, "core", SWAP)
    xt0, al0 = turn_input(xp)
    xt1, al1 = turn_input(xp_sib)

    wh = jnp.concatenate(
        [lax.dynamic_slice_in_dim(proj_weight, p * 1536 + head * HD, HD, 1) for p in range(3)], axis=1
    )

    st = att_stats(own, qg, kv)
    st2 = lax.ppermute(st, "z", A_PAIR)
    dq_own, dq_send, dkv_own, dkv_send = att_grads(own, qg, kv, st, st2)
    dq_in = lax.ppermute(dq_send, "z", A_PAIR)
    dkv_in = lax.ppermute(dkv_send, "z", B_PAIR)
    pool_part, s0, s_send = att_join(core, dq_own, dkv_own, dq_in, dkv_in, wh)
    parts = lax.all_to_all(pool_part.reshape(HEADS, ATT, C), HAX, 0, 0, tiled=True)
    s1 = lax.ppermute(s_send, "core", SWAP)

    pre, y_send, y0, pool = pre_grads(core, parts, skip, slope)
    y1 = lax.ppermute(y_send, "core", SWAP)
    terms = weight_grads(xt0, al0, xt1, al1, y0, y1, pooled_blk, pooled_sib, s0, s1)
    got = lax.all_to_all(terms.reshape(32, 24, 2304), SEQ, 0, 0, tiled=True)

    ptop, pbottom = halo(pre)
    input_grad = conv_adjoint(pre, ptop, pbottom, conv_weight, skip, pool)

    conv, proj = sum_partials(got)
    far = [(0, 1), (1, 0)]
    mine = add_pair(conv, lax.ppermute(conv, "yh", far), proj, lax.ppermute(proj, "yh", far))
    other = lax.ppermute(mine, "core", SWAP)
    conv_grad, proj_grad = place(core, mine, other)
    return input_grad[None], conv_grad, proj_grad


def solution(mesh):
    fine = Mesh(mesh.devices.reshape(2, 2, 2, 4, 4), ("yh", "core", "yl", "x", "z"))
    rows = P(DP, SEQ, None)
    return jax.shard_map(
        local,
        mesh=fine,
        in_specs=(rows, rows, P(), P(), rows, rows, rows, rows),
        out_specs=(rows, P(None, SEQ, None), P(SEQ, None)),
        check_vma=False,
    )
```

time: 505 us -> 223 us (0.44)
  the two profiles are of different devices: /device:TPU:7 before, /device:TPU:8 now
where the time goes in v1:
time: 223 us; the launch traced here: 222 us
  blocking collectives  97.2 us (44%)
  Pallas kernels  45.1 us (20%)
  waiting for transfers between devices  29.4 us (13%)
  starting transfers between devices  28.6 us (13%)
  local copies, waits for them, and re-layouts  20.3 us (9%)
    all_to_all x1, blocking collectives, local(): got = lax.all_to_all(terms.reshape(32, 24, 2304), SEQ, 0, 0, tiled=True)  50.9 us
    all_gather x1, blocking collectives, local(): pooled_blk = lax.all_gather(pooled.astype(BF), HAX, axis=0, tiled=True)  31.1 us
    unnamed x42, local copies, waits for them, and re-layouts  17.8 us
    all_to_all x1, blocking collectives, local(): own = lax.all_to_all(packed, HAX, 0, 0, tiled=True).reshape(BLK, 4 * HD)  15.2 us
    ppermute x2, waiting for transfers between devices, halo(): lax.ppermute(x[ROWS - 2:], SEQ, up)  13.1 us
    ppermute x2, starting transfers between devices, halo(): lax.ppermute(x[0:2], SEQ, down)  10.8 us
    pallas_call x1, Pallas kernels, weight_grads(): pl.pallas_call(weights_kernel, grid=(3,), out_shape=sds((C, 2304), BF), i...  10.2 us
    pallas_call x1, Pallas kernels, conv_adjoint(): pl.pallas_call(adjoint_kernel, grid=(TAPS,), out_shape=sds((ROWS, C), BF)...  7.28 us
  transfers between devices with their start and end apart: 17, of which 7 were waited for; matrix products, arithmetic and copies ran while one was open for 1% of the time, Pallas kernels for 10%

profile of v1, /device:TPU:8, one launch (start us, length us, event | category | flops | bytes accessed | tf_op | source)
XLA Modules:
  0.0 221.8 jit_solution(2184520154457278887)
XLA Ops:
  0.6 2.1 pack_heads.1
  2.7 15.2 %all_to_all.15 = bf16[8,48,768]{2,1,0:T(8,128)(2,1)S(1)} all-to-all(bf16[8,48,768]{2,1,0:T(8,128)(2,1)} %pack_heads.1), channel_id=1, replica_groups=mesh['yh'=2,'core'=2,'yl'=2,'x'=4,'z'=4] {'yl','x'}, dimensions={0} | all-to-all | bytes 1179648 | tf_op jit(solution)/shard_map/all_to_all | solution.py:526
  18.0 4.1 %collective-permute-start.1 = (bf16[384,384]{1,0:T(8,128)(2,1)S(1)}, bf16[384,384]{1,0:T(8,128)(2,1)S(1)}, u32[]{:S(2)}, u32[]{:S(2)}) collective-permute-start(bf16[384,384]{1,0:T(8,128)(2,1)S(1)} %get-tuple-element.48), channel_id=1, source_target_pairs={{0,3},{3,0},{1,2},{2,1},{4,7},{7,4},{5,6},{6,5},{8,11},{11,8},{9,1... | collective-permute-start | bytes 884744 | tf_op jit(solution)/shard_map/ppermute | solution.py:528
  22.1 5.5 %collective-permute-done.1.kv = bf16[384,384]{1,0:T(8,128)(2,1)S(1)} collective-permute-done((bf16[384,384]{1,0:T(8,128)(2,1)S(1)}, bf16[384,384]{1,0:T(8,128)(2,1)S(1)}, u32[]{:S(2)}, u32[]{:S(2)}) %collective-permute-start.1) | collective-permute-done | bytes 294944 | tf_op jit(solution)/shard_map/ppermute | solution.py:528
  27.6 1.5 collective-permute-done.qg
  29.0 1.2 att_stats.1.st
  30.6 3.5 %collective-permute-done.2.st2 = f32[8,768]{1,0:T(8,128)S(1)} collective-permute-done((f32[8,768]{1,0:T(8,128)S(1)}, f32[8,768]{1,0:T(8,128)S(1)}, u32[]{:S(2)}, u32[]{:S(2)}) %collective-permute-start.2) | collective-permute-done | bytes 24608 | tf_op jit(solution)/shard_map/ppermute | solution.py:545
  34.1 3.2 %att_grads.1 = (f32[384,192]{1,0:T(8,128)S(1)}, bf16[192,384]{1,0:T(8,128)(2,1)}, f32[384,384]{1,0:T(8,128)S(1)}, bf16[384,384]{1,0:T(8,128)(2,1)}) custom-call(bf16[384,768]{1,0:T(8,128)(2,1)S(1)} %bitcast.18, bf16[384,384]{1,0:T(8,128)(2,1)S(1)} %collective-permute-done.qg, bf16[384,384]{1,0:T(8,128)(2,1)S(1)} %collective-permute-done.1.kv, ...), custom_call_target="tpu_custom_call" | custom-call | flops 1132462080 | bytes 3000000 | tf_op jit(solution)/shard_map/att_grads/pallas_call | solution.py:149
  37.3 0.8 copy-done.5
  38.1 0.7 copy-done.7
  38.9 1.5 collective-permute-start.4
  40.4 5.3 %collective-permute-start.6 = (bf16[2,768]{1,0:T(2,128)(2,1)S(1)}, bf16[2,768]{1,0:T(2,128)(2,1)S(1)}, u32[]{:S(2)}, u32[]{:S(2)}) collective-permute-start(bf16[2,768]{1,0:T(2,128)(2,1)S(1)} %get-tuple-element.46), channel_id=1, source_target_pairs={{1,0},{2,1},{3,2},{4,3},{5,4},{6,5},{7,6},{8,7},{9,8},{10,9},{11,1... | collective-permute-start | bytes 9224 | tf_op jit(solution)/shard_map/ppermute | solution.py:517
  45.7 1.9 collective-permute-start.5
  47.7 2.0 constant_dynamic-slice_fusion.2
  50.0 5.3 %collective-permute-done.5 = bf16[2,768]{1,0:T(2,128)(2,1)S(1)} collective-permute-done((bf16[2,768]{1,0:T(2,128)(2,1)S(1)}, bf16[2,768]{1,0:T(2,128)(2,1)S(1)}, u32[]{:S(2)}, u32[]{:S(2)}) %collective-permute-start.5) | collective-permute-done | bytes 3104 | tf_op jit(solution)/shard_map/ppermute | solution.py:517
  55.9 1.1 copy-done.6
  56.9 1.0 copy-done.8
  57.9 1.8 att_join.1
  59.8 0.8 copy-done.4
  60.6 0.7 copy-done.13
  61.3 0.7 copy-done.15
  62.0 3.7 %all-to-all-start.1 = ((bf16[8,48,768]{2,1,0:T(8,128)(2,1)}), bf16[8,48,768]{2,1,0:T(8,128)(2,1)S(1)}, u32[]{:S(2)}, u32[]{:S(2)}) async-start(bf16[8,48,768]{2,1,0:T(8,128)(2,1)} %bitcast.21), calls=%async_computation.1 | async-start | bytes 1179648 | tf_op jit(solution)/shard_map/all_to_all | solution.py:550
  65.7 2.7 %copy-done.11 = bf16[5,768,768]{2,1,0:T(8,128)(2,1)S(1)} copy-done((bf16[5,768,768]{2,1,0:T(8,128)(2,1)S(1)}, bf16[5,768,768]{2,1,0:T(8,128)(2,1)}, u32[]{:S(2)}) %copy-start.11) | copy-done | bytes 5898264
  68.4 7.3 %conv_forward.1 = (bf16[768,768]{1,0:T(8,128)(2,1)S(1)}, f32[48,768]{1,0:T(8,128)S(1)}) custom-call(bf16[784,768]{1,0:T(8,128)(2,1)S(1)} %concatenate.7.xp, bf16[5,768,768]{2,1,0:T(8,128)(2,1)S(1)} %copy-done.11), custom_call_target="tpu_custom_call" | custom-call | flops 4529848320 | bytes 9500000 | tf_op jit(solution)/shard_map/conv_forward/pallas_call | solution.py:235
  75.6 1.0 copy-done.2
  76.6 31.1 %all_gather.3.p0 = bf16[384,768]{1,0:T(8,128)(2,1)} all-gather(bf16[48,768]{1,0:T(8,128)(2,1)S(1)} %convert_element_type.3), channel_id=1, replica_groups=mesh['yh'=2,'core'=2,'yl'=2,'x'=4,'z'=4] {'yl','x'}, dimensions={0}, use_global_device_ids=true | all-gather | bytes 663552 | tf_op jit(solution)/shard_map/all_gather | solution.py:535
  107.7 1.3 copy-done
  109.0 1.3 copy-done.3
  110.9 1.0 copy-done.9
  113.1 0.6 turn_input.3
  113.7 0.8 collective-permute-done.12.s1
  114.4 10.2 %weight_grads.1 = bf16[768,2304]{1,0:T(8,128)(2,1)S(1)} custom-call(bf16[768,768]{1,0:T(8,128)(2,1)S(1)} %get-tuple-element.30.xt0, bf16[768,512]{1,0:T(8,128)(2,1)S(1)} %get-tuple-element.31.al0, bf16[768,768]{1,0:T(8,128)(2,1)S(1)} %get-tuple-element.32.xt1, bf16[768,512]{1,0:T(8,128)(2,1)S(1)} %get-tuple-element.33.al1, ...), custom_call_target="tpu_custom_call" | custom-call | flops 4529848320 | bytes 10000000 | tf_op jit(solution)/shard_map/weight_grads/pallas_call | solution.py:354
  124.6 50.9 %all_to_all.16.parts = bf16[32,24,2304]{2,1,0:T(8,128)(2,1)} all-to-all(bf16[32,24,2304]{2,1,0:T(8,128)(2,1)S(1)} %bitcast.15), channel_id=1, replica_groups=mesh['yh'=2,'core'=2,'yl'=2,'x'=4,'z'=4] {'yl','x','z'}, dimensions={0} | all-to-all | bytes 7077888 | tf_op jit(solution)/shard_map/all_to_all | solution.py:556
  175.5 1.8 sum_proj.1.c
  177.3 2.3 %collective-permute-start.14 = (bf16[8,24,384]{2,1,0:T(8,128)(2,1)}, bf16[8,24,384]{2,1,0:T(8,128)(2,1)S(1)}, u32[]{:S(2)}, u32[]{:S(2)}) collective-permute-start(bf16[8,24,384]{2,1,0:T(8,128)(2,1)} %sum_proj.1.c), channel_id=1, source_target_pairs={{0,64},{64,0},{1,65},{65,1},{2,66},{66,2},{3,67},{67,3},{4,68},{68... | collective-permute-start | bytes 442376 | tf_op jit(solution)/shard_map/ppermute | solution.py:563
  179.6 4.2 %sum_conv.1.a = bf16[5,24,384]{2,1,0:T(8,128)(2,1)} custom-call(bf16[32,24,2304]{2,1,0:T(8,128)(2,1)} %all_to_all.16.parts), custom_call_target="tpu_custom_call" | custom-call | flops 1474560 | bytes 3000000 | tf_op jit(solution)/shard_map/sum_conv/pallas_call | solution.py:445
  183.8 1.2 collective-permute-start.13
  185.0 5.0 %collective-permute-done.13.b = bf16[5,24,384]{2,1,0:T(8,128)(2,1)S(1)} collective-permute-done((bf16[5,24,384]{2,1,0:T(8,128)(2,1)}, bf16[5,24,384]{2,1,0:T(8,128)(2,1)S(1)}, u32[]{:S(2)}, u32[]{:S(2)}) %collective-permute-start.13) | collective-permute-done | bytes 92192 | tf_op jit(solution)/shard_map/ppermute | solution.py:563
  190.1 0.6 copy-done.20
  190.7 0.7 copy-done.19
  191.4 1.9 add_pair.1.mine
  193.3 5.5 %collective-permute-start.8 = (bf16[2,768]{1,0:T(2,128)(2,1)S(1)}, bf16[2,768]{1,0:T(2,128)(2,1)S(1)}, u32[]{:S(2)}, u32[]{:S(2)}) collective-permute-start(bf16[2,768]{1,0:T(2,128)(2,1)S(1)} %get-tuple-element.44), channel_id=1, source_target_pairs={{1,0},{2,1},{3,2},{4,3},{5,4},{6,5},{7,6},{8,7},{9,8},{10,9},{11,1... | collective-permute-start | bytes 9224 | tf_op jit(solution)/shard_map/ppermute | solution.py:517
  198.8 1.9 collective-permute-start.7
  200.8 7.8 %collective-permute-done.7.top = bf16[2,768]{1,0:T(2,128)(2,1)S(1)} collective-permute-done((bf16[2,768]{1,0:T(2,128)(2,1)S(1)}, bf16[2,768]{1,0:T(2,128)(2,1)S(1)}, u32[]{:S(2)}, u32[]{:S(2)}) %collective-permute-start.7) | collective-permute-done | bytes 3104 | tf_op jit(solution)/shard_map/ppermute | solution.py:517
  208.6 2.7 %copy-done.12 = bf16[5,768,768]{2,1,0:T(8,128)(2,1)S(1)} copy-done((bf16[5,768,768]{2,1,0:T(8,128)(2,1)S(1)}, bf16[5,768,768]{2,1,0:T(8,128)(2,1)}, u32[]{:S(2)}) %copy-start.12) | copy-done | bytes 5898264
  211.2 7.3 %conv_adjoint.1 = bf16[768,768]{1,0:T(8,128)(2,1)} custom-call(bf16[768,768]{1,0:T(8,128)(2,1)S(1)} %copy-done.10, bf16[2,768]{1,0:T(2,128)(2,1)S(1)} %collective-permute-done.7.top, bf16[2,768]{1,0:T(2,128)(2,1)S(1)} %collective-permute-done.8.bottom, bf16[5,768,768]{2,1,0:T(8,128)(2,1)S(1)} %copy-done.12, bf16[768,768]{1,0:T(8,128)(2,1)S(1)} %bitcast.20, ...), custom_call_target="tpu_custom_call" | custom-call | flops 4529848320 | bytes 9500000 | tf_op jit(solution)/shard_map/conv_adjoint/pallas_call | solution.py:409
  218.5 0.8 copy-done.18
  219.3 2.5 %place.1 = (f32[5,24,768]{2,1,0:T(8,128)}, f32[24,4608]{1,0:T(8,128)}) custom-call(s32[1]{0:T(128)} %bitcast.core, f32[13,24,384]{2,1,0:T(8,128)} %add_pair.1.mine, f32[13,24,384]{2,1,0:T(8,128)} %copy-done.18), custom_call_target="tpu_custom_call" | custom-call | bytes 2500000 | tf_op jit(solution)/shard_map/place/pallas_call | solution.py:504
  (53 shorter events, 3.2 us)
Async XLA Ops:
  18.0 9.6 %collective-permute-start.1 = (bf16[384,384]{1,0:T(8,128)(2,1)S(1)}, bf16[384,384]{1,0:T(8,128)(2,1)S(1)}, u32[]{:S(2)}, u32[]{:S(2)}) collective-permute-start(bf16[384,384]{1,0:T(8,128)(2,1)S(1)} %get-tuple-element.48), channel_id=1, source_target_pairs={{0,3},{3,0},{1,2},{2,1},{4,7},{7,4},{5,6},{6,5},{8,11},{11,8},{9,1... | collective-permute-start | bytes 884744 | tf_op jit(solution)/shard_map/ppermute | solution.py:528
  22.1 6.9 %collective-permute-start = (bf16[384,384]{1,0:T(8,128)(2,1)S(1)}, bf16[384,384]{1,0:T(8,128)(2,1)S(1)}, u32[]{:S(2)}, u32[]{:S(2)}) collective-permute-start(bf16[384,384]{1,0:T(8,128)(2,1)S(1)} %get-tuple-element.49), channel_id=1, source_target_pairs={{0,1},{1,0},{2,3},{3,2},{4,5},{5,4},{6,7},{7,6},{8,9},{9,8},{10,11... | collective-permute-start | bytes 884744 | tf_op jit(solution)/shard_map/ppermute | solution.py:527
  30.2 10.1 %copy-start.17 = (bf16[1,768,768]{2,1,0:T(8,128)(2,1)S(1)}, bf16[1,768,768]{2,1,0:T(8,128)(2,1)}, u32[]{:S(2)}) copy-start(bf16[1,768,768]{2,1,0:T(8,128)(2,1)} %param.8) | copy-start | bytes 3538948
  30.2 3.9 %collective-permute-start.2 = (f32[8,768]{1,0:T(8,128)S(1)}, f32[8,768]{1,0:T(8,128)S(1)}, u32[]{:S(2)}, u32[]{:S(2)}) collective-permute-start(f32[8,768]{1,0:T(8,128)S(1)} %att_stats.1.st), channel_id=1, source_target_pairs={{0,1},{1,0},{2,3},{3,2},{4,5},{5,4},{6,7},{7,6},{8,9},{9,8},{10,11... | collective-permute-start | bytes 73736 | tf_op jit(solution)/shard_map/ppermute | solution.py:545
  37.3 0.8 copy-start.5
  38.1 0.7 copy-start.7
  38.9 17.0 %collective-permute-start.4 = (bf16[384,384]{1,0:T(8,128)(2,1)}, bf16[384,384]{1,0:T(8,128)(2,1)}, u32[]{:S(2)}, u32[]{:S(2)}) collective-permute-start(bf16[384,384]{1,0:T(8,128)(2,1)} %get-tuple-element.25), channel_id=1, source_target_pairs={{0,3},{3,0},{1,2},{2,1},{4,7},{7,4},{5,6},{6,5},{8,11},{11,8},{9,1... | collective-permute-start | bytes 884744 | tf_op jit(solution)/shard_map/ppermute | solution.py:548
  40.4 9.7 %collective-permute-start.6 = (bf16[2,768]{1,0:T(2,128)(2,1)S(1)}, bf16[2,768]{1,0:T(2,128)(2,1)S(1)}, u32[]{:S(2)}, u32[]{:S(2)}) collective-permute-start(bf16[2,768]{1,0:T(2,128)(2,1)S(1)} %get-tuple-element.46), channel_id=1, source_target_pairs={{1,0},{2,1},{3,2},{4,3},{5,4},{6,5},{7,6},{8,7},{9,8},{10,9},{11,1... | collective-permute-start | bytes 9224 | tf_op jit(solution)/shard_map/ppermute | solution.py:517
  45.7 9.7 %collective-permute-start.5 = (bf16[2,768]{1,0:T(2,128)(2,1)S(1)}, bf16[2,768]{1,0:T(2,128)(2,1)S(1)}, u32[]{:S(2)}, u32[]{:S(2)}) collective-permute-start(bf16[2,768]{1,0:T(2,128)(2,1)S(1)} %get-tuple-element.47), channel_id=1, source_target_pairs={{0,1},{1,2},{2,3},{3,4},{4,5},{5,6},{6,7},{7,8},{8,9},{9,10},{10,1... | collective-permute-start | bytes 9224 | tf_op jit(solution)/shard_map/ppermute | solution.py:517
  47.6 8.3 %collective-permute-start.3 = (bf16[192,384]{1,0:T(8,128)(2,1)}, bf16[192,384]{1,0:T(8,128)(2,1)S(1)}, u32[]{:S(2)}, u32[]{:S(2)}) collective-permute-start(bf16[192,384]{1,0:T(8,128)(2,1)} %get-tuple-element.24), channel_id=1, source_target_pairs={{0,1},{1,0},{2,3},{3,2},{4,5},{5,4},{6,7},{7,6},{8,9},{9,8},{10,11... | collective-permute-start | bytes 442376 | tf_op jit(solution)/shard_map/ppermute | solution.py:547
  55.8 57.3 %collective-permute-start.9 = (bf16[784,768]{1,0:T(8,128)(2,1)S(1)}, bf16[784,768]{1,0:T(8,128)(2,1)S(1)}, u32[]{:S(2)}, u32[]{:S(2)}) collective-permute-start(bf16[784,768]{1,0:T(8,128)(2,1)S(1)} %concatenate.7.xp), channel_id=1, source_target_pairs={{0,32},{32,0},{1,33},{33,1},{2,34},{34,2},{3,35},{35,3},{4,36},{36... | collective-permute-start | bytes 3612680 | tf_op jit(solution)/shard_map/ppermute | solution.py:533
  55.9 1.1 copy-start.6
  56.9 1.0 copy-start.8
  59.8 0.8 copy-start.4
  60.6 0.7 copy-start.13
  61.3 0.7 copy-start.15
  62.0 45.7 %all-to-all-start.1 = ((bf16[8,48,768]{2,1,0:T(8,128)(2,1)}), bf16[8,48,768]{2,1,0:T(8,128)(2,1)S(1)}, u32[]{:S(2)}, u32[]{:S(2)}) async-start(bf16[8,48,768]{2,1,0:T(8,128)(2,1)} %bitcast.21), calls=%async_computation.1 | async-start | bytes 1179648 | tf_op jit(solution)/shard_map/all_to_all | solution.py:550
  65.7 2.7 %copy-start.11 = (bf16[5,768,768]{2,1,0:T(8,128)(2,1)S(1)}, bf16[5,768,768]{2,1,0:T(8,128)(2,1)}, u32[]{:S(2)}) copy-start(bf16[5,768,768]{2,1,0:T(8,128)(2,1)} %w.3) | copy-start | bytes 17694724
  75.6 1.0 copy-start.2
  107.7 5.9 %collective-permute-start.11 = (bf16[384,768]{1,0:T(8,128)(2,1)}, bf16[384,768]{1,0:T(8,128)(2,1)}, u32[]{:S(2)}, u32[]{:S(2)}) collective-permute-start(bf16[384,768]{1,0:T(8,128)(2,1)} %all_gather.3.p0), channel_id=1, source_target_pairs={{0,32},{32,0},{1,33},{33,1},{2,34},{34,2},{3,35},{35,3},{4,36},{36... | collective-permute-start | bytes 1769480 | tf_op jit(solution)/shard_map/ppermute | solution.py:536
  107.7 1.3 copy-start
  109.0 1.3 copy-start.3
  110.3 2.1 copy-start.16
  110.9 1.0 copy-start.9
  111.9 2.6 %collective-permute-start.10 = (bf16[768,384]{1,0:T(8,128)(2,1)S(1)}, bf16[768,384]{1,0:T(8,128)(2,1)S(1)}, u32[]{:S(2)}, u32[]{:S(2)}) collective-permute-start(bf16[768,384]{1,0:T(8,128)(2,1)S(1)} %get-tuple-element.35), channel_id=1, source_target_pairs={{0,32},{32,0},{1,33},{33,1},{2,34},{34,2},{3,35},{35,3},{4,36},{36... | collective-permute-start | bytes 1769480 | tf_op jit(solution)/shard_map/ppermute | solution.py:554
  112.4 2.1 copy-start.14
  112.4 2.0 collective-permute-start.12
  177.3 15.9 %copy-start.10 = (bf16[768,768]{1,0:T(8,128)(2,1)S(1)}, bf16[768,768]{1,0:T(8,128)(2,1)}, u32[]{:S(2)}) copy-start(bf16[768,768]{1,0:T(8,128)(2,1)} %copy-done.9) | copy-start | bytes 3538948
  177.3 31.2 %copy-start.1 = (bf16[1,768,768]{2,1,0:T(8,128)(2,1)S(1)}, bf16[1,768,768]{2,1,0:T(8,128)(2,1)}, u32[]{:S(2)}) copy-start(bf16[1,768,768]{2,1,0:T(8,128)(2,1)} %param.9) | copy-start | bytes 3538948
  177.3 12.7 %collective-permute-start.14 = (bf16[8,24,384]{2,1,0:T(8,128)(2,1)}, bf16[8,24,384]{2,1,0:T(8,128)(2,1)S(1)}, u32[]{:S(2)}, u32[]{:S(2)}) collective-permute-start(bf16[8,24,384]{2,1,0:T(8,128)(2,1)} %sum_proj.1.c), channel_id=1, source_target_pairs={{0,64},{64,0},{1,65},{65,1},{2,66},{66,2},{3,67},{67,3},{4,68},{68... | collective-permute-start | bytes 442376 | tf_op jit(solution)/shard_map/ppermute | solution.py:563
  183.8 6.3 %collective-permute-start.13 = (bf16[5,24,384]{2,1,0:T(8,128)(2,1)}, bf16[5,24,384]{2,1,0:T(8,128)(2,1)S(1)}, u32[]{:S(2)}, u32[]{:S(2)}) collective-permute-start(bf16[5,24,384]{2,1,0:T(8,128)(2,1)} %sum_conv.1.a), channel_id=1, source_target_pairs={{0,64},{64,0},{1,65},{65,1},{2,66},{66,2},{3,67},{67,3},{4,68},{68... | collective-permute-start | bytes 276488 | tf_op jit(solution)/shard_map/ppermute | solution.py:563
  190.1 0.6 copy-start.20
  190.7 0.7 copy-start.19
  193.3 25.2 %collective-permute-start.15 = (f32[13,24,384]{2,1,0:T(8,128)}, f32[13,24,384]{2,1,0:T(8,128)S(1)}, u32[]{:S(2)}, u32[]{:S(2)}) collective-permute-start(f32[13,24,384]{2,1,0:T(8,128)} %add_pair.1.mine), channel_id=1, source_target_pairs={{0,32},{32,0},{1,33},{33,1},{2,34},{34,2},{3,35},{35,3},{4,36},{36... | collective-permute-start | bytes 1437704 | tf_op jit(solution)/shard_map/ppermute | solution.py:564
  193.3 7.5 %collective-permute-start.8 = (bf16[2,768]{1,0:T(2,128)(2,1)S(1)}, bf16[2,768]{1,0:T(2,128)(2,1)S(1)}, u32[]{:S(2)}, u32[]{:S(2)}) collective-permute-start(bf16[2,768]{1,0:T(2,128)(2,1)S(1)} %get-tuple-element.44), channel_id=1, source_target_pairs={{1,0},{2,1},{3,2},{4,3},{5,4},{6,5},{7,6},{8,7},{9,8},{10,9},{11,1... | collective-permute-start | bytes 9224 | tf_op jit(solution)/shard_map/ppermute | solution.py:517
  198.8 9.7 %collective-permute-start.7 = (bf16[2,768]{1,0:T(2,128)(2,1)S(1)}, bf16[2,768]{1,0:T(2,128)(2,1)S(1)}, u32[]{:S(2)}, u32[]{:S(2)}) collective-permute-start(bf16[2,768]{1,0:T(2,128)(2,1)S(1)} %get-tuple-element.45), channel_id=1, source_target_pairs={{0,1},{1,2},{2,3},{3,4},{4,5},{5,6},{6,7},{7,8},{8,9},{9,10},{10,1... | collective-permute-start | bytes 9224 | tf_op jit(solution)/shard_map/ppermute | solution.py:517
  208.6 2.7 %copy-start.12 = (bf16[5,768,768]{2,1,0:T(8,128)(2,1)S(1)}, bf16[5,768,768]{2,1,0:T(8,128)(2,1)}, u32[]{:S(2)}) copy-start(bf16[5,768,768]{2,1,0:T(8,128)(2,1)} %w.3) | copy-start | bytes 17694724
  218.5 0.8 copy-start.18

commit v2 on v1

v2 whole, which is shorter than its diff:
```python
import jax
import jax.numpy as jnp
from jax import lax
from jax.experimental import pallas as pl
from jax.experimental.pallas import tpu as pltpu
from jax.sharding import Mesh, PartitionSpec as P

HEADS = 8
TAPS = 5
LOSS_SCALE = 32
HD = 192
C = 768
ROWS = 768
ATT = 48
BLK = 384
FACTOR = 16
HALF = 384
QH = 288
SCALE = HD ** (-0.5)
SQRT_HALF = 0.7071067811865476
INV_ROOT_TWO_PI = 0.3989422804014327

BF = jnp.bfloat16
F32 = jnp.float32
DP = ("yh", "core")
SEQ = ("yl", "x", "z")
HAX = ("yl", "x")

NT = (((1,), (1,)), ((), ()))
TN = (((0,), (0,)), ((), ()))

A_PAIR = [(0, 1), (1, 0), (2, 3), (3, 2)]
B_PAIR = [(0, 3), (3, 0), (1, 2), (2, 1)]
SWAP = [(0, 1), (1, 0)]


def sds(shape, dtype):
    return jax.ShapeDtypeStruct(shape, dtype)


def far(shape, dtype):
    return pltpu.HBM(shape, dtype)


def hbm(x):
    return pltpu.with_memory_space_constraint(x, pltpu.HBM)


def params(mib):
    return pltpu.CompilerParams(vmem_limit_bytes=mib * 1024 * 1024)


def cost(flops, nbytes, trans=0):
    return pl.CostEstimate(flops=flops, bytes_accessed=nbytes, transcendentals=trans)


VM = pl.BlockSpec(memory_space=pltpu.VMEM)
ANY = pl.BlockSpec(memory_space=pl.ANY)
SM = pl.BlockSpec(memory_space=pltpu.SMEM)


def nt(a, b):
    return lax.dot_general(a, b, NT, preferred_element_type=F32)


def tn(a, b):
    return lax.dot_general(a, b, TN, preferred_element_type=F32)


def mm(a, b):
    return jnp.dot(a, b, preferred_element_type=F32)


def pack_kernel(q, k, v, g, out):
    for h in range(HEADS):
        cols = slice(h * HD, (h + 1) * HD)
        for slot, ref in enumerate((q, g, k, v)):
            out[h, :, slot * HD : (slot + 1) * HD] = ref[:, cols]


def pack_heads(q, k, v, g):
    return pl.pallas_call(
        pack_kernel,
        out_shape=far((HEADS, ATT, 4 * HD), BF),
        in_specs=[VM] * 4,
        out_specs=VM,
        name="pack_heads",
        compiler_params=params(8),
        cost_estimate=cost(0, 1200000),
    )(hbm(q), hbm(k), hbm(v), hbm(g))


def att_parts(own, qg, kv):
    query = jnp.concatenate([own[:, 0:HD], qg[:, 0:HD]], axis=0)
    grads = jnp.concatenate([own[:, HD : 2 * HD], qg[:, HD : 2 * HD]], axis=0)
    keys = jnp.concatenate([own[:, 2 * HD : 3 * HD], kv[:, 0:HD]], axis=0)
    values = jnp.concatenate([own[:, 3 * HD : 4 * HD], kv[:, HD : 2 * HD]], axis=0)
    return query, grads, keys, values


def stats_kernel(own, qg, kv, after, out):
    query, grads, keys, values = att_parts(own, qg, kv)
    out[...] = jnp.zeros_like(out)
    for i in range(2):
        rows = slice(i * BLK, (i + 1) * BLK)
        scores = nt(keys, query[rows]) * SCALE
        top = jnp.max(scores, axis=0, keepdims=True)
        powers = jnp.exp(scores - top)
        pgrad = nt(values, grads[rows])
        out[0:1, rows] = top
        out[1:2, rows] = jnp.sum(powers, axis=0, keepdims=True)
        out[2:3, rows] = jnp.sum(powers * pgrad, axis=0, keepdims=True)


def att_stats(own, qg, kv, after):
    return pl.pallas_call(
        stats_kernel,
        out_shape=sds((8, 2 * BLK), F32),
        in_specs=[VM] * 3 + [ANY],
        out_specs=VM,
        name="att_stats",
        compiler_params=params(16),
        cost_estimate=cost(8000000000, 1200000, 768 * 768),
    )(own, qg, kv, after)


def grads_kernel(own, qg, kv, st, st2, dq_own, dq_send, dkv_own, dkv_send):
    query, grads, keys, values = att_parts(own, qg, kv)
    dk = jnp.zeros((2 * BLK, HD), F32)
    dv = jnp.zeros((2 * BLK, HD), F32)
    for i in range(2):
        rows = slice(i * BLK, (i + 1) * BLK)
        other = slice((1 - i) * BLK, (2 - i) * BLK)
        m0, m1 = st[0:1, rows], st2[0:1, other]
        top = jnp.maximum(m0, m1)
        e0, e1 = jnp.exp(m0 - top), jnp.exp(m1 - top)
        inv = 1.0 / (st[1:2, rows] * e0 + st2[1:2, other] * e1)
        delta = (st[2:3, rows] * e0 + st2[2:3, other] * e1) * inv
        scores = nt(keys, query[rows]) * SCALE
        probs = jnp.exp(scores - top) * inv
        pgrad = nt(values, grads[rows])
        sgrad = (probs * (pgrad - delta)).astype(BF)
        dq = tn(sgrad, keys) * SCALE
        dk = dk + mm(sgrad, query[rows])
        dv = dv + mm(probs.astype(BF), grads[rows])
        if i == 0:
            dq_own[...] = dq
        else:
            dq_send[:, 0:HD] = dq[0 : BLK // 2].astype(BF)
            dq_send[:, HD : 2 * HD] = dq[BLK // 2 : BLK].astype(BF)
    dk = dk * SCALE
    dkv_own[:, 0:HD] = dk[0:BLK]
    dkv_own[:, HD : 2 * HD] = dv[0:BLK]
    dkv_send[:, 0:HD] = dk[BLK:].astype(BF)
    dkv_send[:, HD : 2 * HD] = dv[BLK:].astype(BF)


def att_grads(own, qg, kv, st, st2):
    return pl.pallas_call(
        grads_kernel,
        out_shape=(
            sds((BLK, HD), F32),
            sds((BLK // 2, 2 * HD), BF),
            sds((BLK, 2 * HD), F32),
            sds((BLK, 2 * HD), BF),
        ),
        in_specs=[VM] * 5,
        out_specs=(VM,) * 4,
        name="att_grads",
        compiler_params=params(20),
        cost_estimate=cost(20000000000, 3000000, 768 * 768),
    )(own, qg, kv, st, st2)


def split_kernel(own, qg, kv):
    qg[...] = own[:, 0 : 2 * HD]
    kv[...] = own[:, 2 * HD : 4 * HD]


def split_own(own):
    return pl.pallas_call(
        split_kernel,
        out_shape=(sds((BLK, 2 * HD), BF), sds((BLK, 2 * HD), BF)),
        in_specs=[VM],
        out_specs=(VM, VM),
        name="split_own",
        compiler_params=params(8),
        cost_estimate=cost(0, 1200000),
    )(own)


def head_kernel(pair, odd, wq, wk, wv, out):
    for p, ref in enumerate((wq, wk, wv)):
        turned = ref[...].T

        @pl.when(odd[0] == 0)
        def _():
            out[p * HD : (p + 1) * HD, :] = turned[0:HD]

        @pl.when(odd[0] != 0)
        def _():
            out[p * HD : (p + 1) * HD, :] = turned[HD : 2 * HD]


def head_weights(pair, odd, weight):
    part = lambda p: pl.BlockSpec((C, 2 * HD), lambda i, pair, odd, p=p: (0, 4 * p + pair[0]))
    return pl.pallas_call(
        head_kernel,
        out_shape=sds((3 * HD, C), BF),
        grid_spec=pltpu.PrefetchScalarGridSpec(
            num_scalar_prefetch=2,
            grid=(1,),
            in_specs=[part(0), part(1), part(2)],
            out_specs=pl.BlockSpec((3 * HD, C), lambda i, pair, odd: (0, 0)),
        ),
        name="head_weights",
        compiler_params=params(12),
        cost_estimate=cost(0, 3000000),
    )(pair, odd, hbm(weight), hbm(weight), hbm(weight))


def join_kernel(core, dq_own, dkv_own, dq_in, dkv_in, wh, after, pool, keep, send):
    dq_got = jnp.concatenate([dq_in[:, 0:HD], dq_in[:, HD : 2 * HD]], axis=0).astype(F32)
    dq = (dq_own[...] + dq_got).astype(BF)
    dkv = (dkv_own[...] + dkv_in[...].astype(F32)).astype(BF)
    qkv = jnp.concatenate([dq, dkv], axis=1)
    pool[...] = mm(qkv, wh[...]).astype(BF)

    @pl.when(core[0] == 0)
    def _():
        keep[...] = qkv[:, 0:QH]
        send[...] = qkv[:, QH : 2 * QH]

    @pl.when(core[0] != 0)
    def _():
        keep[...] = qkv[:, QH : 2 * QH]
        send[...] = qkv[:, 0:QH]


def att_join(core, dq_own, dkv_own, dq_in, dkv_in, wh, after):
    return pl.pallas_call(
        join_kernel,
        out_shape=(far((BLK, C), BF), sds((BLK, QH), BF), sds((BLK, QH), BF)),
        in_specs=[SM] + [VM] * 5 + [ANY],
        out_specs=(VM,) * 3,
        name="att_join",
        compiler_params=params(12),
        cost_estimate=cost(10000000000, 3500000),
    )(core, dq_own, dkv_own, dq_in, dkv_in, wh, after)


def forward_kernel(xp, w, after, slope, pooled, xf, acc):
    tap = pl.program_id(0)

    @pl.when(tap == 0)
    def _():
        xf[...] = xp[...].astype(F32)

    for t in range(TAPS):

        @pl.when(tap == t)
        def _(t=t):
            for r in range(0, ROWS, 256):
                rows = xf[6 + t + r : 6 + t + r + 256, :].astype(BF)
                got = mm(rows, w[0])
                if t == 0:
                    acc[r : r + 256, :] = got
                else:
                    acc[r : r + 256, :] += got

    @pl.when(tap == TAPS - 1)
    def _():
        @pl.loop(0, ROWS // 64)
        def _(i):
            at = pl.multiple_of(i * 64, 64)
            pre = acc[pl.ds(at, 64), :]
            cumul = 0.5 * (1.0 + lax.erf(pre * SQRT_HALF))
            slope[pl.ds(at, 64), :] = (
                cumul + pre * INV_ROOT_TWO_PI * jnp.exp(-0.5 * pre * pre)
            ).astype(BF)
            rows = xf[pl.ds(pl.multiple_of(at + 8, 8), 64), :]
            block = (rows + pre * cumul).astype(BF).astype(F32)
            acc[pl.ds(pl.multiple_of(i * 8, 8), 8), :] = jnp.concatenate(
                [jnp.mean(block.reshape(4, FACTOR, C), axis=1), jnp.zeros((4, C), F32)], axis=0
            )

        for i in range(ROWS // 64):
            xf[4 * i : 4 * i + 4, :] = acc[8 * i : 8 * i + 4, :]
        rows = xf[0:ATT, :].astype(BF)
        for h in range(HEADS):
            pooled[h] = rows


def conv_forward(xp, w, after):
    return pl.pallas_call(
        forward_kernel,
        grid=(TAPS,),
        out_shape=(sds((ROWS, C), BF), far((HEADS, ATT, C), BF)),
        in_specs=[
            pl.BlockSpec((ROWS + 16, C), lambda t: (0, 0)),
            pl.BlockSpec((1, C, C), lambda t: (t, 0, 0)),
            ANY,
        ],
        out_specs=(
            pl.BlockSpec((ROWS, C), lambda t: (0, 0)),
            pl.BlockSpec((HEADS, ATT, C), lambda t: (0, 0, 0)),
        ),
        scratch_shapes=[pltpu.VMEM((ROWS + 16, C), F32), pltpu.VMEM((ROWS, C), F32)],
        name="conv_forward",
        compiler_params=params(20),
        cost_estimate=cost(2 * 5 * 768**3, 9500000, 2 * 768 * 768),
    )(xp, hbm(w), after)


def turn_kernel(xp, xt, alts, edge):
    for r in range(0, ROWS, 128):
        xt[:, r : r + 128] = xp[8 + r : 8 + r + 128, :].T
    last = xp[8 + ROWS - 128 : 8 + ROWS, :].astype(F32)
    first = xp[8 : 8 + 128, :].astype(F32)
    top = xp[0:16, :].astype(F32)[0:8]
    bottom = xp[ROWS : ROWS + 16, :].astype(F32)[8:16]
    edge[...] = last
    edge[126:128, :] = top[6:8]
    alts[:, 0:128] = edge[...].astype(BF).T
    edge[126:127, :] = last[126:127]
    alts[:, 128:256] = edge[...].astype(BF).T
    edge[...] = first
    edge[0:1, :] = bottom[0:1]
    alts[:, 256:384] = edge[...].astype(BF).T
    edge[1:2, :] = bottom[1:2]
    alts[:, 384:512] = edge[...].astype(BF).T


def turn_input(xp):
    return pl.pallas_call(
        turn_kernel,
        out_shape=(sds((C, ROWS), BF), sds((C, 512), BF)),
        in_specs=[VM],
        out_specs=(VM, VM),
        scratch_shapes=[pltpu.VMEM((128, C), F32)],
        name="turn_input",
        compiler_params=params(12),
        cost_estimate=cost(10 * 768 * 768, 3200000),
    )(xp)


def slope_kernel(core, parts, skip, slope, pre, send, keep, pool):
    total = jnp.sum(parts[...].astype(F32), axis=0) * (1.0 / FACTOR)
    pool[...] = total
    for r in range(0, ATT, 8):
        piece = jnp.broadcast_to(total[r : r + 8, None, :], (8, FACTOR, C)).reshape(128, C)
        rows = slice(r * FACTOR, r * FACTOR + 128)
        grad = (skip[rows, :].astype(F32) + piece) * slope[rows, :].astype(F32)
        pre[rows, :] = grad.astype(BF)

    @pl.when(core[0] == 0)
    def _():
        keep[...] = pre[:, 0:HALF]
        send[...] = pre[:, HALF:]

    @pl.when(core[0] != 0)
    def _():
        keep[...] = pre[:, HALF:]
        send[...] = pre[:, 0:HALF]


def pre_grads(core, parts, skip, slope):
    return pl.pallas_call(
        slope_kernel,
        out_shape=(
            sds((ROWS, C), BF),
            sds((ROWS, HALF), BF),
            sds((ROWS, HALF), BF),
            sds((ATT, C), F32),
        ),
        in_specs=[SM] + [VM] * 3,
        out_specs=(VM,) * 4,
        name="pre_grads",
        compiler_params=params(12),
        cost_estimate=cost(5 * 768 * 768, 6000000),
    )(core, parts, skip, slope)


def weights_kernel(xt0, al0, xt1, al1, y0, y1, p0, p1, s0, s1, out, yf, yt, made, sems):
    def copy(t):
        cols = pl.ds(t * HALF, HALF)
        return pltpu.make_async_copy(made.at[t], out.at[:, cols], sems.at[t])

    def shifted(xt, al, t, rows):
        if t < 2:
            return jnp.concatenate([xt[rows, : ROWS - 128], al[rows, t * 128 : t * 128 + 128]], axis=1)
        if t > 2:
            return jnp.concatenate([al[rows, (t - 1) * 128 : t * 128], xt[rows, 128:]], axis=1)
        return xt[rows, :]

    made[TAPS, :, 0:QH] = (tn(p0[...], s0[...]) + tn(p1[...], s1[...])).astype(BF)
    made[TAPS, :, QH:HALF] = jnp.zeros((C, HALF - QH), BF)
    copy(TAPS).start()
    for i, ref in enumerate((y0, y1)):
        got = ref[...].astype(F32)
        yf[i, 8 : 8 + ROWS, :] = got
        yf[i, 0:8, :] = got[ROWS - 8 :]
        yf[i, 8 + ROWS : 16 + ROWS, :] = got[0:8]
    for t in (2, 0, 1, 3, 4):
        if t == 2:
            right = [y0[...], y1[...]]
        else:
            for i in range(2):
                yt[t, i] = yf[i, 10 - t : 10 - t + ROWS, :].astype(BF)
            right = [yt[t, 0], yt[t, 1]]
        for r in range(0, C, 256):
            rows = slice(r, r + 256)
            made[t, rows, :] = (
                mm(shifted(xt0, al0, t, rows), right[0]) + mm(shifted(xt1, al1, t, rows), right[1])
            ).astype(BF)
        copy(t).start()
    for t in range(TAPS + 1):
        copy(t).wait()


def weight_grads(xt0, al0, xt1, al1, y0, y1, p0, p1, s0, s1):
    return pl.pallas_call(
        weights_kernel,
        out_shape=far((C, 2304), BF),
        in_specs=[VM] * 10,
        out_specs=pl.BlockSpec(memory_space=pltpu.HBM),
        scratch_shapes=[
            pltpu.VMEM((2, ROWS + 16, HALF), F32),
            pltpu.VMEM((TAPS, 2, ROWS, HALF), BF),
            pltpu.VMEM((TAPS + 1, C, HALF), BF),
            pltpu.SemaphoreType.DMA((TAPS + 1,)),
        ],
        name="weight_grads",
        compiler_params=params(32),
        cost_estimate=cost(2 * 5 * 768 * 1536 * 384, 10000000),
    )(xt0, al0, xt1, al1, y0, y1, p0, p1, s0, s1)


def adjoint_kernel(pre, w, skip, pool, out, before, after, first, last, yf, acc):
    tap = pl.program_id(0)

    @pl.when(tap == 0)
    def _():
        yf[0:16, :] = jnp.zeros((16, C), F32)
        yf[16 : 16 + ROWS, :] = pre[...].astype(F32)
        yf[16 + ROWS :, :] = jnp.zeros((16, C), F32)
        acc[0:8, :] = jnp.zeros((8, C), F32)
        acc[8 + ROWS :, :] = jnp.zeros((8, C), F32)
        for r in range(0, ATT, 8):
            piece = jnp.broadcast_to(pool[r : r + 8, :][:, None, :], (8, FACTOR, C)).reshape(128, C)
            rows = slice(r * FACTOR, r * FACTOR + 128)
            acc[8 + r * FACTOR : 136 + r * FACTOR, :] = skip[rows, :].astype(F32) + piece

    for t in range(TAPS):

        @pl.when(tap == t)
        def _(t=t):
            for r, n in ((0, 256), (256, 256), (512, 272)):
                rows = yf[10 - t + r : 10 - t + r + n, :].astype(BF)
                acc[r : r + n, :] += nt(rows, w[0])

    @pl.when(tap == TAPS - 1)
    def _():
        out[...] = acc[8 : 8 + ROWS, :].astype(BF)
        before[...] = acc[0:8, :]
        first[...] = acc[8:16, :]
        last[...] = acc[ROWS : ROWS + 8, :]
        after[...] = acc[ROWS + 8 :, :]


def conv_adjoint(pre, w, skip, pool):
    whole = lambda a, b: pl.BlockSpec((a, b), lambda t: (0, 0))
    return pl.pallas_call(
        adjoint_kernel,
        grid=(TAPS,),
        out_shape=(far((ROWS, C), BF),) + (sds((8, C), F32),) * 4,
        in_specs=[
            whole(ROWS, C),
            pl.BlockSpec((1, C, C), lambda t: (t, 0, 0)),
            whole(ROWS, C),
            whole(ATT, C),
        ],
        out_specs=(whole(ROWS, C),) + (whole(8, C),) * 4,
        scratch_shapes=[pltpu.VMEM((ROWS + 32, C), F32), pltpu.VMEM((ROWS + 16, C), F32)],
        name="conv_adjoint",
        compiler_params=params(24),
        cost_estimate=cost(2 * 5 * 768**3, 9500000),
    )(pre, hbm(w), skip, pool)


def edge_kernel(rows, first, last, top, bottom, out):
    step = pl.program_id(0)
    held = rows[...].astype(F32)

    @pl.when(step == 0)
    def _():
        out[...] = jnp.concatenate([first[...] + top[...], held[8:16]], axis=0).astype(BF)

    @pl.when(step != 0)
    def _():
        out[...] = jnp.concatenate([held[0:8], last[...] + bottom[...]], axis=0).astype(BF)


def add_edges(rows, first, last, top, bottom):
    block = pl.BlockSpec((16, C), lambda i: (i * (ROWS // 16 - 1), 0))
    whole = pl.BlockSpec((8, C), lambda i: (0, 0))
    return pl.pallas_call(
        edge_kernel,
        grid=(2,),
        out_shape=far((ROWS, C), BF),
        in_specs=[block, whole, whole, whole, whole],
        out_specs=block,
        input_output_aliases={0: 0},
        name="add_edges",
        compiler_params=params(8),
        cost_estimate=cost(30000, 150000),
    )(hbm(rows), first, last, top, bottom)


def sum_kernel(parts, after, after2, out):
    step = pl.program_id(0)

    @pl.when(step < TAPS)
    def _():
        total = parts[0].astype(F32)
        for s in range(1, 32):
            total = total + parts[s].astype(F32)
        out[step] = total.astype(BF)

    @pl.when(step == TAPS)
    def _():
        for h in range(HEADS):
            total = parts[4 * h].astype(F32)
            for s in range(4 * h + 1, 4 * h + 4):
                total = total + parts[s].astype(F32)
            out[TAPS + h] = total.astype(BF)


def sum_partials(parts, after, after2):
    return pl.pallas_call(
        sum_kernel,
        grid=(TAPS + 1,),
        out_shape=sds((TAPS + HEADS, 24, HALF), BF),
        in_specs=[pl.BlockSpec((32, 24, HALF), lambda t: (0, 0, t)), ANY, ANY],
        out_specs=pl.BlockSpec((TAPS + HEADS, 24, HALF), lambda t: (0, 0, 0)),
        name="sum_partials",
        compiler_params=params(8),
        cost_estimate=cost(32 * 24 * 2304, 3700000),
    )(parts, after, after2)


def add_kernel(a, b, after, out):
    out[...] = (a[...].astype(F32) + b[...].astype(F32)) * (1.0 / LOSS_SCALE)


def add_pair(a, b, after):
    return pl.pallas_call(
        add_kernel,
        out_shape=sds((TAPS + HEADS, 24, HALF), F32),
        in_specs=[VM] * 2 + [ANY],
        out_specs=VM,
        name="add_pair",
        compiler_params=params(8),
        cost_estimate=cost(300000, 1500000),
    )(a, b, after)


def place_kernel(core, mine, other, conv, proj):
    def put(low, high):
        conv[:, :, 0:HALF] = low[0:TAPS]
        conv[:, :, HALF:] = high[0:TAPS]
        for h in range(HEADS):
            at = h * HD
            proj[:, at : at + HD] = low[TAPS + h, :, 0:HD]
            proj[:, 1536 + at : 1536 + at + HD] = jnp.concatenate(
                [low[TAPS + h, :, HD:QH], high[TAPS + h, :, 0 : HD // 2]], axis=1
            )
            proj[:, 3072 + at : 3072 + at + HD] = high[TAPS + h, :, HD // 2 : QH]

    @pl.when(core[0] == 0)
    def _():
        put(mine, other)

    @pl.when(core[0] != 0)
    def _():
        put(other, mine)


def place(core, mine, other):
    return pl.pallas_call(
        place_kernel,
        out_shape=(far((TAPS, 24, C), F32), far((24, 4608), F32)),
        in_specs=[SM, VM, VM],
        out_specs=(VM, VM),
        name="place",
        compiler_params=params(8),
        cost_estimate=cost(0, 2500000),
    )(core, mine, other)


UP = [(i, i + 1) for i in range(31)]
DOWN = [(i + 1, i) for i in range(31)]


def local(conv_input, skip_grad, conv_weight, proj_weight, query, key, value, grad):
    core = lax.axis_index("core").astype(jnp.int32).reshape(1)
    head = lax.axis_index(HAX).astype(jnp.int32)
    pair, odd = (head // 2).reshape(1), (head % 2).reshape(1)
    x, skip = conv_input[0], skip_grad[0]

    packed = pack_heads(query[0], key[0], value[0], grad[0])
    own = lax.all_to_all(packed, HAX, 0, 0, tiled=True).reshape(BLK, 4 * HD)
    qg_own, kv_own = split_own(own)
    qg = lax.ppermute(qg_own, "z", A_PAIR)
    kv = lax.ppermute(kv_own, "z", B_PAIR)

    top = lax.ppermute(x[ROWS - 2 :], SEQ, UP)
    bottom = lax.ppermute(x[0:2], SEQ, DOWN)
    edge = jnp.zeros((6, C), BF)
    xp = jnp.concatenate([edge, top, x, bottom, edge], axis=0)
    xp_sib = lax.ppermute(xp, "core", SWAP)
    slope, pooled = conv_forward(xp, conv_weight, own)
    wh = head_weights(pair, odd, proj_weight)

    st = att_stats(own, qg, kv, slope)
    st2 = lax.ppermute(st, "z", A_PAIR)
    dq_own, dq_send, dkv_own, dkv_send = att_grads(own, qg, kv, st, st2)
    dq_in = lax.ppermute(dq_send, "z", A_PAIR)
    dkv_in = lax.ppermute(dkv_send, "z", B_PAIR)
    pooled_blk = lax.all_to_all(pooled, HAX, 0, 0, tiled=True).reshape(BLK, C)
    pool_part, s0, s_send = att_join(core, dq_own, dkv_own, dq_in, dkv_in, wh, pooled_blk)
    parts = lax.all_to_all(pool_part.reshape(HEADS, ATT, C), HAX, 0, 0, tiled=True)
    pooled_sib = lax.ppermute(pooled_blk, "core", SWAP)
    s1 = lax.ppermute(s_send, "core", SWAP)
    xt0, al0 = turn_input(xp)
    xt1, al1 = turn_input(xp_sib)

    pre, y_send, y0, pool = pre_grads(core, parts, skip, slope)
    y1 = lax.ppermute(y_send, "core", SWAP)
    terms = weight_grads(xt0, al0, xt1, al1, y0, y1, pooled_blk, pooled_sib, s0, s1)
    got = lax.all_to_all(terms.reshape(32, 24, 2304), SEQ, 0, 0, tiled=True)

    rows, before, after, first, last = conv_adjoint(pre, conv_weight, skip, pool)
    from_left = lax.ppermute(after, SEQ, UP)
    from_right = lax.ppermute(before, SEQ, DOWN)

    total = sum_partials(got, from_left, from_right)
    total_far = lax.ppermute(total, "yh", SWAP)
    input_grad = add_edges(rows, first, last, from_left, from_right)
    mine = add_pair(total, total_far, input_grad)
    other = lax.ppermute(mine, "core", SWAP)
    conv_grad, proj_grad = place(core, mine, other)
    return input_grad[None], conv_grad, proj_grad


def solution(mesh):
    fine = Mesh(mesh.devices.reshape(2, 2, 2, 4, 4), ("yh", "core", "yl", "x", "z"))
    rows = P(DP, SEQ, None)
    return jax.shard_map(
        local,
        mesh=fine,
        in_specs=(rows, rows, P(), P(), rows, rows, rows, rows),
        out_specs=(rows, P(None, SEQ, None), P(SEQ, None)),
        check_vma=False,
    )
```

time: 223 us -> 163 us (0.73)
  the two profiles are of different devices: /device:TPU:8 before, /device:TPU:7 now
where the time goes in v2:
time: 163 us; the launch traced here: 161 us
  starting transfers between devices  58.9 us (36%)
  Pallas kernels  43.1 us (26%)
  waiting for transfers between devices  39.3 us (24%)
  local copies, waits for them, and re-layouts  19 us (12%)
    ppermute x1, waiting for transfers between devices, local(): from_left = lax.ppermute(after, SEQ, UP)  26.3 us
    unnamed x56, local copies, waits for them, and re-layouts  18.6 us
    pallas_call x1, Pallas kernels, weight_grads(): pl.pallas_call(weights_kernel, out_shape=far((C, 2304), BF), in_specs=[VM...  9.67 us
    pallas_call x1, Pallas kernels, conv_forward(): pl.pallas_call(forward_kernel, grid=(TAPS,), out_shape=(sds((ROWS, C), BF...  9.67 us
    pallas_call x1, Pallas kernels, conv_adjoint(): pl.pallas_call(adjoint_kernel, grid=(TAPS,), out_shape=(far((ROWS, C), BF...  8.33 us
    all_to_all x1, starting transfers between devices, local(): got = lax.all_to_all(terms.reshape(32, 24, 2304), SEQ, 0, 0, tiled=True)  6.43 us
    ppermute x1, starting transfers between devices, local(): bottom = lax.ppermute(x[0:2], SEQ, DOWN)  5.96 us
    all_to_all x1, starting transfers between devices, local(): pooled_blk = lax.all_to_all(pooled, HAX, 0, 0, tiled=True).reshape(BLK, C)  5.69 us
  transfers between devices with their start and end apart: 19, of which 6 were waited for; matrix products, arithmetic and copies ran while one was open for 0% of the time, Pallas kernels for 17%

profile of v2, /device:TPU:7, one launch (start us, length us, event | category | flops | bytes accessed | tf_op | source)
XLA Modules:
  0.0 161.3 jit_solution(7766368007986580866)
XLA Ops:
  0.6 2.2 %pack_heads.1 = bf16[8,48,768]{2,1,0:T(8,128)(2,1)} custom-call(bf16[48,1536]{1,0:T(8,128)(2,1)} %bitcast.28, bf16[48,1536]{1,0:T(8,128)(2,1)} %bitcast.29, bf16[48,1536]{1,0:T(8,128)(2,1)} %bitcast.30, bf16[48,1536]{1,0:T(8,128)(2,1)} %bitcast.31), custom_call_target="tpu_custom_call" | custom-call | bytes 1200000 | tf_op jit(solution)/shard_map/pack_heads/pallas_call | solution.py:82
  2.8 5.2 %all-to-all-start = ((bf16[8,48,768]{2,1,0:T(8,128)(2,1)}), bf16[8,48,768]{2,1,0:T(8,128)(2,1)S(1)}, u32[]{:S(2)}, u32[]{:S(2)}) async-start(bf16[8,48,768]{2,1,0:T(8,128)(2,1)} %pack_heads.1), calls=%async_computation | async-start | bytes 1179648 | tf_op jit(solution)/shard_map/all_to_all | solution.py:612
  8.1 6.0 %collective-permute-start.3 = (bf16[2,768]{1,0:T(2,128)(2,1)S(1)}, bf16[2,768]{1,0:T(2,128)(2,1)S(1)}, u32[]{:S(2)}, u32[]{:S(2)}) collective-permute-start(bf16[2,768]{1,0:T(2,128)(2,1)S(1)} %get-tuple-element.55), channel_id=1, source_target_pairs={{1,0},{2,1},{3,2},{4,3},{5,4},{6,5},{7,6},{8,7},{9,8},{10,9},{11,1... | collective-permute-start | bytes 9224 | tf_op jit(solution)/shard_map/ppermute | solution.py:618
  14.1 1.9 %collective-permute-start.2 = (bf16[2,768]{1,0:T(2,128)(2,1)S(1)}, bf16[2,768]{1,0:T(2,128)(2,1)S(1)}, u32[]{:S(2)}, u32[]{:S(2)}) collective-permute-start(bf16[2,768]{1,0:T(2,128)(2,1)S(1)} %get-tuple-element.56), channel_id=1, source_target_pairs={{0,1},{1,2},{2,3},{3,4},{4,5},{5,6},{6,7},{7,8},{8,9},{9,10},{10,1... | collective-permute-start | bytes 9224 | tf_op jit(solution)/shard_map/ppermute | solution.py:617
  16.0 4.5 %collective-permute-done.2 = bf16[2,768]{1,0:T(2,128)(2,1)S(1)} collective-permute-done((bf16[2,768]{1,0:T(2,128)(2,1)S(1)}, bf16[2,768]{1,0:T(2,128)(2,1)S(1)}, u32[]{:S(2)}, u32[]{:S(2)}) %collective-permute-start.2) | collective-permute-done | bytes 3104 | tf_op jit(solution)/shard_map/ppermute | solution.py:617
  21.1 1.7 %collective-permute-start.1 = (bf16[384,384]{1,0:T(8,128)(2,1)S(1)}, bf16[384,384]{1,0:T(8,128)(2,1)S(1)}, u32[]{:S(2)}, u32[]{:S(2)}) collective-permute-start(bf16[384,384]{1,0:T(8,128)(2,1)S(1)} %get-tuple-element.30), channel_id=1, source_target_pairs={{0,3},{3,0},{1,2},{2,1},{4,7},{7,4},{5,6},{6,5},{8,11},{11,8},{9,1... | collective-permute-start | bytes 884744 | tf_op jit(solution)/shard_map/ppermute | solution.py:615
  22.7 9.7 %conv_forward.1 = (bf16[768,768]{1,0:T(8,128)(2,1)S(1)}, bf16[8,48,768]{2,1,0:T(8,128)(2,1)}) custom-call(bf16[784,768]{1,0:T(8,128)(2,1)S(1)} %concatenate.3.xp, bf16[5,768,768]{2,1,0:T(8,128)(2,1)} %w.3, bf16[384,768]{1,0:T(8,128)(2,1)S(1)} %bitcast.20), custom_call_target="tpu_custom_call" | custom-call | flops 4529848320 | bytes 9500000 | tf_op jit(solution)/shard_map/conv_forward/pallas_call | solution.py:295
  32.4 1.2 att_stats.1.st
  33.6 0.8 collective-permute-start.4
  34.4 5.7 %all-to-all-start.1 = ((bf16[8,48,768]{2,1,0:T(8,128)(2,1)}), bf16[8,48,768]{2,1,0:T(8,128)(2,1)}, u32[]{:S(2)}, u32[]{:S(2)}) async-start(bf16[8,48,768]{2,1,0:T(8,128)(2,1)} %get-tuple-element.36), calls=%async_computation.1 | async-start | bytes 1179648 | tf_op jit(solution)/shard_map/all_to_all | solution.py:630
  40.1 2.5 %att_grads.1 = (f32[384,192]{1,0:T(8,128)S(1)}, bf16[192,384]{1,0:T(8,128)(2,1)S(1)}, f32[384,384]{1,0:T(8,128)S(1)}, bf16[384,384]{1,0:T(8,128)(2,1)S(1)}) custom-call(bf16[384,768]{1,0:T(8,128)(2,1)S(1)} %bitcast.22, bf16[384,384]{1,0:T(8,128)(2,1)S(1)} %collective-permute-done.qg, bf16[384,384]{1,0:T(8,128)(2,1)S(1)} %collective-permute-done.1.kv, ...), custom_call_target="tpu_custom_call" | custom-call | flops 20000000000 | bytes 3000000 | tf_op jit(solution)/shard_map/att_grads/pallas_call | solution.py:159
  42.6 0.8 copy-done.23
  43.5 0.7 copy-done.25
  44.2 2.1 %collective-permute-start.6 = (bf16[384,384]{1,0:T(8,128)(2,1)S(1)}, bf16[384,384]{1,0:T(8,128)(2,1)S(1)}, u32[]{:S(2)}, u32[]{:S(2)}) collective-permute-start(bf16[384,384]{1,0:T(8,128)(2,1)S(1)} %get-tuple-element.35), channel_id=1, source_target_pairs={{0,3},{3,0},{1,2},{2,1},{4,7},{7,4},{5,6},{6,5},{8,11},{11,8},{9,1... | collective-permute-start | bytes 884744 | tf_op jit(solution)/shard_map/ppermute | solution.py:629
  46.4 2.1 %head_weights.1.wh = bf16[576,768]{1,0:T(8,128)(2,1)S(1)} custom-call(s32[1]{0:T(128)} %bitcast.9.pair, s32[1]{0:T(128)} %bitcast.10.odd, bf16[768,4608]{1,0:T(8,128)(2,1)} %wv.1, bf16[768,4608]{1,0:T(8,128)(2,1)} %wv.1, bf16[768,4608]{1,0:T(8,128)(2,1)} %wv.1), custom_call_target="tpu_custom_call" | custom-call | bytes 3000000 | tf_op jit(solution)/shard_map/head_weights/pallas_call | solution.py:207
  48.5 0.9 copy-done.5
  49.4 4.3 %collective-permute-start.9 = (bf16[784,768]{1,0:T(8,128)(2,1)S(1)}, bf16[784,768]{1,0:T(8,128)(2,1)S(1)}, u32[]{:S(2)}, u32[]{:S(2)}) collective-permute-start(bf16[784,768]{1,0:T(8,128)(2,1)S(1)} %concatenate.3.xp), channel_id=1, source_target_pairs={{0,32},{32,0},{1,33},{33,1},{2,34},{34,2},{3,35},{35,3},{4,36},{36... | collective-permute-start | bytes 3612680 | tf_op jit(solution)/shard_map/ppermute | solution.py:621
  53.8 1.2 copy-done.6
  54.9 1.1 copy-done.24
  56.0 1.0 copy-done.26
  57.0 1.9 %att_join.1 = (bf16[384,768]{1,0:T(8,128)(2,1)}, bf16[384,288]{1,0:T(8,128)(2,1)S(1)}, bf16[384,288]{1,0:T(8,128)(2,1)S(1)}) custom-call(s32[1]{0:T(128)} %bitcast.core, f32[384,192]{1,0:T(8,128)S(1)} %copy-done.26, f32[384,384]{1,0:T(8,128)S(1)} %copy-done.24, bf16[192,384]{1,0:T(8,128)(2,1)S(1)} %collective-permute-done.5.dq_in, ...), custom_call_target="tpu_custom_call" | custom-call | flops 10000000000 | bytes 3500000 | tf_op jit(solution)/shard_map/att_join/pallas_call | solution.py:241
  59.6 5.1 %all-to-all-start.2 = ((bf16[8,48,768]{2,1,0:T(8,128)(2,1)}), bf16[8,48,768]{2,1,0:T(8,128)(2,1)S(1)}, u32[]{:S(2)}, u32[]{:S(2)}) async-start(bf16[8,48,768]{2,1,0:T(8,128)(2,1)} %bitcast.27), calls=%async_computation.2 | async-start | bytes 1179648 | tf_op jit(solution)/shard_map/all_to_all | solution.py:632
  64.7 2.7 %collective-permute-start.11 = (bf16[384,768]{1,0:T(8,128)(2,1)}, bf16[384,768]{1,0:T(8,128)(2,1)}, u32[]{:S(2)}, u32[]{:S(2)}) collective-permute-start(bf16[384,768]{1,0:T(8,128)(2,1)} %bitcast.11.after.p0), channel_id=1, source_target_pairs={{0,32},{32,0},{1,33},{33,1},{2,34},{34,2},{3,35},{35,3},{4,36},{36... | collective-permute-start | bytes 1769480 | tf_op jit(solution)/shard_map/ppermute | solution.py:633
  67.4 3.4 %all-to-all-done.2.parts = bf16[8,48,768]{2,1,0:T(8,128)(2,1)S(1)} async-done(((bf16[8,48,768]{2,1,0:T(8,128)(2,1)}), bf16[8,48,768]{2,1,0:T(8,128)(2,1)S(1)}, u32[]{:S(2)}, u32[]{:S(2)}) %all-to-all-start.2) | async-done | bytes 589856 | tf_op jit(solution)/shard_map/all_to_all | solution.py:632
  70.8 1.3 copy-done.1
  72.1 1.3 copy-done.4
  74.0 1.0 copy-done.17
  75.0 3.6 %collective-permute-start.10 = (bf16[768,384]{1,0:T(8,128)(2,1)S(1)}, bf16[768,384]{1,0:T(8,128)(2,1)S(1)}, u32[]{:S(2)}, u32[]{:S(2)}) collective-permute-start(bf16[768,384]{1,0:T(8,128)(2,1)S(1)} %get-tuple-element.50), channel_id=1, source_target_pairs={{0,32},{32,0},{1,33},{33,1},{2,34},{34,2},{3,35},{35,3},{4,36},{36... | collective-permute-start | bytes 1769480 | tf_op jit(solution)/shard_map/ppermute | solution.py:639
  79.8 0.9 collective-permute-done.12.s1
  80.7 9.7 %weight_grads.1 = bf16[768,2304]{1,0:T(8,128)(2,1)} custom-call(bf16[768,768]{1,0:T(8,128)(2,1)S(1)} %get-tuple-element.45.xt0, bf16[768,512]{1,0:T(8,128)(2,1)S(1)} %get-tuple-element.46.al0, bf16[768,768]{1,0:T(8,128)(2,1)S(1)} %get-tuple-element.47.xt1, bf16[768,512]{1,0:T(8,128)(2,1)S(1)} %get-tuple-element.48.al1, ...), custom_call_target="tpu_custom_call" | custom-call | flops 4529848320 | bytes 10000000 | tf_op jit(solution)/shard_map/weight_grads/pallas_call | solution.py:422
  90.4 6.4 %all-to-all-start.3 = ((bf16[32,24,2304]{2,1,0:T(8,128)(2,1)}), bf16[32,24,2304]{2,1,0:T(8,128)(2,1)S(1)}, u32[]{:S(2)}, u32[]{:S(2)}) async-start(bf16[32,24,2304]{2,1,0:T(8,128)(2,1)} %bitcast.25), calls=%async_computation.3 | async-start | bytes 7077888 | tf_op jit(solution)/shard_map/all_to_all | solution.py:641
  96.8 1.3 copy-done.2
  98.1 1.3 copy-done.18
  99.4 0.9 copy-done.20
  100.3 8.3 %conv_adjoint.1 = (bf16[768,768]{1,0:T(8,128)(2,1)}, f32[8,768]{1,0:T(8,128)S(1)}, f32[8,768]{1,0:T(8,128)S(1)}, f32[8,768]{1,0:T(8,128)S(1)}, f32[8,768]{1,0:T(8,128)S(1)}) custom-call(bf16[768,768]{1,0:T(8,128)(2,1)S(1)} %copy-done.18, bf16[5,768,768]{2,1,0:T(8,128)(2,1)} %w.3, bf16[768,768]{1,0:T(8,128)(2,1)S(1)} %bitcast.24, f32[48,768]{1,0:T(8,128)S(1)} %copy-done.20), custom_call_target="tpu_custom_call" | custom-call | flops 4529848320 | bytes 9500000 | tf_op jit(solution)/shard_map/conv_adjoint/pallas_call | solution.py:473
  109.8 3.1 %collective-permute-start.7 = (f32[8,768]{1,0:T(8,128)S(1)}, f32[8,768]{1,0:T(8,128)S(1)}, u32[]{:S(2)}, u32[]{:S(2)}) collective-permute-start(f32[8,768]{1,0:T(8,128)S(1)} %get-tuple-element.43), channel_id=1, source_target_pairs={{0,1},{1,2},{2,3},{3,4},{4,5},{5,6},{6,7},{7,8},{8,9},{9,10},{10,1... | collective-permute-start | bytes 73736 | tf_op jit(solution)/shard_map/ppermute | solution.py:644
  112.9 4.3 %collective-permute-start.8 = (f32[8,768]{1,0:T(8,128)S(1)}, f32[8,768]{1,0:T(8,128)S(1)}, u32[]{:S(2)}, u32[]{:S(2)}) collective-permute-start(f32[8,768]{1,0:T(8,128)S(1)} %get-tuple-element.44), channel_id=1, source_target_pairs={{1,0},{2,1},{3,2},{4,3},{5,4},{6,5},{7,6},{8,7},{9,8},{10,9},{11,1... | collective-permute-start | bytes 73736 | tf_op jit(solution)/shard_map/ppermute | solution.py:645
  117.2 26.3 %collective-permute-done.7.top.after = f32[8,768]{1,0:T(8,128)S(1)} collective-permute-done((f32[8,768]{1,0:T(8,128)S(1)}, f32[8,768]{1,0:T(8,128)S(1)}, u32[]{:S(2)}, u32[]{:S(2)}) %collective-permute-start.7) | collective-permute-done | bytes 24608 | tf_op jit(solution)/shard_map/ppermute | solution.py:644
  144.7 0.7 copy-done.8
  145.5 0.7 copy-done.11
  146.2 1.0 sum_partials.1.a
  147.2 2.7 %collective-permute-start.13 = (bf16[13,24,384]{2,1,0:T(8,128)(2,1)S(1)}, bf16[13,24,384]{2,1,0:T(8,128)(2,1)S(1)}, u32[]{:S(2)}, u32[]{:S(2)}) collective-permute-start(bf16[13,24,384]{2,1,0:T(8,128)(2,1)S(1)} %sum_partials.1.a), channel_id=1, source_target_pairs={{0,64},{64,0},{1,65},{65,1},{2,66},{66,2},{3,67},{67,3},{4,68},{68... | collective-permute-start | bytes 718856 | tf_op jit(solution)/shard_map/ppermute | solution.py:648
  150.0 1.4 add_edges.1.after
  151.3 2.8 %collective-permute-done.13.b = bf16[13,24,384]{2,1,0:T(8,128)(2,1)S(1)} collective-permute-done((bf16[13,24,384]{2,1,0:T(8,128)(2,1)S(1)}, bf16[13,24,384]{2,1,0:T(8,128)(2,1)S(1)}, u32[]{:S(2)}, u32[]{:S(2)}) %collective-permute-start.13) | collective-permute-done | bytes 239648 | tf_op jit(solution)/shard_map/ppermute | solution.py:648
  154.1 1.3 copy-done
  155.5 3.0 %collective-permute-start.14 = (f32[13,24,384]{2,1,0:T(8,128)S(1)}, f32[13,24,384]{2,1,0:T(8,128)S(1)}, u32[]{:S(2)}, u32[]{:S(2)}) collective-permute-start(f32[13,24,384]{2,1,0:T(8,128)S(1)} %add_pair.1.mine), channel_id=1, source_target_pairs={{0,32},{32,0},{1,33},{33,1},{2,34},{34,2},{3,35},{35,3},{4,36},{36... | collective-permute-start | bytes 1437704 | tf_op jit(solution)/shard_map/ppermute | solution.py:651
  158.5 1.5 collective-permute-done.14.other
  160.0 1.3 place.1
  (65 shorter events, 5.7 us)
Async XLA Ops:
  0.6 7.4 %copy-start.27 = (bf16[1,768,768]{2,1,0:T(8,128)(2,1)S(1)}, bf16[1,768,768]{2,1,0:T(8,128)(2,1)}, u32[]{:S(2)}) copy-start(bf16[1,768,768]{2,1,0:T(8,128)(2,1)} %param.8) | copy-start | bytes 3538948
  2.8 18.1 %all-to-all-start = ((bf16[8,48,768]{2,1,0:T(8,128)(2,1)}), bf16[8,48,768]{2,1,0:T(8,128)(2,1)S(1)}, u32[]{:S(2)}, u32[]{:S(2)}) async-start(bf16[8,48,768]{2,1,0:T(8,128)(2,1)} %pack_heads.1), calls=%async_computation | async-start | bytes 1179648 | tf_op jit(solution)/shard_map/all_to_all | solution.py:612
  8.1 7.9 %collective-permute-start.3 = (bf16[2,768]{1,0:T(2,128)(2,1)S(1)}, bf16[2,768]{1,0:T(2,128)(2,1)S(1)}, u32[]{:S(2)}, u32[]{:S(2)}) collective-permute-start(bf16[2,768]{1,0:T(2,128)(2,1)S(1)} %get-tuple-element.55), channel_id=1, source_target_pairs={{1,0},{2,1},{3,2},{4,3},{5,4},{6,5},{7,6},{8,7},{9,8},{10,9},{11,1... | collective-permute-start | bytes 9224 | tf_op jit(solution)/shard_map/ppermute | solution.py:618
  14.1 6.5 %collective-permute-start.2 = (bf16[2,768]{1,0:T(2,128)(2,1)S(1)}, bf16[2,768]{1,0:T(2,128)(2,1)S(1)}, u32[]{:S(2)}, u32[]{:S(2)}) collective-permute-start(bf16[2,768]{1,0:T(2,128)(2,1)S(1)} %get-tuple-element.56), channel_id=1, source_target_pairs={{0,1},{1,2},{2,3},{3,4},{4,5},{5,6},{6,7},{7,8},{8,9},{9,10},{10,1... | collective-permute-start | bytes 9224 | tf_op jit(solution)/shard_map/ppermute | solution.py:617
  21.0 11.4 %collective-permute-start = (bf16[384,384]{1,0:T(8,128)(2,1)S(1)}, bf16[384,384]{1,0:T(8,128)(2,1)S(1)}, u32[]{:S(2)}, u32[]{:S(2)}) collective-permute-start(bf16[384,384]{1,0:T(8,128)(2,1)S(1)} %get-tuple-element.29), channel_id=1, source_target_pairs={{0,1},{1,0},{2,3},{3,2},{4,5},{5,4},{6,7},{7,6},{8,9},{9,8},{10,11... | collective-permute-start | bytes 884744 | tf_op jit(solution)/shard_map/ppermute | solution.py:614
  21.1 11.3 %collective-permute-start.1 = (bf16[384,384]{1,0:T(8,128)(2,1)S(1)}, bf16[384,384]{1,0:T(8,128)(2,1)S(1)}, u32[]{:S(2)}, u32[]{:S(2)}) collective-permute-start(bf16[384,384]{1,0:T(8,128)(2,1)S(1)} %get-tuple-element.30), channel_id=1, source_target_pairs={{0,3},{3,0},{1,2},{2,1},{4,7},{7,4},{5,6},{6,5},{8,11},{11,8},{9,1... | collective-permute-start | bytes 884744 | tf_op jit(solution)/shard_map/ppermute | solution.py:615
  32.4 1.2 copy-start.3
  33.6 6.5 %collective-permute-start.4 = (f32[8,768]{1,0:T(8,128)S(1)}, f32[8,768]{1,0:T(8,128)S(1)}, u32[]{:S(2)}, u32[]{:S(2)}) collective-permute-start(f32[8,768]{1,0:T(8,128)S(1)} %att_stats.1.st), channel_id=1, source_target_pairs={{0,1},{1,0},{2,3},{3,2},{4,5},{5,4},{6,7},{7,6},{8,9},{9,8},{10,11... | collective-permute-start | bytes 73736 | tf_op jit(solution)/shard_map/ppermute | solution.py:626
  34.4 19.3 %all-to-all-start.1 = ((bf16[8,48,768]{2,1,0:T(8,128)(2,1)}), bf16[8,48,768]{2,1,0:T(8,128)(2,1)}, u32[]{:S(2)}, u32[]{:S(2)}) async-start(bf16[8,48,768]{2,1,0:T(8,128)(2,1)} %get-tuple-element.36), calls=%async_computation.1 | async-start | bytes 1179648 | tf_op jit(solution)/shard_map/all_to_all | solution.py:630
  42.6 0.8 copy-start.23
  43.5 0.7 copy-start.25
  44.2 9.6 %collective-permute-start.6 = (bf16[384,384]{1,0:T(8,128)(2,1)S(1)}, bf16[384,384]{1,0:T(8,128)(2,1)S(1)}, u32[]{:S(2)}, u32[]{:S(2)}) collective-permute-start(bf16[384,384]{1,0:T(8,128)(2,1)S(1)} %get-tuple-element.35), channel_id=1, source_target_pairs={{0,3},{3,0},{1,2},{2,1},{4,7},{7,4},{5,6},{6,5},{8,11},{11,8},{9,1... | collective-permute-start | bytes 884744 | tf_op jit(solution)/shard_map/ppermute | solution.py:629
  46.3 7.5 %collective-permute-start.5 = (bf16[192,384]{1,0:T(8,128)(2,1)S(1)}, bf16[192,384]{1,0:T(8,128)(2,1)S(1)}, u32[]{:S(2)}, u32[]{:S(2)}) collective-permute-start(bf16[192,384]{1,0:T(8,128)(2,1)S(1)} %get-tuple-element.34), channel_id=1, source_target_pairs={{0,1},{1,0},{2,3},{3,2},{4,5},{5,4},{6,7},{7,6},{8,9},{9,8},{10,11... | collective-permute-start | bytes 442376 | tf_op jit(solution)/shard_map/ppermute | solution.py:628
  48.5 0.9 copy-start.5
  49.4 29.8 %collective-permute-start.9 = (bf16[784,768]{1,0:T(8,128)(2,1)S(1)}, bf16[784,768]{1,0:T(8,128)(2,1)S(1)}, u32[]{:S(2)}, u32[]{:S(2)}) collective-permute-start(bf16[784,768]{1,0:T(8,128)(2,1)S(1)} %concatenate.3.xp), channel_id=1, source_target_pairs={{0,32},{32,0},{1,33},{33,1},{2,34},{34,2},{3,35},{35,3},{4,36},{36... | collective-permute-start | bytes 3612680 | tf_op jit(solution)/shard_map/ppermute | solution.py:621
  53.8 1.2 copy-start.6
  54.9 1.1 copy-start.24
  56.0 1.0 copy-start.26
  58.9 0.7 copy-start.21
  59.6 11.2 %all-to-all-start.2 = ((bf16[8,48,768]{2,1,0:T(8,128)(2,1)}), bf16[8,48,768]{2,1,0:T(8,128)(2,1)S(1)}, u32[]{:S(2)}, u32[]{:S(2)}) async-start(bf16[8,48,768]{2,1,0:T(8,128)(2,1)} %bitcast.27), calls=%async_computation.2 | async-start | bytes 1179648 | tf_op jit(solution)/shard_map/all_to_all | solution.py:632
  64.7 16.0 %collective-permute-start.11 = (bf16[384,768]{1,0:T(8,128)(2,1)}, bf16[384,768]{1,0:T(8,128)(2,1)}, u32[]{:S(2)}, u32[]{:S(2)}) collective-permute-start(bf16[384,768]{1,0:T(8,128)(2,1)} %bitcast.11.after.p0), channel_id=1, source_target_pairs={{0,32},{32,0},{1,33},{33,1},{2,34},{34,2},{3,35},{35,3},{4,36},{36... | collective-permute-start | bytes 1769480 | tf_op jit(solution)/shard_map/ppermute | solution.py:633
  70.8 1.3 copy-start.1
  72.1 1.3 copy-start.4
  74.0 1.0 copy-start.17
  75.0 4.8 %copy-start.19 = (f32[48,768]{1,0:T(8,128)}, f32[48,768]{1,0:T(8,128)S(1)}, u32[]{:S(2)}) copy-start(f32[48,768]{1,0:T(8,128)S(1)} %get-tuple-element.39.pool) | copy-start | bytes 442372
  75.0 5.7 %collective-permute-start.10 = (bf16[768,384]{1,0:T(8,128)(2,1)S(1)}, bf16[768,384]{1,0:T(8,128)(2,1)S(1)}, u32[]{:S(2)}, u32[]{:S(2)}) collective-permute-start(bf16[768,384]{1,0:T(8,128)(2,1)S(1)} %get-tuple-element.50), channel_id=1, source_target_pairs={{0,32},{32,0},{1,33},{33,1},{2,34},{34,2},{3,35},{35,3},{4,36},{36... | collective-permute-start | bytes 1769480 | tf_op jit(solution)/shard_map/ppermute | solution.py:639
  78.6 2.1 %copy-start.22 = (bf16[384,288]{1,0:T(8,128)(2,1)S(1)}, bf16[384,288]{1,0:T(8,128)(2,1)}, u32[]{:S(2)}) copy-start(bf16[384,288]{1,0:T(8,128)(2,1)} %copy-done.21) | copy-start | bytes 663556
  78.6 2.1 %collective-permute-start.12 = (bf16[384,288]{1,0:T(8,128)(2,1)S(1)}, bf16[384,288]{1,0:T(8,128)(2,1)S(1)}, u32[]{:S(2)}, u32[]{:S(2)}) collective-permute-start(bf16[384,288]{1,0:T(8,128)(2,1)S(1)} %get-tuple-element.52), channel_id=1, source_target_pairs={{0,32},{32,0},{1,33},{33,1},{2,34},{34,2},{3,35},{35,3},{4,36},{36... | collective-permute-start | bytes 663560 | tf_op jit(solution)/shard_map/ppermute | solution.py:634
  90.4 54.3 %all-to-all-start.3 = ((bf16[32,24,2304]{2,1,0:T(8,128)(2,1)}), bf16[32,24,2304]{2,1,0:T(8,128)(2,1)S(1)}, u32[]{:S(2)}, u32[]{:S(2)}) async-start(bf16[32,24,2304]{2,1,0:T(8,128)(2,1)} %bitcast.25), calls=%async_computation.3 | async-start | bytes 7077888 | tf_op jit(solution)/shard_map/all_to_all | solution.py:641
  96.8 1.3 copy-start.2
  98.1 1.3 copy-start.18
  99.3 0.9 copy-start.20
  108.6 0.6 copy-start.13
  109.2 0.6 copy-start.15
  109.8 33.7 %collective-permute-start.7 = (f32[8,768]{1,0:T(8,128)S(1)}, f32[8,768]{1,0:T(8,128)S(1)}, u32[]{:S(2)}, u32[]{:S(2)}) collective-permute-start(f32[8,768]{1,0:T(8,128)S(1)} %get-tuple-element.43), channel_id=1, source_target_pairs={{0,1},{1,2},{2,3},{3,4},{4,5},{5,6},{6,7},{7,8},{8,9},{9,10},{10,1... | collective-permute-start | bytes 73736 | tf_op jit(solution)/shard_map/ppermute | solution.py:644
  112.9 31.2 %collective-permute-start.8 = (f32[8,768]{1,0:T(8,128)S(1)}, f32[8,768]{1,0:T(8,128)S(1)}, u32[]{:S(2)}, u32[]{:S(2)}) collective-permute-start(f32[8,768]{1,0:T(8,128)S(1)} %get-tuple-element.44), channel_id=1, source_target_pairs={{1,0},{2,1},{3,2},{4,3},{5,4},{6,5},{7,6},{8,7},{9,8},{10,9},{11,1... | collective-permute-start | bytes 73736 | tf_op jit(solution)/shard_map/ppermute | solution.py:645
  143.5 0.6 copy-start.7
  144.1 0.6 copy-start.10
  144.7 0.7 copy-start.8
  145.5 0.7 copy-start.11
  146.2 3.8 %copy-start.9 = (f32[8,768]{1,0:T(8,128)S(1)}, f32[8,768]{1,0:T(8,128)}, u32[]{:S(2)}) copy-start(f32[8,768]{1,0:T(8,128)} %copy-done.7) | copy-start | bytes 73732
  146.2 3.8 %copy-start.12 = (f32[8,768]{1,0:T(8,128)S(1)}, f32[8,768]{1,0:T(8,128)}, u32[]{:S(2)}) copy-start(f32[8,768]{1,0:T(8,128)} %copy-done.10) | copy-start | bytes 73732
  146.2 3.8 %copy-start.14 = (f32[8,768]{1,0:T(8,128)S(1)}, f32[8,768]{1,0:T(8,128)}, u32[]{:S(2)}) copy-start(f32[8,768]{1,0:T(8,128)} %copy-done.13) | copy-start | bytes 73732
  146.2 3.8 %copy-start.16 = (f32[8,768]{1,0:T(8,128)S(1)}, f32[8,768]{1,0:T(8,128)}, u32[]{:S(2)}) copy-start(f32[8,768]{1,0:T(8,128)} %copy-done.15) | copy-start | bytes 73732
  147.2 6.9 %collective-permute-start.13 = (bf16[13,24,384]{2,1,0:T(8,128)(2,1)S(1)}, bf16[13,24,384]{2,1,0:T(8,128)(2,1)S(1)}, u32[]{:S(2)}, u32[]{:S(2)}) collective-permute-start(bf16[13,24,384]{2,1,0:T(8,128)(2,1)S(1)} %sum_partials.1.a), channel_id=1, source_target_pairs={{0,64},{64,0},{1,65},{65,1},{2,66},{66,2},{3,67},{67,3},{4,68},{68... | collective-permute-start | bytes 718856 | tf_op jit(solution)/shard_map/ppermute | solution.py:648
  154.1 1.3 copy-start
  155.5 4.5 %collective-permute-start.14 = (f32[13,24,384]{2,1,0:T(8,128)S(1)}, f32[13,24,384]{2,1,0:T(8,128)S(1)}, u32[]{:S(2)}, u32[]{:S(2)}) collective-permute-start(f32[13,24,384]{2,1,0:T(8,128)S(1)} %add_pair.1.mine), channel_id=1, source_target_pairs={{0,32},{32,0},{1,33},{33,1},{2,34},{34,2},{3,35},{35,3},{4,36},{36... | collective-permute-start | bytes 1437704 | tf_op jit(solution)/shard_map/ppermute | solution.py:651

commit v3 on v2

--- a/solution.py
+++ b/solution.py
@@ -16,6 +16,7 @@
 FACTOR = 16
 HALF = 384
 QH = 288
+WIDE = 5 * HALF + 8 * QH
 SCALE = HD ** (-0.5)
 SQRT_HALF = 0.7071067811865476
 INV_ROOT_TWO_PI = 0.3989422804014327
@@ -54,7 +55,7 @@
     return pl.CostEstimate(flops=flops, bytes_accessed=nbytes, transcendentals=trans)
 
 
-VM = pl.BlockSpec(memory_space=pltpu.VMEM)
+VM = pl.BlockSpec()
 ANY = pl.BlockSpec(memory_space=pl.ANY)
 SM = pl.BlockSpec(memory_space=pltpu.SMEM)
 
@@ -121,10 +122,10 @@
         name="att_stats",
         compiler_params=params(16),
         cost_estimate=cost(8000000000, 1200000, 768 * 768),
-    )(own, qg, kv, after)
-
-
-def grads_kernel(own, qg, kv, st, st2, dq_own, dq_send, dkv_own, dkv_send):
+    )(own, qg, kv, hbm(after))
+
+
+def grads_kernel(own, qg, kv, st, st2, after, dq_own, dq_send, dkv_own, dkv_send):
     query, grads, keys, values = att_parts(own, qg, kv)
     dk = jnp.zeros((2 * BLK, HD), F32)
     dv = jnp.zeros((2 * BLK, HD), F32)
@@ -155,41 +156,41 @@
     dkv_send[:, HD : 2 * HD] = dv[BLK:].astype(BF)
 
 
-def att_grads(own, qg, kv, st, st2):
+def att_grads(own, qg, kv, st, st2, after):
     return pl.pallas_call(
         grads_kernel,
         out_shape=(
-            sds((BLK, HD), F32),
+            far((BLK, HD), F32),
             sds((BLK // 2, 2 * HD), BF),
-            sds((BLK, 2 * HD), F32),
+            far((BLK, 2 * HD), F32),
             sds((BLK, 2 * HD), BF),
         ),
-        in_specs=[VM] * 5,
+        in_specs=[VM] * 5 + [ANY],
         out_specs=(VM,) * 4,
         name="att_grads",
         compiler_params=params(20),
         cost_estimate=cost(20000000000, 3000000, 768 * 768),
-    )(own, qg, kv, st, st2)
-
-
-def split_kernel(own, qg, kv):
+    )(own, qg, kv, st, st2, hbm(after))
+
+
+def split_kernel(own, after, qg, kv):
     qg[...] = own[:, 0 : 2 * HD]
     kv[...] = own[:, 2 * HD : 4 * HD]
 
 
-def split_own(own):
+def split_own(own, after):
     return pl.pallas_call(
         split_kernel,
         out_shape=(sds((BLK, 2 * HD), BF), sds((BLK, 2 * HD), BF)),
-        in_specs=[VM],
+        in_specs=[VM, ANY],
         out_specs=(VM, VM),
         name="split_own",
         compiler_params=params(8),
         cost_estimate=cost(0, 1200000),
-    )(own)
-
-
-def head_kernel(pair, odd, wq, wk, wv, out):
+    )(own, hbm(after))
+
+
+def head_kernel(pair, odd, wq, wk, wv, after, out):
     for p, ref in enumerate((wq, wk, wv)):
         turned = ref[...].T
 
@@ -202,29 +203,40 @@
             out[p * HD : (p + 1) * HD, :] = turned[HD : 2 * HD]
 
 
-def head_weights(pair, odd, weight):
+def head_weights(pair, odd, weight, after):
     part = lambda p: pl.BlockSpec((C, 2 * HD), lambda i, pair, odd, p=p: (0, 4 * p + pair[0]))
     return pl.pallas_call(
         head_kernel,
-        out_shape=sds((3 * HD, C), BF),
+        out_shape=far((3 * HD, C), BF),
         grid_spec=pltpu.PrefetchScalarGridSpec(
             num_scalar_prefetch=2,
             grid=(1,),
-            in_specs=[part(0), part(1), part(2)],
+            in_specs=[part(0), part(1), part(2), ANY],
             out_specs=pl.BlockSpec((3 * HD, C), lambda i, pair, odd: (0, 0)),
         ),
         name="head_weights",
         compiler_params=params(12),
         cost_estimate=cost(0, 3000000),
-    )(pair, odd, hbm(weight), hbm(weight), hbm(weight))
-
-
-def join_kernel(core, dq_own, dkv_own, dq_in, dkv_in, wh, after, pool, keep, send):
+    )(pair, odd, hbm(weight), hbm(weight), hbm(weight), after)
+
+
+def join_kernel(core, dq_own, dkv_own, dq_in, dkv_in, wh, pooled, pool, keep, send, made, sems, sem2):
+    others = [
+        pltpu.make_async_copy(pooled, pool.at[h, pl.ds(ATT, ATT)], sem2.at[h]) for h in range(HEADS)
+    ]
+    for other in others:
+        other.start()
     dq_got = jnp.concatenate([dq_in[:, 0:HD], dq_in[:, HD : 2 * HD]], axis=0).astype(F32)
     dq = (dq_own[...] + dq_got).astype(BF)
     dkv = (dkv_own[...] + dkv_in[...].astype(F32)).astype(BF)
     qkv = jnp.concatenate([dq, dkv], axis=1)
-    pool[...] = mm(qkv, wh[...]).astype(BF)
+    stores = []
+    for r in range(0, BLK, 2 * ATT):
+        made[r : r + 2 * ATT, :] = mm(qkv[r : r + 2 * ATT], wh[...]).astype(BF)
+        for h in (r // ATT, r // ATT + 1):
+            rows = pl.ds(h * ATT, ATT)
+            stores.append(pltpu.make_async_copy(made.at[rows], pool.at[h, pl.ds(0, ATT)], sems.at[h]))
+            stores[-1].start()
 
     @pl.when(core[0] == 0)
     def _():
@@ -236,80 +248,107 @@
         keep[...] = qkv[:, QH : 2 * QH]
         send[...] = qkv[:, 0:QH]
 
-
-def att_join(core, dq_own, dkv_own, dq_in, dkv_in, wh, after):
+    for copy in others + stores:
+        copy.wait()
+
+
+def att_join(core, dq_own, dkv_own, dq_in, dkv_in, wh, pooled):
     return pl.pallas_call(
         join_kernel,
-        out_shape=(far((BLK, C), BF), sds((BLK, QH), BF), sds((BLK, QH), BF)),
-        in_specs=[SM] + [VM] * 5 + [ANY],
-        out_specs=(VM,) * 3,
+        out_shape=(far((HEADS, 2 * ATT, C), BF), sds((BLK, QH), BF), sds((BLK, QH), BF)),
+        in_specs=[SM] + [VM] * 6,
+        out_specs=(pl.BlockSpec(memory_space=pltpu.HBM), VM, VM),
+        scratch_shapes=[
+            pltpu.VMEM((BLK, C), BF),
+            pltpu.SemaphoreType.DMA((HEADS,)),
+            pltpu.SemaphoreType.DMA((HEADS,)),
+        ],
         name="att_join",
         compiler_params=params(12),
         cost_estimate=cost(10000000000, 3500000),
-    )(core, dq_own, dkv_own, dq_in, dkv_in, wh, after)
-
-
-def forward_kernel(xp, w, after, slope, pooled, xf, acc):
-    tap = pl.program_id(0)
-
-    @pl.when(tap == 0)
-    def _():
-        xf[...] = xp[...].astype(F32)
-
+    )(core, hbm(dq_own), hbm(dkv_own), dq_in, dkv_in, hbm(wh), hbm(pooled))
+
+
+def conv_kernel(par, x, got1, got2, w, after, pre, xp, xb, xf, wv, pv, xsem, wsems, psems):
+    chunks = range(0, ROWS, 256)
+    load = pltpu.make_async_copy(x, xb, xsem)
+    loads = [pltpu.make_async_copy(w.at[t], wv.at[t], wsems.at[t]) for t in range(TAPS)]
+    stores = [
+        pltpu.make_async_copy(pv.at[pl.ds(r, 256)], pre.at[pl.ds(r, 256)], psems.at[r // 256])
+        for r in chunks
+    ]
+    load.start()
+    loads[0].start()
+    xf[0:8, :] = jnp.zeros((8, C), F32)
+    xf[8 + ROWS :, :] = jnp.zeros((8, C), F32)
+    even = par[0] == 0
+    one, two = got1[...].astype(F32), got2[...].astype(F32)
+    xf[6:8, :] = jnp.where(even, two, one)
+    xf[8 + ROWS : 10 + ROWS, :] = jnp.where(even, one, two)
+    load.wait()
+    loads[1].start()
+    xf[8 : 8 + ROWS, :] = xb[...].astype(F32)
     for t in range(TAPS):
-
-        @pl.when(tap == t)
-        def _(t=t):
-            for r in range(0, ROWS, 256):
-                rows = xf[6 + t + r : 6 + t + r + 256, :].astype(BF)
-                got = mm(rows, w[0])
-                if t == 0:
-                    acc[r : r + 256, :] = got
-                else:
-                    acc[r : r + 256, :] += got
-
-    @pl.when(tap == TAPS - 1)
-    def _():
-        @pl.loop(0, ROWS // 64)
-        def _(i):
-            at = pl.multiple_of(i * 64, 64)
-            pre = acc[pl.ds(at, 64), :]
-            cumul = 0.5 * (1.0 + lax.erf(pre * SQRT_HALF))
-            slope[pl.ds(at, 64), :] = (
-                cumul + pre * INV_ROOT_TWO_PI * jnp.exp(-0.5 * pre * pre)
-            ).astype(BF)
-            rows = xf[pl.ds(pl.multiple_of(at + 8, 8), 64), :]
-            block = (rows + pre * cumul).astype(BF).astype(F32)
-            acc[pl.ds(pl.multiple_of(i * 8, 8), 8), :] = jnp.concatenate(
-                [jnp.mean(block.reshape(4, FACTOR, C), axis=1), jnp.zeros((4, C), F32)], axis=0
-            )
-
-        for i in range(ROWS // 64):
-            xf[4 * i : 4 * i + 4, :] = acc[8 * i : 8 * i + 4, :]
-        rows = xf[0:ATT, :].astype(BF)
-        for h in range(HEADS):
-            pooled[h] = rows
-
-
-def conv_forward(xp, w, after):
-    return pl.pallas_call(
-        forward_kernel,
-        grid=(TAPS,),
-        out_shape=(sds((ROWS, C), BF), far((HEADS, ATT, C), BF)),
-        in_specs=[
-            pl.BlockSpec((ROWS + 16, C), lambda t: (0, 0)),
-            pl.BlockSpec((1, C, C), lambda t: (t, 0, 0)),
-            ANY,
+        loads[t].wait()
+        if t + 2 < TAPS:
+            loads[t + 2].start()
+        for r in chunks:
+            got = mm(xf[6 + t + r : 6 + t + r + 256, :].astype(BF), wv[t])
+            if t == 0:
+                pv[r : r + 256, :] = got
+            else:
+                pv[r : r + 256, :] += got
+            if t == TAPS - 1:
+                stores[r // 256].start()
+    xp[...] = xf[...].astype(BF)
+    for store in stores:
+        store.wait()
+
+
+def conv_apply(par, x, got1, got2, w, after):
+    near = pl.BlockSpec(memory_space=pltpu.HBM)
+    return pl.pallas_call(
+        conv_kernel,
+        out_shape=(far((ROWS, C), F32), sds((ROWS + 16, C), BF)),
+        in_specs=[SM, near, VM, VM, near, ANY],
+        out_specs=(near, VM),
+        scratch_shapes=[
+            pltpu.VMEM((ROWS, C), BF),
+            pltpu.VMEM((ROWS + 16, C), F32),
+            pltpu.VMEM((TAPS, C, C), BF),
+            pltpu.VMEM((ROWS, C), F32),
+            pltpu.SemaphoreType.DMA,
+            pltpu.SemaphoreType.DMA((TAPS,)),
+            pltpu.SemaphoreType.DMA((3,)),
         ],
-        out_specs=(
-            pl.BlockSpec((ROWS, C), lambda t: (0, 0)),
-            pl.BlockSpec((HEADS, ATT, C), lambda t: (0, 0, 0)),
-        ),
-        scratch_shapes=[pltpu.VMEM((ROWS + 16, C), F32), pltpu.VMEM((ROWS, C), F32)],
-        name="conv_forward",
-        compiler_params=params(20),
-        cost_estimate=cost(2 * 5 * 768**3, 9500000, 2 * 768 * 768),
-    )(xp, hbm(w), after)
+        name="conv_apply",
+        compiler_params=params(24),
+        cost_estimate=cost(2 * 5 * 768**3, 9500000),
+    )(par, hbm(x), got1, got2, hbm(w), after)
+
+
+def gelu_kernel(pre, x, after, slope, pooled, means):
+    for p in range(0, ROWS, 64):
+        value = pre[p : p + 64, :]
+        cumul = 0.5 * (1.0 + lax.erf(value * SQRT_HALF))
+        bell = value * INV_ROOT_TWO_PI * jnp.exp(-0.5 * value * value)
+        slope[p : p + 64, :] = (cumul + bell).astype(BF)
+        block = (x[p : p + 64, :].astype(F32) + value * cumul).astype(BF).astype(F32)
+        means[p // FACTOR : p // FACTOR + 4, :] = jnp.mean(block.reshape(4, FACTOR, C), axis=1)
+    pooled[...] = means[...].astype(BF)
+
+
+def gelu_pool(pre, x, after):
+    return pl.pallas_call(
+        gelu_kernel,
+        out_shape=(far((ROWS, C), BF), far((ATT, C), BF)),
+        in_specs=[VM, VM, ANY],
+        out_specs=(VM, VM),
+        scratch_shapes=[pltpu.VMEM((ATT, C), F32)],
+        name="gelu_pool",
+        compiler_params=params(16),
+        cost_estimate=cost(3000000000, 5000000, 2 * 768 * 768),
+    )(hbm(pre), hbm(x), after)
 
 
 def turn_kernel(xp, xt, alts, edge):
@@ -344,41 +383,73 @@
     )(xp)
 
 
-def slope_kernel(core, parts, skip, slope, pre, send, keep, pool):
-    total = jnp.sum(parts[...].astype(F32), axis=0) * (1.0 / FACTOR)
-    pool[...] = total
-    for r in range(0, ATT, 8):
-        piece = jnp.broadcast_to(total[r : r + 8, None, :], (8, FACTOR, C)).reshape(128, C)
-        rows = slice(r * FACTOR, r * FACTOR + 128)
-        grad = (skip[rows, :].astype(F32) + piece) * slope[rows, :].astype(F32)
-        pre[rows, :] = grad.astype(BF)
+def slope_kernel(
+    core, parts, skip, slope, pre, send, keep, pool, skip_v, slope_v, pre_v, pool_v, in_sems, out_sems, pool_sem
+):
+    chunks = range(0, ROWS, 256)
+    loads = []
+    for r in chunks:
+        rows = pl.ds(r, 256)
+        loads.append(pltpu.make_async_copy(skip.at[rows], skip_v.at[rows], in_sems.at[0, r // 256]))
+        loads.append(pltpu.make_async_copy(slope.at[rows], slope_v.at[rows], in_sems.at[1, r // 256]))
+    for load in loads:
+        load.start()
+    total = jnp.sum(parts[:, 0:ATT, :].astype(F32), axis=0) * (1.0 / FACTOR)
+    pool_v[...] = total
+    stores = [pltpu.make_async_copy(pool_v, pool, pool_sem)]
+    stores[0].start()
+    for r in chunks:
+        loads[r // 128].wait()
+        loads[r // 128 + 1].wait()
+        for p in range(r, r + 256, 128):
+            j = p // FACTOR
+            piece = jnp.broadcast_to(total[j : j + 8, None, :], (8, FACTOR, C)).reshape(128, C)
+            rows = slice(p, p + 128)
+            grad = (skip_v[rows, :].astype(F32) + piece) * slope_v[rows, :].astype(F32)
+            pre_v[rows, :] = grad.astype(BF)
+        rows = pl.ds(r, 256)
+        stores.append(pltpu.make_async_copy(pre_v.at[rows], pre.at[rows], out_sems.at[r // 256]))
+        stores[-1].start()
 
     @pl.when(core[0] == 0)
     def _():
-        keep[...] = pre[:, 0:HALF]
-        send[...] = pre[:, HALF:]
+        keep[...] = pre_v[:, 0:HALF]
+        send[...] = pre_v[:, HALF:]
 
     @pl.when(core[0] != 0)
     def _():
-        keep[...] = pre[:, HALF:]
-        send[...] = pre[:, 0:HALF]
+        keep[...] = pre_v[:, HALF:]
+        send[...] = pre_v[:, 0:HALF]
+
+    for store in stores:
+        store.wait()
 
 
 def pre_grads(core, parts, skip, slope):
+    near = pl.BlockSpec(memory_space=pltpu.HBM)
     return pl.pallas_call(
         slope_kernel,
         out_shape=(
-            sds((ROWS, C), BF),
+            far((ROWS, C), BF),
             sds((ROWS, HALF), BF),
             sds((ROWS, HALF), BF),
-            sds((ATT, C), F32),
+            far((ATT, C), F32),
         ),
-        in_specs=[SM] + [VM] * 3,
-        out_specs=(VM,) * 4,
+        in_specs=[SM, VM, near, near],
+        out_specs=(near, VM, VM, near),
+        scratch_shapes=[
+            pltpu.VMEM((ROWS, C), BF),
+            pltpu.VMEM((ROWS, C), BF),
+            pltpu.VMEM((ROWS, C), BF),
+            pltpu.VMEM((ATT, C), F32),
+            pltpu.SemaphoreType.DMA((2, 3)),
+            pltpu.SemaphoreType.DMA((3,)),
+            pltpu.SemaphoreType.DMA,
+        ],
         name="pre_grads",
         compiler_params=params(12),
         cost_estimate=cost(5 * 768 * 768, 6000000),
-    )(core, parts, skip, slope)
+    )(core, parts, hbm(skip), hbm(slope))
 
 
 def weights_kernel(xt0, al0, xt1, al1, y0, y1, p0, p1, s0, s1, out, yf, yt, made, sems):
@@ -393,7 +464,10 @@
             return jnp.concatenate([al[rows, (t - 1) * 128 : t * 128], xt[rows, 128:]], axis=1)
         return xt[rows, :]
 
-    made[TAPS, :, 0:QH] = (tn(p0[...], s0[...]) + tn(p1[...], s1[...])).astype(BF)
+    def pooled(ref):
+        return jnp.concatenate([ref[h, ATT : 2 * ATT, :] for h in range(HEADS)], axis=0)
+
+    made[TAPS, :, 0:QH] = (tn(pooled(p0), s0[...]) + tn(pooled(p1), s1[...])).astype(BF)
     made[TAPS, :, QH:HALF] = jnp.zeros((C, HALF - QH), BF)
     copy(TAPS).start()
     for i, ref in enumerate((y0, y1)):
@@ -436,7 +510,7 @@
     )(xt0, al0, xt1, al1, y0, y1, p0, p1, s0, s1)
 
 
-def adjoint_kernel(pre, w, skip, pool, out, before, after, first, last, yf, acc):
+def adjoint_kernel(par, pre, w, skip, pool, out, near, far_, first, last, yf, acc):
     tap = pl.program_id(0)
 
     @pl.when(tap == 0)
@@ -462,19 +536,22 @@
     @pl.when(tap == TAPS - 1)
     def _():
         out[...] = acc[8 : 8 + ROWS, :].astype(BF)
-        before[...] = acc[0:8, :]
         first[...] = acc[8:16, :]
         last[...] = acc[ROWS : ROWS + 8, :]
-        after[...] = acc[ROWS + 8 :, :]
-
-
-def conv_adjoint(pre, w, skip, pool):
+        even = par[0] == 0
+        before, after = acc[0:8, :], acc[ROWS + 8 :, :]
+        near[...] = jnp.where(even, after, before)
+        far_[...] = jnp.where(even, before, after)
+
+
+def conv_adjoint(par, pre, w, skip, pool):
     whole = lambda a, b: pl.BlockSpec((a, b), lambda t: (0, 0))
     return pl.pallas_call(
         adjoint_kernel,
         grid=(TAPS,),
         out_shape=(far((ROWS, C), BF),) + (sds((8, C), F32),) * 4,
         in_specs=[
+            SM,
             whole(ROWS, C),
             pl.BlockSpec((1, C, C), lambda t: (t, 0, 0)),
             whole(ROWS, C),
@@ -485,36 +562,39 @@
         name="conv_adjoint",
         compiler_params=params(24),
         cost_estimate=cost(2 * 5 * 768**3, 9500000),
-    )(pre, hbm(w), skip, pool)
-
-
-def edge_kernel(rows, first, last, top, bottom, out):
+    )(par, hbm(pre), hbm(w), hbm(skip), hbm(pool))
+
+
+def edge_kernel(par, rows, first, last, got1, got2, out):
     step = pl.program_id(0)
     held = rows[...].astype(F32)
+    even = par[0] == 0
 
     @pl.when(step == 0)
     def _():
-        out[...] = jnp.concatenate([first[...] + top[...], held[8:16]], axis=0).astype(BF)
+        top = jnp.where(even, got2[...], got1[...])
+        out[...] = jnp.concatenate([first[...] + top, held[8:16]], axis=0).astype(BF)
 
     @pl.when(step != 0)
     def _():
-        out[...] = jnp.concatenate([held[0:8], last[...] + bottom[...]], axis=0).astype(BF)
-
-
-def add_edges(rows, first, last, top, bottom):
+        bottom = jnp.where(even, got1[...], got2[...])
+        out[...] = jnp.concatenate([held[0:8], last[...] + bottom], axis=0).astype(BF)
+
+
+def add_edges(par, rows, first, last, got1, got2):
     block = pl.BlockSpec((16, C), lambda i: (i * (ROWS // 16 - 1), 0))
     whole = pl.BlockSpec((8, C), lambda i: (0, 0))
     return pl.pallas_call(
         edge_kernel,
         grid=(2,),
         out_shape=far((ROWS, C), BF),
-        in_specs=[block, whole, whole, whole, whole],
+        in_specs=[SM, block, whole, whole, whole, whole],
         out_specs=block,
-        input_output_aliases={0: 0},
+        input_output_aliases={1: 0},
         name="add_edges",
         compiler_params=params(8),
         cost_estimate=cost(30000, 150000),
-    )(hbm(rows), first, last, top, bottom)
+    )(par, hbm(rows), first, last, got1, got2)
 
 
 def sum_kernel(parts, after, after2, out):
@@ -525,7 +605,7 @@
         total = parts[0].astype(F32)
         for s in range(1, 32):
             total = total + parts[s].astype(F32)
-        out[step] = total.astype(BF)
+        out[:, pl.ds(pl.multiple_of(step * HALF, HALF), HALF)] = total.astype(BF)
 
     @pl.when(step == TAPS)
     def _():
@@ -533,20 +613,21 @@
             total = parts[4 * h].astype(F32)
             for s in range(4 * h + 1, 4 * h + 4):
                 total = total + parts[s].astype(F32)
-            out[TAPS + h] = total.astype(BF)
+            at = TAPS * HALF + h * QH
+            out[:, at : at + QH] = total[:, 0:QH].astype(BF)
 
 
 def sum_partials(parts, after, after2):
     return pl.pallas_call(
         sum_kernel,
         grid=(TAPS + 1,),
-        out_shape=sds((TAPS + HEADS, 24, HALF), BF),
+        out_shape=sds((24, WIDE), BF),
         in_specs=[pl.BlockSpec((32, 24, HALF), lambda t: (0, 0, t)), ANY, ANY],
-        out_specs=pl.BlockSpec((TAPS + HEADS, 24, HALF), lambda t: (0, 0, 0)),
+        out_specs=pl.BlockSpec((24, WIDE), lambda t: (0, 0)),
         name="sum_partials",
         compiler_params=params(8),
         cost_estimate=cost(32 * 24 * 2304, 3700000),
-    )(parts, after, after2)
+    )(parts, hbm(after), hbm(after2))
 
 
 def add_kernel(a, b, after, out):
@@ -556,26 +637,28 @@
 def add_pair(a, b, after):
     return pl.pallas_call(
         add_kernel,
-        out_shape=sds((TAPS + HEADS, 24, HALF), F32),
+        out_shape=sds((24, WIDE), F32),
         in_specs=[VM] * 2 + [ANY],
         out_specs=VM,
         name="add_pair",
         compiler_params=params(8),
         cost_estimate=cost(300000, 1500000),
-    )(a, b, after)
+    )(a, b, hbm(after))
 
 
 def place_kernel(core, mine, other, conv, proj):
     def put(low, high):
-        conv[:, :, 0:HALF] = low[0:TAPS]
-        conv[:, :, HALF:] = high[0:TAPS]
+        for t in range(TAPS):
+            conv[t, :, 0:HALF] = low[:, t * HALF : (t + 1) * HALF]
+            conv[t, :, HALF:] = high[:, t * HALF : (t + 1) * HALF]
         for h in range(HEADS):
             at = h * HD
-            proj[:, at : at + HD] = low[TAPS + h, :, 0:HD]
+            got = TAPS * HALF + h * QH
+            proj[:, at : at + HD] = low[:, got : got + HD]
             proj[:, 1536 + at : 1536 + at + HD] = jnp.concatenate(
-                [low[TAPS + h, :, HD:QH], high[TAPS + h, :, 0 : HD // 2]], axis=1
+                [low[:, got + HD : got + QH], high[:, got : got + HD // 2]], axis=1
             )
-            proj[:, 3072 + at : 3072 + at + HD] = high[TAPS + h, :, HD // 2 : QH]
+            proj[:, 3072 + at : 3072 + at + HD] = high[:, got + HD // 2 : got + QH]
 
     @pl.when(core[0] == 0)
     def _():
@@ -598,8 +681,8 @@
     )(core, mine, other)
 
 
-UP = [(i, i + 1) for i in range(31)]
-DOWN = [(i + 1, i) for i in range(31)]
+NEAR = [(i, i ^ 1) for i in range(32)]
+NEXT = [pair for i in range(1, 31, 2) for pair in ((i, i + 1), (i + 1, i))]
 
 
 def local(conv_input, skip_grad, conv_weight, proj_weight, query, key, value, grad):
@@ -610,43 +693,43 @@
 
     packed = pack_heads(query[0], key[0], value[0], grad[0])
     own = lax.all_to_all(packed, HAX, 0, 0, tiled=True).reshape(BLK, 4 * HD)
-    qg_own, kv_own = split_own(own)
+    wh = head_weights(pair, odd, proj_weight, packed)
+    qg_own, kv_own = split_own(own, wh)
     qg = lax.ppermute(qg_own, "z", A_PAIR)
     kv = lax.ppermute(kv_own, "z", B_PAIR)
 
-    top = lax.ppermute(x[ROWS - 2 :], SEQ, UP)
-    bottom = lax.ppermute(x[0:2], SEQ, DOWN)
-    edge = jnp.zeros((6, C), BF)
-    xp = jnp.concatenate([edge, top, x, bottom, edge], axis=0)
+    par = (lax.axis_index("z") % 2).astype(jnp.int32).reshape(1)
+    head_rows, tail_rows = x[0:2], x[ROWS - 2 :]
+    got1 = lax.ppermute(jnp.where(par[0] == 0, tail_rows, head_rows), SEQ, NEAR)
+    got2 = lax.ppermute(jnp.where(par[0] == 0, head_rows, tail_rows), SEQ, NEXT)
+    early, xp = conv_apply(par, x, got1, got2, conv_weight, qg_own)
     xp_sib = lax.ppermute(xp, "core", SWAP)
-    slope, pooled = conv_forward(xp, conv_weight, own)
-    wh = head_weights(pair, odd, proj_weight)
-
-    st = att_stats(own, qg, kv, slope)
+
+    st = att_stats(own, qg, kv, early)
     st2 = lax.ppermute(st, "z", A_PAIR)
-    dq_own, dq_send, dkv_own, dkv_send = att_grads(own, qg, kv, st, st2)
+    dq_own, dq_send, dkv_own, dkv_send = att_grads(own, qg, kv, st, st2, wh)
     dq_in = lax.ppermute(dq_send, "z", A_PAIR)
     dkv_in = lax.ppermute(dkv_send, "z", B_PAIR)
-    pooled_blk = lax.all_to_all(pooled, HAX, 0, 0, tiled=True).reshape(BLK, C)
-    pool_part, s0, s_send = att_join(core, dq_own, dkv_own, dq_in, dkv_in, wh, pooled_blk)
-    parts = lax.all_to_all(pool_part.reshape(HEADS, ATT, C), HAX, 0, 0, tiled=True)
-    pooled_sib = lax.ppermute(pooled_blk, "core", SWAP)
+    slope, pooled = gelu_pool(early, x, dq_send)
+    pool_part, s0, s_send = att_join(core, dq_own, dkv_own, dq_in, dkv_in, wh, pooled)
+    parts = lax.all_to_all(pool_part, HAX, 0, 0, tiled=True)
+    parts_sib = lax.ppermute(parts, "core", SWAP)
     s1 = lax.ppermute(s_send, "core", SWAP)
     xt0, al0 = turn_input(xp)
     xt1, al1 = turn_input(xp_sib)
 
     pre, y_send, y0, pool = pre_grads(core, parts, skip, slope)
     y1 = lax.ppermute(y_send, "core", SWAP)
-    terms = weight_grads(xt0, al0, xt1, al1, y0, y1, pooled_blk, pooled_sib, s0, s1)
+    terms = weight_grads(xt0, al0, xt1, al1, y0, y1, parts, parts_sib, s0, s1)
     got = lax.all_to_all(terms.reshape(32, 24, 2304), SEQ, 0, 0, tiled=True)
 
-    rows, before, after, first, last = conv_adjoint(pre, conv_weight, skip, pool)
-    from_left = lax.ppermute(after, SEQ, UP)
-    from_right = lax.ppermute(before, SEQ, DOWN)
-
-    total = sum_partials(got, from_left, from_right)
+    rows, near, next_, first, last = conv_adjoint(par, pre, conv_weight, skip, pool)
+    rim1 = lax.ppermute(near, SEQ, NEAR)
+    rim2 = lax.ppermute(next_, SEQ, NEXT)
+
+    total = sum_partials(got, rim1, rim2)
     total_far = lax.ppermute(total, "yh", SWAP)
-    input_grad = add_edges(rows, first, last, from_left, from_right)
+    input_grad = add_edges(par, rows, first, last, rim1, rim2)
     mine = add_pair(total, total_far, input_grad)
     other = lax.ppermute(mine, "core", SWAP)
     conv_grad, proj_grad = place(core, mine, other)

time: 163 us -> 155 us (0.951)
  local copies, waits for them, and re-layouts: 19 us -> 1.84 us
  waiting for transfers between devices: 39.3 us -> 51.7 us
  starting transfers between devices: 58.9 us -> 46.7 us
  Pallas kernels: 43.1 us -> 52.3 us
    unnamed x56 -> x14, local copies, waits for them, and re-layouts: 18.6 us -> 1.84 us
    pallas_call x7 -> x8, Pallas kernels: 17.8 us -> 26.4 us  [the longest x1 8.52 us: conv_apply(): pl.pallas_call(conv_kernel, out_shape=(far((ROWS, C), F32), sds((ROWS + 1...]
    all_to_all x2 -> x1, waiting for transfers between devices: 3.4 us -> 9.45 us  [local(): parts = lax.all_to_all(pool_part, HAX, 0, 0, tiled=True)]
    ppermute x5, waiting for transfers between devices: 30.8 us -> 36.4 us  [the longest x1 22.1 us: local(): rim2 = lax.ppermute(next_, SEQ, NEXT)]
    ppermute x5, starting transfers between devices: 18 us -> 14.3 us  [the longest x1 5.96 us: local(): got2 = lax.ppermute(jnp.where(par[0] == 0, head_rows, tail_rows), SEQ, NEXT)]
    ppermute x1, starting transfers between devices: 3.64 us -> 0.09 us  [local(): y1 = lax.ppermute(y_send, 'core', SWAP)]
    all_to_all x2 -> x1, starting transfers between devices: 10.8 us -> 7.42 us  [local(): parts = lax.all_to_all(pool_part, HAX, 0, 0, tiled=True)]
    ppermute x1, waiting for transfers between devices: 0.01 us -> 1.65 us  [local(): st2 = lax.ppermute(st, 'z', A_PAIR)]
  transfers between devices with their start and end apart: 19 -> 18, of which waited for: 6 -> 7; matrix products, arithmetic and copies ran while one was open for 0% -> 0% of each run, Pallas kernels for 17% -> 21%
where the time goes in v3:
time: 155 us; the launch traced here: 154 us
  Pallas kernels  52.3 us (34%)
  waiting for transfers between devices  51.7 us (33%)
  starting transfers between devices  46.7 us (30%)
  local copies, waits for them, and re-layouts  1.84 us (1%)
    ppermute x1, waiting for transfers between devices, local(): rim2 = lax.ppermute(next_, SEQ, NEXT)  22.1 us
    ppermute x1, waiting for transfers between devices, local(): rim1 = lax.ppermute(near, SEQ, NEAR)  14.3 us
    all_to_all x1, waiting for transfers between devices, local(): parts = lax.all_to_all(pool_part, HAX, 0, 0, tiled=True)  9.45 us
    pallas_call x1, Pallas kernels, conv_adjoint(): pl.pallas_call(adjoint_kernel, grid=(TAPS,), out_shape=(far((ROWS, C), BF...  9.08 us
    pallas_call x1, Pallas kernels, conv_apply(): pl.pallas_call(conv_kernel, out_shape=(far((ROWS, C), F32), sds((ROWS + 1...  8.52 us
    pallas_call x1, Pallas kernels, weight_grads(): pl.pallas_call(weights_kernel, out_shape=far((C, 2304), BF), in_specs=[VM...  8.38 us
    all_to_all x1, starting transfers between devices, local(): parts = lax.all_to_all(pool_part, HAX, 0, 0, tiled=True)  7.42 us
    all_to_all x1, starting transfers between devices, local(): got = lax.all_to_all(terms.reshape(32, 24, 2304), SEQ, 0, 0, tiled=True)  5.99 us
  transfers between devices with their start and end apart: 18, of which 7 were waited for; matrix products, arithmetic and copies ran while one was open for 0% of the time, Pallas kernels for 21%

profile of v3, /device:TPU:7, one launch (start us, length us, event | category | flops | bytes accessed | tf_op | source)
XLA Modules:
  0.0 154.2 jit_solution(6580680018302742999)
XLA Ops:
  0.6 2.1 %pack_heads.1.after = bf16[8,48,768]{2,1,0:T(8,128)(2,1)} custom-call(bf16[48,1536]{1,0:T(8,128)(2,1)} %bitcast.24, bf16[48,1536]{1,0:T(8,128)(2,1)} %bitcast.25, bf16[48,1536]{1,0:T(8,128)(2,1)} %bitcast.26, bf16[48,1536]{1,0:T(8,128)(2,1)} %bitcast.27), custom_call_target="tpu_custom_call" | custom-call | bytes 1200000 | tf_op jit(solution)/shard_map/pack_heads/pallas_call | solution.py:83
  2.7 5.4 %all-to-all-start = ((bf16[8,48,768]{2,1,0:T(8,128)(2,1)}), bf16[8,48,768]{2,1,0:T(8,128)(2,1)S(1)}, u32[]{:S(2)}, u32[]{:S(2)}) async-start(bf16[8,48,768]{2,1,0:T(8,128)(2,1)} %pack_heads.1.after), calls=%async_computation | async-start | bytes 1179648 | tf_op jit(solution)/shard_map/all_to_all | solution.py:695
  8.1 0.7 fusion.1
  8.8 6.0 %collective-permute-start.3 = (bf16[2,768]{1,0:T(2,128)(2,1)S(1)}, bf16[2,768]{1,0:T(2,128)(2,1)S(1)}, u32[]{:S(2)}, u32[]{:S(2)}) collective-permute-start(bf16[2,768]{1,0:T(2,128)(2,1)S(1)} %get-tuple-element.59), channel_id=1, source_target_pairs={{1,2},{2,1},{3,4},{4,3},{5,6},{6,5},{7,8},{8,7},{9,10},{10,9},{11,... | collective-permute-start | bytes 9224 | tf_op jit(solution)/shard_map/ppermute | solution.py:704
  14.8 0.1 collective-permute-start.2
  14.9 3.0 %head_weights.1.after.wh = bf16[576,768]{1,0:T(8,128)(2,1)} custom-call(s32[1]{0:T(128)} %bitcast.7.pair, s32[1]{0:T(128)} %bitcast.8.odd, bf16[768,4608]{1,0:T(8,128)(2,1)} %wv.1, bf16[768,4608]{1,0:T(8,128)(2,1)} %wv.1, bf16[768,4608]{1,0:T(8,128)(2,1)} %wv.1, bf16[8,48,768]{2,1,0:T(8,128)(2,1)S(1)} %copy-done), custom_call_target="tpu_custom_call" | custom-call | bytes 3000000 | tf_op jit(solution)/shard_map/head_weights/pallas_call | solution.py:208
  18.0 0.1 split_own.1
  18.0 1.1 collective-permute-start.1
  19.2 0.4 collective-permute-start
  19.6 0.0 collective-permute-done.3.got2
  19.6 0.0 collective-permute-done.2.got1
  19.6 8.5 %conv_apply.1 = (f32[768,768]{1,0:T(8,128)}, bf16[784,768]{1,0:T(8,128)(2,1)S(1)}) custom-call(s32[1]{0:T(128)} %bitcast.par, bf16[768,768]{1,0:T(8,128)(2,1)} %bitcast.28, bf16[2,768]{1,0:T(2,128)(2,1)S(1)} %collective-permute-done.2.got1, bf16[2,768]{1,0:T(2,128)(2,1)S(1)} %collective-permute-done.3.got2, bf16[5,768,768]{2,1,0:T(8,128)(2,1)} %w.3, ...), custom_call_target="tpu_custom_call" | custom-call | flops 4529848320 | bytes 9500000 | tf_op jit(solution)/shard_map/conv_apply/pallas_call | solution.py:310
  28.2 1.2 att_stats.1.st
  29.3 1.1 collective-permute-start.4
  30.5 1.6 %collective-permute-done.4.st2 = f32[8,768]{1,0:T(8,128)S(1)} collective-permute-done((f32[8,768]{1,0:T(8,128)S(1)}, f32[8,768]{1,0:T(8,128)S(1)}, u32[]{:S(2)}, u32[]{:S(2)}) %collective-permute-start.4) | collective-permute-done | bytes 24608 | tf_op jit(solution)/shard_map/ppermute | solution.py:709
  32.1 3.3 %att_grads.1 = (f32[384,192]{1,0:T(8,128)}, bf16[192,384]{1,0:T(8,128)(2,1)S(1)}, f32[384,384]{1,0:T(8,128)}, bf16[384,384]{1,0:T(8,128)(2,1)S(1)}) custom-call(bf16[384,768]{1,0:T(8,128)(2,1)S(1)} %bitcast.19, bf16[384,384]{1,0:T(8,128)(2,1)S(1)} %collective-permute-done.qg, bf16[384,384]{1,0:T(8,128)(2,1)S(1)} %collective-permute-done.1.kv, ...), custom_call_target="tpu_custom_call" | custom-call | flops 20000000000 | bytes 3000000 | tf_op jit(solution)/shard_map/att_grads/pallas_call | solution.py:160
  35.4 2.0 %collective-permute-start.6 = (bf16[384,384]{1,0:T(8,128)(2,1)S(1)}, bf16[384,384]{1,0:T(8,128)(2,1)S(1)}, u32[]{:S(2)}, u32[]{:S(2)}) collective-permute-start(bf16[384,384]{1,0:T(8,128)(2,1)S(1)} %get-tuple-element.37), channel_id=1, source_target_pairs={{0,3},{3,0},{1,2},{2,1},{4,7},{7,4},{5,6},{6,5},{8,11},{11,8},{9,1... | collective-permute-start | bytes 884744 | tf_op jit(solution)/shard_map/ppermute | solution.py:712
  37.4 0.0 collective-permute-start.5
  37.4 4.7 %gelu_pool.1 = (bf16[768,768]{1,0:T(8,128)(2,1)}, bf16[48,768]{1,0:T(8,128)(2,1)}) custom-call(f32[768,768]{1,0:T(8,128)} %get-tuple-element.33.after.pre, bf16[768,768]{1,0:T(8,128)(2,1)} %bitcast.29, bf16[192,384]{1,0:T(8,128)(2,1)S(1)} %get-tuple-element.36.after), custom_call_target="tpu_custom_call" | custom-call | flops 3000000000 | bytes 5000000 | tf_op jit(solution)/shard_map/gelu_pool/pallas_call | solution.py:342
  42.1 0.1 collective-permute-done.6.dkv_in
  42.2 3.1 %att_join.1 = (bf16[8,96,768]{2,1,0:T(8,128)(2,1)}, bf16[384,288]{1,0:T(8,128)(2,1)S(1)}, bf16[384,288]{1,0:T(8,128)(2,1)S(1)}) custom-call(s32[1]{0:T(128)} %bitcast.1.core, f32[384,192]{1,0:T(8,128)} %get-tuple-element.34.dq_own, f32[384,384]{1,0:T(8,128)} %get-tuple-element.35.dkv_own, bf16[192,384]{1,0:T(8,128)(2,1)S(1)} %collective-permute-done.5.dq_in, ...), custom_call_target="tpu_custom_call" | custom-call | flops 10000000000 | bytes 3500000 | tf_op jit(solution)/shard_map/att_join/pallas_call | solution.py:256
  45.3 7.4 %all-to-all-start.1 = ((bf16[8,96,768]{2,1,0:T(8,128)(2,1)}), bf16[8,96,768]{2,1,0:T(8,128)(2,1)S(1)}, u32[]{:S(2)}, u32[]{:S(2)}) async-start(bf16[8,96,768]{2,1,0:T(8,128)(2,1)} %get-tuple-element.39), calls=%async_computation.1 | async-start | bytes 2359296 | tf_op jit(solution)/shard_map/all_to_all | solution.py:715
  52.7 3.5 %collective-permute-start.9 = (bf16[784,768]{1,0:T(8,128)(2,1)S(1)}, bf16[784,768]{1,0:T(8,128)(2,1)}, u32[]{:S(2)}, u32[]{:S(2)}) collective-permute-start(bf16[784,768]{1,0:T(8,128)(2,1)S(1)} %get-tuple-element.48.xp), channel_id=1, source_target_pairs={{0,32},{32,0},{1,33},{33,1},{2,34},{34,2},{3,35},{35,3},{4,36},{36... | collective-permute-start | bytes 3612680 | tf_op jit(solution)/shard_map/ppermute | solution.py:706
  56.2 9.5 %all-to-all-done.1.parts.p0 = bf16[8,96,768]{2,1,0:T(8,128)(2,1)S(1)} async-done(((bf16[8,96,768]{2,1,0:T(8,128)(2,1)}), bf16[8,96,768]{2,1,0:T(8,128)(2,1)S(1)}, u32[]{:S(2)}, u32[]{:S(2)}) %all-to-all-start.1) | async-done | bytes 1179680 | tf_op jit(solution)/shard_map/all_to_all | solution.py:715
  65.6 3.1 %collective-permute-start.11 = (bf16[8,96,768]{2,1,0:T(8,128)(2,1)S(1)}, bf16[8,96,768]{2,1,0:T(8,128)(2,1)S(1)}, u32[]{:S(2)}, u32[]{:S(2)}) collective-permute-start(bf16[8,96,768]{2,1,0:T(8,128)(2,1)S(1)} %all-to-all-done.1.parts.p0), channel_id=1, source_target_pairs={{0,32},{32,0},{1,33},{33,1},{2,34},{34,2},{3,35},{35,3},{4,36},{36... | collective-permute-start | bytes 3538952 | tf_op jit(solution)/shard_map/ppermute | solution.py:716
  68.7 2.6 %pre_grads.1 = (bf16[768,768]{1,0:T(8,128)(2,1)}, bf16[768,384]{1,0:T(8,128)(2,1)S(1)}, bf16[768,384]{1,0:T(8,128)(2,1)S(1)}, f32[48,768]{1,0:T(8,128)}) custom-call(s32[1]{0:T(128)} %bitcast.1.core, bf16[8,96,768]{2,1,0:T(8,128)(2,1)S(1)} %all-to-all-done.1.parts.p0, bf16[768,768]{1,0:T(8,128)(2,1)} %bitcast.22, bf16[768,768]{1,0:T(8,128)(2,1)} %get-tuple-element.40.slope), custom_call_target="tpu_custom_call" | custom-call | flops 2949120 | bytes 6000000 | tf_op jit(solution)/shard_map/pre_grads/pallas_call | solution.py:430
  71.4 0.1 collective-permute-start.10
  71.5 0.5 collective-permute-start.12
  72.0 0.6 turn_input.2
  72.6 1.9 %turn_input.3 = (bf16[768,768]{1,0:T(8,128)(2,1)S(1)}, bf16[768,512]{1,0:T(8,128)(2,1)S(1)}) custom-call(bf16[784,768]{1,0:T(8,128)(2,1)} %collective-permute-done.9.xp), custom_call_target="tpu_custom_call" | custom-call | flops 5898240 | bytes 3200000 | tf_op jit(solution)/shard_map/turn_input/pallas_call | solution.py:374
  74.4 8.4 %weight_grads.1 = bf16[768,2304]{1,0:T(8,128)(2,1)} custom-call(bf16[768,768]{1,0:T(8,128)(2,1)S(1)} %get-tuple-element.49.xt0, bf16[768,512]{1,0:T(8,128)(2,1)S(1)} %get-tuple-element.50.al0, bf16[768,768]{1,0:T(8,128)(2,1)S(1)} %get-tuple-element.51.xt1, bf16[768,512]{1,0:T(8,128)(2,1)S(1)} %get-tuple-element.52.al1, ...), custom_call_target="tpu_custom_call" | custom-call | flops 4529848320 | bytes 10000000 | tf_op jit(solution)/shard_map/weight_grads/pallas_call | solution.py:496
  82.8 6.0 %all-to-all-start.2 = ((bf16[32,24,2304]{2,1,0:T(8,128)(2,1)}), bf16[32,24,2304]{2,1,0:T(8,128)(2,1)S(1)}, u32[]{:S(2)}, u32[]{:S(2)}) async-start(bf16[32,24,2304]{2,1,0:T(8,128)(2,1)} %bitcast.21), calls=%async_computation.2 | async-start | bytes 7077888 | tf_op jit(solution)/shard_map/all_to_all | solution.py:724
  88.8 9.1 %conv_adjoint.1 = (bf16[768,768]{1,0:T(8,128)(2,1)}, f32[8,768]{1,0:T(8,128)S(1)}, f32[8,768]{1,0:T(8,128)S(1)}, f32[8,768]{1,0:T(8,128)S(1)}, f32[8,768]{1,0:T(8,128)S(1)}) custom-call(s32[1]{0:T(128)} %bitcast.par, bf16[768,768]{1,0:T(8,128)(2,1)} %get-tuple-element.41.pre, bf16[5,768,768]{2,1,0:T(8,128)(2,1)} %w.3, bf16[768,768]{1,0:T(8,128)(2,1)} %bitcast.23, ...), custom_call_target="tpu_custom_call" | custom-call | flops 4529848320 | bytes 9500000 | tf_op jit(solution)/shard_map/conv_adjoint/pallas_call | solution.py:549
  97.9 0.6 copy-done.3
  98.5 0.6 copy-done.5
  99.1 1.2 collective-permute-start.7
  100.3 4.0 %collective-permute-start.8 = (f32[8,768]{1,0:T(8,128)S(1)}, f32[8,768]{1,0:T(8,128)}, u32[]{:S(2)}, u32[]{:S(2)}) collective-permute-start(f32[8,768]{1,0:T(8,128)S(1)} %get-tuple-element.47), channel_id=1, source_target_pairs={{1,2},{2,1},{3,4},{4,3},{5,6},{6,5},{7,8},{8,7},{9,10},{10,9},{11,... | collective-permute-start | bytes 73736 | tf_op jit(solution)/shard_map/ppermute | solution.py:728
  104.3 14.3 %collective-permute-done.7.got1.after = f32[8,768]{1,0:T(8,128)S(1)} collective-permute-done((f32[8,768]{1,0:T(8,128)S(1)}, f32[8,768]{1,0:T(8,128)S(1)}, u32[]{:S(2)}, u32[]{:S(2)}) %collective-permute-start.7) | collective-permute-done | bytes 24608 | tf_op jit(solution)/shard_map/ppermute | solution.py:727
  118.6 0.6 copy-done.1
  119.2 22.1 %collective-permute-done.8.got2.after2 = f32[8,768]{1,0:T(8,128)} collective-permute-done((f32[8,768]{1,0:T(8,128)S(1)}, f32[8,768]{1,0:T(8,128)}, u32[]{:S(2)}, u32[]{:S(2)}) %collective-permute-start.8) | collective-permute-done | bytes 24608 | tf_op jit(solution)/shard_map/ppermute | solution.py:728
  141.3 1.1 sum_partials.1.a
  142.4 2.7 %collective-permute-start.13 = (bf16[24,4224]{1,0:T(8,128)(2,1)S(1)}, bf16[24,4224]{1,0:T(8,128)(2,1)S(1)}, u32[]{:S(2)}, u32[]{:S(2)}) collective-permute-start(bf16[24,4224]{1,0:T(8,128)(2,1)S(1)} %sum_partials.1.a), channel_id=1, source_target_pairs={{0,64},{64,0},{1,65},{65,1},{2,66},{66,2},{3,67},{67,3},{4,68},{68... | collective-permute-start | bytes 608264 | tf_op jit(solution)/shard_map/ppermute | solution.py:731
  145.1 1.4 add_edges.1.after
  146.5 2.8 %collective-permute-done.13.b = bf16[24,4224]{1,0:T(8,128)(2,1)S(1)} collective-permute-done((bf16[24,4224]{1,0:T(8,128)(2,1)S(1)}, bf16[24,4224]{1,0:T(8,128)(2,1)S(1)}, u32[]{:S(2)}, u32[]{:S(2)}) %collective-permute-start.13) | collective-permute-done | bytes 202784 | tf_op jit(solution)/shard_map/ppermute | solution.py:731
  149.3 0.1 add_pair.1.mine
  149.4 2.2 %collective-permute-start.14 = (f32[24,4224]{1,0:T(8,128)S(1)}, f32[24,4224]{1,0:T(8,128)S(1)}, u32[]{:S(2)}, u32[]{:S(2)}) collective-permute-start(f32[24,4224]{1,0:T(8,128)S(1)} %add_pair.1.mine), channel_id=1, source_target_pairs={{0,32},{32,0},{1,33},{33,1},{2,34},{34,2},{3,35},{35,3},{4,36},{36... | collective-permute-start | bytes 1216520 | tf_op jit(solution)/shard_map/ppermute | solution.py:734
  151.6 1.4 collective-permute-done.14.other
  152.9 1.3 place.1
  (20 shorter events, 0.0 us)
Async XLA Ops:
  2.7 12.2 %copy-start = (bf16[8,48,768]{2,1,0:T(8,128)(2,1)S(1)}, bf16[8,48,768]{2,1,0:T(8,128)(2,1)}, u32[]{:S(2)}) copy-start(bf16[8,48,768]{2,1,0:T(8,128)(2,1)} %pack_heads.1.after) | copy-start | bytes 1769476
  2.7 15.2 %all-to-all-start = ((bf16[8,48,768]{2,1,0:T(8,128)(2,1)}), bf16[8,48,768]{2,1,0:T(8,128)(2,1)S(1)}, u32[]{:S(2)}, u32[]{:S(2)}) async-start(bf16[8,48,768]{2,1,0:T(8,128)(2,1)} %pack_heads.1.after), calls=%async_computation | async-start | bytes 1179648 | tf_op jit(solution)/shard_map/all_to_all | solution.py:695
  8.8 10.8 %collective-permute-start.3 = (bf16[2,768]{1,0:T(2,128)(2,1)S(1)}, bf16[2,768]{1,0:T(2,128)(2,1)S(1)}, u32[]{:S(2)}, u32[]{:S(2)}) collective-permute-start(bf16[2,768]{1,0:T(2,128)(2,1)S(1)} %get-tuple-element.59), channel_id=1, source_target_pairs={{1,2},{2,1},{3,4},{4,3},{5,6},{6,5},{7,8},{8,7},{9,10},{10,9},{11,... | collective-permute-start | bytes 9224 | tf_op jit(solution)/shard_map/ppermute | solution.py:704
  14.8 4.8 %collective-permute-start.2 = (bf16[2,768]{1,0:T(2,128)(2,1)S(1)}, bf16[2,768]{1,0:T(2,128)(2,1)S(1)}, u32[]{:S(2)}, u32[]{:S(2)}) collective-permute-start(bf16[2,768]{1,0:T(2,128)(2,1)S(1)} %get-tuple-element.60), channel_id=1, source_target_pairs={{0,1},{1,0},{2,3},{3,2},{4,5},{5,4},{6,7},{7,6},{8,9},{9,8},{10,11... | collective-permute-start | bytes 9224 | tf_op jit(solution)/shard_map/ppermute | solution.py:703
  18.0 10.1 %collective-permute-start.1 = (bf16[384,384]{1,0:T(8,128)(2,1)S(1)}, bf16[384,384]{1,0:T(8,128)(2,1)S(1)}, u32[]{:S(2)}, u32[]{:S(2)}) collective-permute-start(bf16[384,384]{1,0:T(8,128)(2,1)S(1)} %get-tuple-element.32), channel_id=1, source_target_pairs={{0,3},{3,0},{1,2},{2,1},{4,7},{7,4},{5,6},{6,5},{8,11},{11,8},{9,1... | collective-permute-start | bytes 884744 | tf_op jit(solution)/shard_map/ppermute | solution.py:699
  19.2 9.0 %collective-permute-start = (bf16[384,384]{1,0:T(8,128)(2,1)S(1)}, bf16[384,384]{1,0:T(8,128)(2,1)S(1)}, u32[]{:S(2)}, u32[]{:S(2)}) collective-permute-start(bf16[384,384]{1,0:T(8,128)(2,1)S(1)} %get-tuple-element.31.after), channel_id=1, source_target_pairs={{0,1},{1,0},{2,3},{3,2},{4,5},{5,4},{6,7},{7,6},{8,9},{9,8},{10,11... | collective-permute-start | bytes 884744 | tf_op jit(solution)/shard_map/ppermute | solution.py:698
  29.3 2.8 %collective-permute-start.4 = (f32[8,768]{1,0:T(8,128)S(1)}, f32[8,768]{1,0:T(8,128)S(1)}, u32[]{:S(2)}, u32[]{:S(2)}) collective-permute-start(f32[8,768]{1,0:T(8,128)S(1)} %att_stats.1.st), channel_id=1, source_target_pairs={{0,1},{1,0},{2,3},{3,2},{4,5},{5,4},{6,7},{7,6},{8,9},{9,8},{10,11... | collective-permute-start | bytes 73736 | tf_op jit(solution)/shard_map/ppermute | solution.py:709
  35.4 6.8 %collective-permute-start.6 = (bf16[384,384]{1,0:T(8,128)(2,1)S(1)}, bf16[384,384]{1,0:T(8,128)(2,1)S(1)}, u32[]{:S(2)}, u32[]{:S(2)}) collective-permute-start(bf16[384,384]{1,0:T(8,128)(2,1)S(1)} %get-tuple-element.37), channel_id=1, source_target_pairs={{0,3},{3,0},{1,2},{2,1},{4,7},{7,4},{5,6},{6,5},{8,11},{11,8},{9,1... | collective-permute-start | bytes 884744 | tf_op jit(solution)/shard_map/ppermute | solution.py:712
  37.4 4.7 %collective-permute-start.5 = (bf16[192,384]{1,0:T(8,128)(2,1)S(1)}, bf16[192,384]{1,0:T(8,128)(2,1)S(1)}, u32[]{:S(2)}, u32[]{:S(2)}) collective-permute-start(bf16[192,384]{1,0:T(8,128)(2,1)S(1)} %get-tuple-element.36.after), channel_id=1, source_target_pairs={{0,1},{1,0},{2,3},{3,2},{4,5},{5,4},{6,7},{7,6},{8,9},{9,8},{10,11... | collective-permute-start | bytes 442376 | tf_op jit(solution)/shard_map/ppermute | solution.py:711
  45.3 20.4 %all-to-all-start.1 = ((bf16[8,96,768]{2,1,0:T(8,128)(2,1)}), bf16[8,96,768]{2,1,0:T(8,128)(2,1)S(1)}, u32[]{:S(2)}, u32[]{:S(2)}) async-start(bf16[8,96,768]{2,1,0:T(8,128)(2,1)} %get-tuple-element.39), calls=%async_computation.1 | async-start | bytes 2359296 | tf_op jit(solution)/shard_map/all_to_all | solution.py:715
  52.7 19.8 %collective-permute-start.9 = (bf16[784,768]{1,0:T(8,128)(2,1)S(1)}, bf16[784,768]{1,0:T(8,128)(2,1)}, u32[]{:S(2)}, u32[]{:S(2)}) collective-permute-start(bf16[784,768]{1,0:T(8,128)(2,1)S(1)} %get-tuple-element.48.xp), channel_id=1, source_target_pairs={{0,32},{32,0},{1,33},{33,1},{2,34},{34,2},{3,35},{35,3},{4,36},{36... | collective-permute-start | bytes 3612680 | tf_op jit(solution)/shard_map/ppermute | solution.py:706
  65.6 8.8 %collective-permute-start.11 = (bf16[8,96,768]{2,1,0:T(8,128)(2,1)S(1)}, bf16[8,96,768]{2,1,0:T(8,128)(2,1)S(1)}, u32[]{:S(2)}, u32[]{:S(2)}) collective-permute-start(bf16[8,96,768]{2,1,0:T(8,128)(2,1)S(1)} %all-to-all-done.1.parts.p0), channel_id=1, source_target_pairs={{0,32},{32,0},{1,33},{33,1},{2,34},{34,2},{3,35},{35,3},{4,36},{36... | collective-permute-start | bytes 3538952 | tf_op jit(solution)/shard_map/ppermute | solution.py:716
  71.4 3.1 %collective-permute-start.10 = (bf16[768,384]{1,0:T(8,128)(2,1)S(1)}, bf16[768,384]{1,0:T(8,128)(2,1)S(1)}, u32[]{:S(2)}, u32[]{:S(2)}) collective-permute-start(bf16[768,384]{1,0:T(8,128)(2,1)S(1)} %get-tuple-element.54), channel_id=1, source_target_pairs={{0,32},{32,0},{1,33},{33,1},{2,34},{34,2},{3,35},{35,3},{4,36},{36... | collective-permute-start | bytes 1769480 | tf_op jit(solution)/shard_map/ppermute | solution.py:722
  71.5 3.0 %collective-permute-start.12 = (bf16[384,288]{1,0:T(8,128)(2,1)S(1)}, bf16[384,288]{1,0:T(8,128)(2,1)S(1)}, u32[]{:S(2)}, u32[]{:S(2)}) collective-permute-start(bf16[384,288]{1,0:T(8,128)(2,1)S(1)} %get-tuple-element.56), channel_id=1, source_target_pairs={{0,32},{32,0},{1,33},{33,1},{2,34},{34,2},{3,35},{35,3},{4,36},{36... | collective-permute-start | bytes 663560 | tf_op jit(solution)/shard_map/ppermute | solution.py:717
  82.8 58.5 %all-to-all-start.2 = ((bf16[32,24,2304]{2,1,0:T(8,128)(2,1)}), bf16[32,24,2304]{2,1,0:T(8,128)(2,1)S(1)}, u32[]{:S(2)}, u32[]{:S(2)}) async-start(bf16[32,24,2304]{2,1,0:T(8,128)(2,1)} %bitcast.21), calls=%async_computation.2 | async-start | bytes 7077888 | tf_op jit(solution)/shard_map/all_to_all | solution.py:724
  97.9 0.6 copy-start.3
  98.5 0.6 copy-start.5
  99.1 19.5 %collective-permute-start.7 = (f32[8,768]{1,0:T(8,128)S(1)}, f32[8,768]{1,0:T(8,128)S(1)}, u32[]{:S(2)}, u32[]{:S(2)}) collective-permute-start(f32[8,768]{1,0:T(8,128)S(1)} %get-tuple-element.46), channel_id=1, source_target_pairs={{0,1},{1,0},{2,3},{3,2},{4,5},{5,4},{6,7},{7,6},{8,9},{9,8},{10,11... | collective-permute-start | bytes 73736 | tf_op jit(solution)/shard_map/ppermute | solution.py:727
  100.3 41.0 %collective-permute-start.8 = (f32[8,768]{1,0:T(8,128)S(1)}, f32[8,768]{1,0:T(8,128)}, u32[]{:S(2)}, u32[]{:S(2)}) collective-permute-start(f32[8,768]{1,0:T(8,128)S(1)} %get-tuple-element.47), channel_id=1, source_target_pairs={{1,2},{2,1},{3,4},{4,3},{5,6},{6,5},{7,8},{8,7},{9,10},{10,9},{11,... | collective-permute-start | bytes 73736 | tf_op jit(solution)/shard_map/ppermute | solution.py:728
  118.6 0.6 copy-start.1
  141.3 3.8 %copy-start.2 = (f32[8,768]{1,0:T(8,128)S(1)}, f32[8,768]{1,0:T(8,128)}, u32[]{:S(2)}) copy-start(f32[8,768]{1,0:T(8,128)} %copy-done.1) | copy-start | bytes 73732
  141.3 3.8 %copy-start.4 = (f32[8,768]{1,0:T(8,128)S(1)}, f32[8,768]{1,0:T(8,128)}, u32[]{:S(2)}) copy-start(f32[8,768]{1,0:T(8,128)} %copy-done.3) | copy-start | bytes 73732
  141.3 3.8 %copy-start.6 = (f32[8,768]{1,0:T(8,128)S(1)}, f32[8,768]{1,0:T(8,128)}, u32[]{:S(2)}) copy-start(f32[8,768]{1,0:T(8,128)} %copy-done.5) | copy-start | bytes 73732
  142.4 6.9 %collective-permute-start.13 = (bf16[24,4224]{1,0:T(8,128)(2,1)S(1)}, bf16[24,4224]{1,0:T(8,128)(2,1)S(1)}, u32[]{:S(2)}, u32[]{:S(2)}) collective-permute-start(bf16[24,4224]{1,0:T(8,128)(2,1)S(1)} %sum_partials.1.a), channel_id=1, source_target_pairs={{0,64},{64,0},{1,65},{65,1},{2,66},{66,2},{3,67},{67,3},{4,68},{68... | collective-permute-start | bytes 608264 | tf_op jit(solution)/shard_map/ppermute | solution.py:731
  149.4 3.5 %collective-permute-start.14 = (f32[24,4224]{1,0:T(8,128)S(1)}, f32[24,4224]{1,0:T(8,128)S(1)}, u32[]{:S(2)}, u32[]{:S(2)}) collective-permute-start(f32[24,4224]{1,0:T(8,128)S(1)} %add_pair.1.mine), channel_id=1, source_target_pairs={{0,32},{32,0},{1,33},{33,1},{2,34},{34,2},{3,35},{35,3},{4,36},{36... | collective-permute-start | bytes 1216520 | tf_op jit(solution)/shard_map/ppermute | solution.py:734

commit v4 on v3

--- a/solution.py
+++ b/solution.py
@@ -72,19 +72,36 @@
     return jnp.dot(a, b, preferred_element_type=F32)
 
 
-def pack_kernel(q, k, v, g, out):
-    for h in range(HEADS):
-        cols = slice(h * HD, (h + 1) * HD)
-        for slot, ref in enumerate((q, g, k, v)):
-            out[h, :, slot * HD : (slot + 1) * HD] = ref[:, cols]
+def pack_kernel(q, k, v, g, out, held, made, in_sems, out_sems):
+    loads = [pltpu.make_async_copy(ref, held.at[i], in_sems.at[i]) for i, ref in enumerate((q, g, k, v))]
+    for load in loads:
+        load.start()
+    stores = []
+    for half in range(2):
+        for i in (2 * half, 2 * half + 1):
+            loads[i].wait()
+            for h in range(HEADS):
+                made[h, :, i * HD : (i + 1) * HD] = held[i, :, h * HD : (h + 1) * HD]
+        cols = pl.ds(half * 2 * HD, 2 * HD)
+        stores.append(pltpu.make_async_copy(made.at[:, :, cols], out.at[:, :, cols], out_sems.at[half]))
+        stores[-1].start()
+    for store in stores:
+        store.wait()
 
 
 def pack_heads(q, k, v, g):
+    near = pl.BlockSpec(memory_space=pltpu.HBM)
     return pl.pallas_call(
         pack_kernel,
         out_shape=far((HEADS, ATT, 4 * HD), BF),
-        in_specs=[VM] * 4,
-        out_specs=VM,
+        in_specs=[near] * 4,
+        out_specs=near,
+        scratch_shapes=[
+            pltpu.VMEM((4, ATT, HEADS * HD), BF),
+            pltpu.VMEM((HEADS, ATT, 4 * HD), BF),
+            pltpu.SemaphoreType.DMA((4,)),
+            pltpu.SemaphoreType.DMA((2,)),
+        ],
         name="pack_heads",
         compiler_params=params(8),
         cost_estimate=cost(0, 1200000),
@@ -191,16 +208,15 @@
 
 
 def head_kernel(pair, odd, wq, wk, wv, after, out):
-    for p, ref in enumerate((wq, wk, wv)):
-        turned = ref[...].T
-
-        @pl.when(odd[0] == 0)
-        def _():
-            out[p * HD : (p + 1) * HD, :] = turned[0:HD]
-
-        @pl.when(odd[0] != 0)
-        def _():
-            out[p * HD : (p + 1) * HD, :] = turned[HD : 2 * HD]
+    @pl.when(odd[0] == 0)
+    def _():
+        for p, ref in enumerate((wq, wk, wv)):
+            out[p * HD : (p + 1) * HD, :] = ref[:, 0:HD].T
+
+    @pl.when(odd[0] != 0)
+    def _():
+        for p, ref in enumerate((wq, wk, wv)):
+            out[p * HD : (p + 1) * HD, :] = ref[:, HD : 2 * HD].T
 
 
 def head_weights(pair, odd, weight, after):
@@ -703,7 +719,6 @@
     got1 = lax.ppermute(jnp.where(par[0] == 0, tail_rows, head_rows), SEQ, NEAR)
     got2 = lax.ppermute(jnp.where(par[0] == 0, head_rows, tail_rows), SEQ, NEXT)
     early, xp = conv_apply(par, x, got1, got2, conv_weight, qg_own)
-    xp_sib = lax.ppermute(xp, "core", SWAP)
 
     st = att_stats(own, qg, kv, early)
     st2 = lax.ppermute(st, "z", A_PAIR)
@@ -713,7 +728,9 @@
     slope, pooled = gelu_pool(early, x, dq_send)
     pool_part, s0, s_send = att_join(core, dq_own, dkv_own, dq_in, dkv_in, wh, pooled)
     parts = lax.all_to_all(pool_part, HAX, 0, 0, tiled=True)
+    parts, xp = lax.optimization_barrier((parts, xp))
     parts_sib = lax.ppermute(parts, "core", SWAP)
+    xp_sib = lax.ppermute(xp, "core", SWAP)
     s1 = lax.ppermute(s_send, "core", SWAP)
     xt0, al0 = turn_input(xp)
     xt1, al1 = turn_input(xp_sib)

time: 155 us -> 152 us (0.981)
  blocking collectives: 0 us -> 19.5 us
  waiting for transfers between devices: 51.7 us -> 40.8 us
  starting transfers between devices: 46.7 us -> 36.7 us
    all_to_all x0 -> x1, blocking collectives: none -> 19.5 us  [local(): parts = lax.all_to_all(pool_part, HAX, 0, 0, tiled=True)]
    all_to_all x1 -> x0, waiting for transfers between devices: 9.45 us -> none  [local(): parts = lax.all_to_all(pool_part, HAX, 0, 0, tiled=True)]
    all_to_all x1 -> x0, starting transfers between devices: 7.42 us -> none  [local(): parts = lax.all_to_all(pool_part, HAX, 0, 0, tiled=True)]
    ppermute x1, starting transfers between devices: 3.1 us -> 0.01 us  [local(): parts_sib = lax.ppermute(parts, 'core', SWAP)]
    ppermute x1, waiting for transfers between devices: 22.1 us -> 19.2 us  [local(): rim2 = lax.ppermute(next_, SEQ, NEXT)]
    all_to_all x1, waiting for transfers between devices: 0.01 us -> 2.2 us  [local(): got = lax.all_to_all(terms.reshape(32, 24, 2304), SEQ, 0, 0, tiled=True)]
    ppermute x1, waiting for transfers between devices: 14.3 us -> 12.7 us  [local(): rim1 = lax.ppermute(near, SEQ, NEAR)]
  transfers between devices with their start and end apart: 18 -> 17, of which waited for: 7 -> 8; matrix products, arithmetic and copies ran while one was open for 0% -> 0% of each run, Pallas kernels for 21% -> 20%
where the time goes in v4:
time: 152 us; the launch traced here: 151 us
  Pallas kernels  51.1 us (34%)
  waiting for transfers between devices  40.8 us (27%)
  starting transfers between devices  36.7 us (24%)
  blocking collectives  19.5 us (13%)
  local copies, waits for them, and re-layouts  1.84 us (1%)
    all_to_all x1, blocking collectives, local(): parts = lax.all_to_all(pool_part, HAX, 0, 0, tiled=True)  19.5 us
    ppermute x1, waiting for transfers between devices, local(): rim2 = lax.ppermute(next_, SEQ, NEXT)  19.2 us
    ppermute x1, waiting for transfers between devices, local(): rim1 = lax.ppermute(near, SEQ, NEAR)  12.7 us
    pallas_call x1, Pallas kernels, conv_adjoint(): pl.pallas_call(adjoint_kernel, grid=(TAPS,), out_shape=(far((ROWS, C), BF...  9.09 us
    pallas_call x1, Pallas kernels, conv_apply(): pl.pallas_call(conv_kernel, out_shape=(far((ROWS, C), F32), sds((ROWS + 1...  8.53 us
    pallas_call x1, Pallas kernels, weight_grads(): pl.pallas_call(weights_kernel, out_shape=far((C, 2304), BF), in_specs=[VM...  8.41 us
    ppermute x1, starting transfers between devices, local(): got2 = lax.ppermute(jnp.where(par[0] == 0, head_rows, tail_rows), SEQ, NEXT)  5.96 us
    all_to_all x1, starting transfers between devices, local(): got = lax.all_to_all(terms.reshape(32, 24, 2304), SEQ, 0, 0, tiled=True)  5.5 us
  transfers between devices with their start and end apart: 17, of which 8 were waited for; matrix products, arithmetic and copies ran while one was open for 0% of the time, Pallas kernels for 20%

profile of v4, /device:TPU:7, one launch (start us, length us, event | category | flops | bytes accessed | tf_op | source)
XLA Modules:
  0.0 151.5 jit_solution(5668743155366634693)
XLA Ops:
  0.6 2.1 %pack_heads.1.after = bf16[8,48,768]{2,1,0:T(8,128)(2,1)} custom-call(bf16[48,1536]{1,0:T(8,128)(2,1)} %bitcast.24, bf16[48,1536]{1,0:T(8,128)(2,1)} %bitcast.25, bf16[48,1536]{1,0:T(8,128)(2,1)} %bitcast.26, bf16[48,1536]{1,0:T(8,128)(2,1)} %bitcast.27), custom_call_target="tpu_custom_call" | custom-call | bytes 1200000 | tf_op jit(solution)/shard_map/pack_heads/pallas_call | solution.py:94
  2.7 0.0 copy-start
  2.7 5.4 %all-to-all-start = ((bf16[8,48,768]{2,1,0:T(8,128)(2,1)}), bf16[8,48,768]{2,1,0:T(8,128)(2,1)S(1)}, u32[]{:S(2)}, u32[]{:S(2)}) async-start(bf16[8,48,768]{2,1,0:T(8,128)(2,1)} %pack_heads.1.after), calls=%async_computation | async-start | bytes 1179648 | tf_op jit(solution)/shard_map/all_to_all | solution.py:711
  8.1 0.7 fusion.1
  8.8 6.0 %collective-permute-start.3 = (bf16[2,768]{1,0:T(2,128)(2,1)S(1)}, bf16[2,768]{1,0:T(2,128)(2,1)S(1)}, u32[]{:S(2)}, u32[]{:S(2)}) collective-permute-start(bf16[2,768]{1,0:T(2,128)(2,1)S(1)} %get-tuple-element.63), channel_id=1, source_target_pairs={{1,2},{2,1},{3,4},{4,3},{5,6},{6,5},{7,8},{8,7},{9,10},{10,9},{11,... | collective-permute-start | bytes 9224 | tf_op jit(solution)/shard_map/ppermute | solution.py:720
  14.8 0.1 collective-permute-start.2
  14.9 3.1 %head_weights.1.after.wh = bf16[576,768]{1,0:T(8,128)(2,1)} custom-call(s32[1]{0:T(128)} %bitcast.7.pair, s32[1]{0:T(128)} %bitcast.8.odd, bf16[768,4608]{1,0:T(8,128)(2,1)} %wv.1, bf16[768,4608]{1,0:T(8,128)(2,1)} %wv.1, bf16[768,4608]{1,0:T(8,128)(2,1)} %wv.1, bf16[8,48,768]{2,1,0:T(8,128)(2,1)S(1)} %copy-done), custom_call_target="tpu_custom_call" | custom-call | bytes 3000000 | tf_op jit(solution)/shard_map/head_weights/pallas_call | solution.py:224
  18.0 0.1 split_own.1
  18.0 1.1 collective-permute-start.1
  19.2 0.5 collective-permute-start
  19.6 8.5 %conv_apply.1 = (f32[768,768]{1,0:T(8,128)}, bf16[784,768]{1,0:T(8,128)(2,1)S(1)}) custom-call(s32[1]{0:T(128)} %bitcast.par, bf16[768,768]{1,0:T(8,128)(2,1)} %bitcast.28, bf16[2,768]{1,0:T(2,128)(2,1)S(1)} %collective-permute-done.2.got1, bf16[2,768]{1,0:T(2,128)(2,1)S(1)} %collective-permute-done.3.got2, bf16[5,768,768]{2,1,0:T(8,128)(2,1)} %w.3, ...), custom_call_target="tpu_custom_call" | custom-call | flops 4529848320 | bytes 9500000 | tf_op jit(solution)/shard_map/conv_apply/pallas_call | solution.py:326
  28.2 1.2 att_stats.1.st
  29.4 1.1 collective-permute-start.4
  30.4 1.7 %collective-permute-done.4.st2 = f32[8,768]{1,0:T(8,128)S(1)} collective-permute-done((f32[8,768]{1,0:T(8,128)S(1)}, f32[8,768]{1,0:T(8,128)S(1)}, u32[]{:S(2)}, u32[]{:S(2)}) %collective-permute-start.4) | collective-permute-done | bytes 24608 | tf_op jit(solution)/shard_map/ppermute | solution.py:724
  32.1 3.3 %att_grads.1 = (f32[384,192]{1,0:T(8,128)}, bf16[192,384]{1,0:T(8,128)(2,1)S(1)}, f32[384,384]{1,0:T(8,128)}, bf16[384,384]{1,0:T(8,128)(2,1)S(1)}) custom-call(bf16[384,768]{1,0:T(8,128)(2,1)S(1)} %bitcast.19, bf16[384,384]{1,0:T(8,128)(2,1)S(1)} %collective-permute-done.qg, bf16[384,384]{1,0:T(8,128)(2,1)S(1)} %collective-permute-done.1.kv, ...), custom_call_target="tpu_custom_call" | custom-call | flops 20000000000 | bytes 3000000 | tf_op jit(solution)/shard_map/att_grads/pallas_call | solution.py:177
  35.4 2.0 %collective-permute-start.6 = (bf16[384,384]{1,0:T(8,128)(2,1)S(1)}, bf16[384,384]{1,0:T(8,128)(2,1)S(1)}, u32[]{:S(2)}, u32[]{:S(2)}) collective-permute-start(bf16[384,384]{1,0:T(8,128)(2,1)S(1)} %get-tuple-element.39), channel_id=1, source_target_pairs={{0,3},{3,0},{1,2},{2,1},{4,7},{7,4},{5,6},{6,5},{8,11},{11,8},{9,1... | collective-permute-start | bytes 884744 | tf_op jit(solution)/shard_map/ppermute | solution.py:727
  37.4 0.0 collective-permute-start.5
  37.4 4.7 %gelu_pool.1 = (bf16[768,768]{1,0:T(8,128)(2,1)}, bf16[48,768]{1,0:T(8,128)(2,1)}) custom-call(f32[768,768]{1,0:T(8,128)} %get-tuple-element.35.after.pre, bf16[768,768]{1,0:T(8,128)(2,1)} %bitcast.29, bf16[192,384]{1,0:T(8,128)(2,1)S(1)} %get-tuple-element.38.after), custom_call_target="tpu_custom_call" | custom-call | flops 3000000000 | bytes 5000000 | tf_op jit(solution)/shard_map/gelu_pool/pallas_call | solution.py:358
  42.1 0.1 collective-permute-done.6.dkv_in
  42.2 3.1 %att_join.1 = (bf16[8,96,768]{2,1,0:T(8,128)(2,1)}, bf16[384,288]{1,0:T(8,128)(2,1)S(1)}, bf16[384,288]{1,0:T(8,128)(2,1)S(1)}) custom-call(s32[1]{0:T(128)} %bitcast.1.core, f32[384,192]{1,0:T(8,128)} %get-tuple-element.36.dq_own, f32[384,384]{1,0:T(8,128)} %get-tuple-element.37.dkv_own, bf16[192,384]{1,0:T(8,128)(2,1)S(1)} %collective-permute-done.5.dq_in, ...), custom_call_target="tpu_custom_call" | custom-call | flops 10000000000 | bytes 3500000 | tf_op jit(solution)/shard_map/att_join/pallas_call | solution.py:272
  45.3 19.5 %all_to_all.15.parts.p0 = bf16[8,96,768]{2,1,0:T(8,128)(2,1)S(1)} all-to-all(bf16[8,96,768]{2,1,0:T(8,128)(2,1)} %get-tuple-element.41), channel_id=1, replica_groups=mesh['yh'=2,'core'=2,'yl'=2,'x'=4,'z'=4] {'yl','x'}, dimensions={0} | all-to-all | bytes 2359296 | tf_op jit(solution)/shard_map/all_to_all | solution.py:730
  64.8 4.3 %collective-permute-start.9 = (bf16[784,768]{1,0:T(8,128)(2,1)S(1)}, bf16[784,768]{1,0:T(8,128)(2,1)S(1)}, u32[]{:S(2)}, u32[]{:S(2)}) collective-permute-start(bf16[784,768]{1,0:T(8,128)(2,1)S(1)} %get-tuple-element.52.xp), channel_id=1, source_target_pairs={{0,32},{32,0},{1,33},{33,1},{2,34},{34,2},{3,35},{35,3},{4,36},{36... | collective-permute-start | bytes 3612680 | tf_op jit(solution)/shard_map/ppermute | solution.py:733
  69.1 0.0 collective-permute-start.11
  69.1 2.6 %pre_grads.1 = (bf16[768,768]{1,0:T(8,128)(2,1)}, bf16[768,384]{1,0:T(8,128)(2,1)S(1)}, bf16[768,384]{1,0:T(8,128)(2,1)S(1)}, f32[48,768]{1,0:T(8,128)}) custom-call(s32[1]{0:T(128)} %bitcast.1.core, bf16[8,96,768]{2,1,0:T(8,128)(2,1)S(1)} %all_to_all.15.parts.p0, bf16[768,768]{1,0:T(8,128)(2,1)} %bitcast.22, bf16[768,768]{1,0:T(8,128)(2,1)} %get-tuple-element.44.slope), custom_call_target="tpu_custom_call" | custom-call | flops 2949120 | bytes 6000000 | tf_op jit(solution)/shard_map/pre_grads/pallas_call | solution.py:446
  71.8 0.6 collective-permute-start.10
  72.3 0.1 collective-permute-start.12
  72.4 0.6 turn_input.2
  73.0 0.6 turn_input.3
  73.6 1.0 collective-permute-done.12.s1
  74.6 8.4 %weight_grads.1 = bf16[768,2304]{1,0:T(8,128)(2,1)} custom-call(bf16[768,768]{1,0:T(8,128)(2,1)S(1)} %get-tuple-element.53.xt0, bf16[768,512]{1,0:T(8,128)(2,1)S(1)} %get-tuple-element.54.al0, bf16[768,768]{1,0:T(8,128)(2,1)S(1)} %get-tuple-element.55.xt1, bf16[768,512]{1,0:T(8,128)(2,1)S(1)} %get-tuple-element.56.al1, ...), custom_call_target="tpu_custom_call" | custom-call | flops 4529848320 | bytes 10000000 | tf_op jit(solution)/shard_map/weight_grads/pallas_call | solution.py:512
  83.0 5.5 %all-to-all-start.2 = ((bf16[32,24,2304]{2,1,0:T(8,128)(2,1)}), bf16[32,24,2304]{2,1,0:T(8,128)(2,1)S(1)}, u32[]{:S(2)}, u32[]{:S(2)}) async-start(bf16[32,24,2304]{2,1,0:T(8,128)(2,1)} %bitcast.21), calls=%async_computation.2 | async-start | bytes 7077888 | tf_op jit(solution)/shard_map/all_to_all | solution.py:741
  88.5 9.1 %conv_adjoint.1 = (bf16[768,768]{1,0:T(8,128)(2,1)}, f32[8,768]{1,0:T(8,128)S(1)}, f32[8,768]{1,0:T(8,128)S(1)}, f32[8,768]{1,0:T(8,128)S(1)}, f32[8,768]{1,0:T(8,128)S(1)}) custom-call(s32[1]{0:T(128)} %bitcast.par, bf16[768,768]{1,0:T(8,128)(2,1)} %get-tuple-element.45.pre, bf16[5,768,768]{2,1,0:T(8,128)(2,1)} %w.3, bf16[768,768]{1,0:T(8,128)(2,1)} %bitcast.23, ...), custom_call_target="tpu_custom_call" | custom-call | flops 4529848320 | bytes 9500000 | tf_op jit(solution)/shard_map/conv_adjoint/pallas_call | solution.py:565
  97.6 0.6 copy-done.3
  98.2 0.6 copy-done.5
  98.8 1.2 collective-permute-start.7
  100.0 4.0 %collective-permute-start.8 = (f32[8,768]{1,0:T(8,128)S(1)}, f32[8,768]{1,0:T(8,128)}, u32[]{:S(2)}, u32[]{:S(2)}) collective-permute-start(f32[8,768]{1,0:T(8,128)S(1)} %get-tuple-element.51), channel_id=1, source_target_pairs={{1,2},{2,1},{3,4},{4,3},{5,6},{6,5},{7,8},{8,7},{9,10},{10,9},{11,... | collective-permute-start | bytes 73736 | tf_op jit(solution)/shard_map/ppermute | solution.py:745
  104.0 12.7 %collective-permute-done.7.got1.after = f32[8,768]{1,0:T(8,128)S(1)} collective-permute-done((f32[8,768]{1,0:T(8,128)S(1)}, f32[8,768]{1,0:T(8,128)S(1)}, u32[]{:S(2)}, u32[]{:S(2)}) %collective-permute-start.7) | collective-permute-done | bytes 24608 | tf_op jit(solution)/shard_map/ppermute | solution.py:744
  116.6 0.6 copy-done.1
  117.2 19.2 %collective-permute-done.8.got2.after2 = f32[8,768]{1,0:T(8,128)} collective-permute-done((f32[8,768]{1,0:T(8,128)S(1)}, f32[8,768]{1,0:T(8,128)}, u32[]{:S(2)}, u32[]{:S(2)}) %collective-permute-start.8) | collective-permute-done | bytes 24608 | tf_op jit(solution)/shard_map/ppermute | solution.py:745
  136.4 2.2 %all-to-all-done.2.parts = bf16[32,24,2304]{2,1,0:T(8,128)(2,1)S(1)} async-done(((bf16[32,24,2304]{2,1,0:T(8,128)(2,1)}), bf16[32,24,2304]{2,1,0:T(8,128)(2,1)S(1)}, u32[]{:S(2)}, u32[]{:S(2)}) %all-to-all-start.2) | async-done | bytes 3538976 | tf_op jit(solution)/shard_map/all_to_all | solution.py:741
  138.6 1.1 sum_partials.1.a
  139.7 2.8 %collective-permute-start.13 = (bf16[24,4224]{1,0:T(8,128)(2,1)S(1)}, bf16[24,4224]{1,0:T(8,128)(2,1)S(1)}, u32[]{:S(2)}, u32[]{:S(2)}) collective-permute-start(bf16[24,4224]{1,0:T(8,128)(2,1)S(1)} %sum_partials.1.a), channel_id=1, source_target_pairs={{0,64},{64,0},{1,65},{65,1},{2,66},{66,2},{3,67},{67,3},{4,68},{68... | collective-permute-start | bytes 608264 | tf_op jit(solution)/shard_map/ppermute | solution.py:748
  142.4 1.4 add_edges.1.after
  143.8 2.7 %collective-permute-done.13.b = bf16[24,4224]{1,0:T(8,128)(2,1)S(1)} collective-permute-done((bf16[24,4224]{1,0:T(8,128)(2,1)S(1)}, bf16[24,4224]{1,0:T(8,128)(2,1)S(1)}, u32[]{:S(2)}, u32[]{:S(2)}) %collective-permute-start.13) | collective-permute-done | bytes 202784 | tf_op jit(solution)/shard_map/ppermute | solution.py:748
  146.6 0.1 add_pair.1.mine
  146.6 2.2 %collective-permute-start.14 = (f32[24,4224]{1,0:T(8,128)S(1)}, f32[24,4224]{1,0:T(8,128)S(1)}, u32[]{:S(2)}, u32[]{:S(2)}) collective-permute-start(f32[24,4224]{1,0:T(8,128)S(1)} %add_pair.1.mine), channel_id=1, source_target_pairs={{0,32},{32,0},{1,33},{33,1},{2,34},{34,2},{3,35},{35,3},{4,36},{36... | collective-permute-start | bytes 1216520 | tf_op jit(solution)/shard_map/ppermute | solution.py:751
  148.8 1.4 collective-permute-done.14.other
  150.2 1.3 place.1
  (19 shorter events, 0.0 us)
Async XLA Ops:
  2.7 12.2 %copy-start = (bf16[8,48,768]{2,1,0:T(8,128)(2,1)S(1)}, bf16[8,48,768]{2,1,0:T(8,128)(2,1)}, u32[]{:S(2)}) copy-start(bf16[8,48,768]{2,1,0:T(8,128)(2,1)} %pack_heads.1.after) | copy-start | bytes 1769476
  2.7 15.3 %all-to-all-start = ((bf16[8,48,768]{2,1,0:T(8,128)(2,1)}), bf16[8,48,768]{2,1,0:T(8,128)(2,1)S(1)}, u32[]{:S(2)}, u32[]{:S(2)}) async-start(bf16[8,48,768]{2,1,0:T(8,128)(2,1)} %pack_heads.1.after), calls=%async_computation | async-start | bytes 1179648 | tf_op jit(solution)/shard_map/all_to_all | solution.py:711
  8.8 10.8 %collective-permute-start.3 = (bf16[2,768]{1,0:T(2,128)(2,1)S(1)}, bf16[2,768]{1,0:T(2,128)(2,1)S(1)}, u32[]{:S(2)}, u32[]{:S(2)}) collective-permute-start(bf16[2,768]{1,0:T(2,128)(2,1)S(1)} %get-tuple-element.63), channel_id=1, source_target_pairs={{1,2},{2,1},{3,4},{4,3},{5,6},{6,5},{7,8},{8,7},{9,10},{10,9},{11,... | collective-permute-start | bytes 9224 | tf_op jit(solution)/shard_map/ppermute | solution.py:720
  14.8 4.8 %collective-permute-start.2 = (bf16[2,768]{1,0:T(2,128)(2,1)S(1)}, bf16[2,768]{1,0:T(2,128)(2,1)S(1)}, u32[]{:S(2)}, u32[]{:S(2)}) collective-permute-start(bf16[2,768]{1,0:T(2,128)(2,1)S(1)} %get-tuple-element.64), channel_id=1, source_target_pairs={{0,1},{1,0},{2,3},{3,2},{4,5},{5,4},{6,7},{7,6},{8,9},{9,8},{10,11... | collective-permute-start | bytes 9224 | tf_op jit(solution)/shard_map/ppermute | solution.py:719
  18.0 10.1 %collective-permute-start.1 = (bf16[384,384]{1,0:T(8,128)(2,1)S(1)}, bf16[384,384]{1,0:T(8,128)(2,1)S(1)}, u32[]{:S(2)}, u32[]{:S(2)}) collective-permute-start(bf16[384,384]{1,0:T(8,128)(2,1)S(1)} %get-tuple-element.34), channel_id=1, source_target_pairs={{0,3},{3,0},{1,2},{2,1},{4,7},{7,4},{5,6},{6,5},{8,11},{11,8},{9,1... | collective-permute-start | bytes 884744 | tf_op jit(solution)/shard_map/ppermute | solution.py:715
  19.2 9.0 %collective-permute-start = (bf16[384,384]{1,0:T(8,128)(2,1)S(1)}, bf16[384,384]{1,0:T(8,128)(2,1)S(1)}, u32[]{:S(2)}, u32[]{:S(2)}) collective-permute-start(bf16[384,384]{1,0:T(8,128)(2,1)S(1)} %get-tuple-element.33.after), channel_id=1, source_target_pairs={{0,1},{1,0},{2,3},{3,2},{4,5},{5,4},{6,7},{7,6},{8,9},{9,8},{10,11... | collective-permute-start | bytes 884744 | tf_op jit(solution)/shard_map/ppermute | solution.py:714
  29.4 2.8 %collective-permute-start.4 = (f32[8,768]{1,0:T(8,128)S(1)}, f32[8,768]{1,0:T(8,128)S(1)}, u32[]{:S(2)}, u32[]{:S(2)}) collective-permute-start(f32[8,768]{1,0:T(8,128)S(1)} %att_stats.1.st), channel_id=1, source_target_pairs={{0,1},{1,0},{2,3},{3,2},{4,5},{5,4},{6,7},{7,6},{8,9},{9,8},{10,11... | collective-permute-start | bytes 73736 | tf_op jit(solution)/shard_map/ppermute | solution.py:724
  35.4 6.8 %collective-permute-start.6 = (bf16[384,384]{1,0:T(8,128)(2,1)S(1)}, bf16[384,384]{1,0:T(8,128)(2,1)S(1)}, u32[]{:S(2)}, u32[]{:S(2)}) collective-permute-start(bf16[384,384]{1,0:T(8,128)(2,1)S(1)} %get-tuple-element.39), channel_id=1, source_target_pairs={{0,3},{3,0},{1,2},{2,1},{4,7},{7,4},{5,6},{6,5},{8,11},{11,8},{9,1... | collective-permute-start | bytes 884744 | tf_op jit(solution)/shard_map/ppermute | solution.py:727
  37.4 4.7 %collective-permute-start.5 = (bf16[192,384]{1,0:T(8,128)(2,1)S(1)}, bf16[192,384]{1,0:T(8,128)(2,1)S(1)}, u32[]{:S(2)}, u32[]{:S(2)}) collective-permute-start(bf16[192,384]{1,0:T(8,128)(2,1)S(1)} %get-tuple-element.38.after), channel_id=1, source_target_pairs={{0,1},{1,0},{2,3},{3,2},{4,5},{5,4},{6,7},{7,6},{8,9},{9,8},{10,11... | collective-permute-start | bytes 442376 | tf_op jit(solution)/shard_map/ppermute | solution.py:726
  64.8 8.2 %collective-permute-start.9 = (bf16[784,768]{1,0:T(8,128)(2,1)S(1)}, bf16[784,768]{1,0:T(8,128)(2,1)S(1)}, u32[]{:S(2)}, u32[]{:S(2)}) collective-permute-start(bf16[784,768]{1,0:T(8,128)(2,1)S(1)} %get-tuple-element.52.xp), channel_id=1, source_target_pairs={{0,32},{32,0},{1,33},{33,1},{2,34},{34,2},{3,35},{35,3},{4,36},{36... | collective-permute-start | bytes 3612680 | tf_op jit(solution)/shard_map/ppermute | solution.py:733
  69.1 5.5 %collective-permute-start.11 = (bf16[8,96,768]{2,1,0:T(8,128)(2,1)S(1)}, bf16[8,96,768]{2,1,0:T(8,128)(2,1)S(1)}, u32[]{:S(2)}, u32[]{:S(2)}) collective-permute-start(bf16[8,96,768]{2,1,0:T(8,128)(2,1)S(1)} %all_to_all.15.parts.p0), channel_id=1, source_target_pairs={{0,32},{32,0},{1,33},{33,1},{2,34},{34,2},{3,35},{35,3},{4,36},{36... | collective-permute-start | bytes 3538952 | tf_op jit(solution)/shard_map/ppermute | solution.py:732
  71.8 2.8 %collective-permute-start.10 = (bf16[768,384]{1,0:T(8,128)(2,1)S(1)}, bf16[768,384]{1,0:T(8,128)(2,1)S(1)}, u32[]{:S(2)}, u32[]{:S(2)}) collective-permute-start(bf16[768,384]{1,0:T(8,128)(2,1)S(1)} %get-tuple-element.58), channel_id=1, source_target_pairs={{0,32},{32,0},{1,33},{33,1},{2,34},{34,2},{3,35},{35,3},{4,36},{36... | collective-permute-start | bytes 1769480 | tf_op jit(solution)/shard_map/ppermute | solution.py:739
  72.3 2.2 %collective-permute-start.12 = (bf16[384,288]{1,0:T(8,128)(2,1)S(1)}, bf16[384,288]{1,0:T(8,128)(2,1)S(1)}, u32[]{:S(2)}, u32[]{:S(2)}) collective-permute-start(bf16[384,288]{1,0:T(8,128)(2,1)S(1)} %get-tuple-element.60), channel_id=1, source_target_pairs={{0,32},{32,0},{1,33},{33,1},{2,34},{34,2},{3,35},{35,3},{4,36},{36... | collective-permute-start | bytes 663560 | tf_op jit(solution)/shard_map/ppermute | solution.py:734
  83.0 55.6 %all-to-all-start.2 = ((bf16[32,24,2304]{2,1,0:T(8,128)(2,1)}), bf16[32,24,2304]{2,1,0:T(8,128)(2,1)S(1)}, u32[]{:S(2)}, u32[]{:S(2)}) async-start(bf16[32,24,2304]{2,1,0:T(8,128)(2,1)} %bitcast.21), calls=%async_computation.2 | async-start | bytes 7077888 | tf_op jit(solution)/shard_map/all_to_all | solution.py:741
  97.6 0.6 copy-start.3
  98.2 0.6 copy-start.5
  98.8 17.8 %collective-permute-start.7 = (f32[8,768]{1,0:T(8,128)S(1)}, f32[8,768]{1,0:T(8,128)S(1)}, u32[]{:S(2)}, u32[]{:S(2)}) collective-permute-start(f32[8,768]{1,0:T(8,128)S(1)} %get-tuple-element.50), channel_id=1, source_target_pairs={{0,1},{1,0},{2,3},{3,2},{4,5},{5,4},{6,7},{7,6},{8,9},{9,8},{10,11... | collective-permute-start | bytes 73736 | tf_op jit(solution)/shard_map/ppermute | solution.py:744
  100.0 36.4 %collective-permute-start.8 = (f32[8,768]{1,0:T(8,128)S(1)}, f32[8,768]{1,0:T(8,128)}, u32[]{:S(2)}, u32[]{:S(2)}) collective-permute-start(f32[8,768]{1,0:T(8,128)S(1)} %get-tuple-element.51), channel_id=1, source_target_pairs={{1,2},{2,1},{3,4},{4,3},{5,6},{6,5},{7,8},{8,7},{9,10},{10,9},{11,... | collective-permute-start | bytes 73736 | tf_op jit(solution)/shard_map/ppermute | solution.py:745
  116.6 0.6 copy-start.1
  138.6 3.8 %copy-start.2 = (f32[8,768]{1,0:T(8,128)S(1)}, f32[8,768]{1,0:T(8,128)}, u32[]{:S(2)}) copy-start(f32[8,768]{1,0:T(8,128)} %copy-done.1) | copy-start | bytes 73732
  138.6 3.8 %copy-start.4 = (f32[8,768]{1,0:T(8,128)S(1)}, f32[8,768]{1,0:T(8,128)}, u32[]{:S(2)}) copy-start(f32[8,768]{1,0:T(8,128)} %copy-done.3) | copy-start | bytes 73732
  138.6 3.8 %copy-start.6 = (f32[8,768]{1,0:T(8,128)S(1)}, f32[8,768]{1,0:T(8,128)}, u32[]{:S(2)}) copy-start(f32[8,768]{1,0:T(8,128)} %copy-done.5) | copy-start | bytes 73732
  139.7 6.9 %collective-permute-start.13 = (bf16[24,4224]{1,0:T(8,128)(2,1)S(1)}, bf16[24,4224]{1,0:T(8,128)(2,1)S(1)}, u32[]{:S(2)}, u32[]{:S(2)}) collective-permute-start(bf16[24,4224]{1,0:T(8,128)(2,1)S(1)} %sum_partials.1.a), channel_id=1, source_target_pairs={{0,64},{64,0},{1,65},{65,1},{2,66},{66,2},{3,67},{67,3},{4,68},{68... | collective-permute-start | bytes 608264 | tf_op jit(solution)/shard_map/ppermute | solution.py:748
  146.6 3.6 %collective-permute-start.14 = (f32[24,4224]{1,0:T(8,128)S(1)}, f32[24,4224]{1,0:T(8,128)S(1)}, u32[]{:S(2)}, u32[]{:S(2)}) collective-permute-start(f32[24,4224]{1,0:T(8,128)S(1)} %add_pair.1.mine), channel_id=1, source_target_pairs={{0,32},{32,0},{1,33},{33,1},{2,34},{34,2},{3,35},{35,3},{4,36},{36... | collective-permute-start | bytes 1216520 | tf_op jit(solution)/shard_map/ppermute | solution.py:751

commit v5 on v4

--- a/solution.py
+++ b/solution.py
@@ -468,22 +468,16 @@
     )(core, parts, hbm(skip), hbm(slope))
 
 
-def weights_kernel(xt0, al0, xt1, al1, y0, y1, p0, p1, s0, s1, out, yf, yt, made, sems):
+def weights_kernel(xt0, al0, xt1, al1, y0, y1, p0, p1, s0, s1, out, yf, wide, rest, made, sems):
     def copy(t):
         cols = pl.ds(t * HALF, HALF)
         return pltpu.make_async_copy(made.at[t], out.at[:, cols], sems.at[t])
 
-    def shifted(xt, al, t, rows):
-        if t < 2:
-            return jnp.concatenate([xt[rows, : ROWS - 128], al[rows, t * 128 : t * 128 + 128]], axis=1)
-        if t > 2:
-            return jnp.concatenate([al[rows, (t - 1) * 128 : t * 128], xt[rows, 128:]], axis=1)
-        return xt[rows, :]
-
     def pooled(ref):
         return jnp.concatenate([ref[h, ATT : 2 * ATT, :] for h in range(HEADS)], axis=0)
 
-    made[TAPS, :, 0:QH] = (tn(pooled(p0), s0[...]) + tn(pooled(p1), s1[...])).astype(BF)
+    part = jnp.concatenate([pooled(p0), pooled(p1)], axis=0)
+    made[TAPS, :, 0:QH] = tn(part, jnp.concatenate([s0[...], s1[...]], axis=0)).astype(BF)
     made[TAPS, :, QH:HALF] = jnp.zeros((C, HALF - QH), BF)
     copy(TAPS).start()
     for i, ref in enumerate((y0, y1)):
@@ -491,19 +485,36 @@
         yf[i, 8 : 8 + ROWS, :] = got
         yf[i, 0:8, :] = got[ROWS - 8 :]
         yf[i, 8 + ROWS : 16 + ROWS, :] = got[0:8]
-    for t in (2, 0, 1, 3, 4):
-        if t == 2:
-            right = [y0[...], y1[...]]
-        else:
+    chunks = range(0, C, 256)
+    for r in chunks:
+        rows = slice(r, r + 256)
+        left = jnp.concatenate([xt0[rows, :], xt1[rows, :]], axis=1)
+        made[2, rows, :] = mm(left, jnp.concatenate([y0[...], y1[...]], axis=0)).astype(BF)
+    copy(2).start()
+    for g, taps in enumerate(((0, 1), (3, 4))):
+        base, spot = (0, 2 * 256) if g == 0 else (256, 0)
+        for k, t in enumerate(taps):
+            cols = slice(k * HALF, (k + 1) * HALF)
             for i in range(2):
-                yt[t, i] = yf[i, 10 - t : 10 - t + ROWS, :].astype(BF)
-            right = [yt[t, 0], yt[t, 1]]
-        for r in range(0, C, 256):
+                at = 10 - t + base
+                wide[g, i * 512 : (i + 1) * 512, cols] = yf[i, at : at + 512, :].astype(BF)
+                at = 10 - t + spot
+                rest[2 * g + k, i * 256 : (i + 1) * 256, :] = yf[i, at : at + 256, :].astype(BF)
+        for r in chunks:
             rows = slice(r, r + 256)
-            made[t, rows, :] = (
-                mm(shifted(xt0, al0, t, rows), right[0]) + mm(shifted(xt1, al1, t, rows), right[1])
-            ).astype(BF)
-        copy(t).start()
+            left = jnp.concatenate([xt0[rows, base : base + 512], xt1[rows, base : base + 512]], axis=1)
+            both = mm(left, wide[g])
+            for k, t in enumerate(taps):
+                tiles = []
+                for xt, al in ((xt0, al0), (xt1, al1)):
+                    if g == 0:
+                        tiles += [xt[rows, 512:640], al[rows, t * 128 : t * 128 + 128]]
+                    else:
+                        tiles += [al[rows, (t - 1) * 128 : t * 128], xt[rows, 128:256]]
+                edge = mm(jnp.concatenate(tiles, axis=1), rest[2 * g + k])
+                made[t, rows, :] = (both[:, k * HALF : (k + 1) * HALF] + edge).astype(BF)
+        for t in taps:
+            copy(t).start()
     for t in range(TAPS + 1):
         copy(t).wait()
 
@@ -516,7 +527,8 @@
         out_specs=pl.BlockSpec(memory_space=pltpu.HBM),
         scratch_shapes=[
             pltpu.VMEM((2, ROWS + 16, HALF), F32),
-            pltpu.VMEM((TAPS, 2, ROWS, HALF), BF),
+            pltpu.VMEM((2, 1024, 2 * HALF), BF),
+            pltpu.VMEM((4, 512, HALF), BF),
             pltpu.VMEM((TAPS + 1, C, HALF), BF),
             pltpu.SemaphoreType.DMA((TAPS + 1,)),
         ],

time: 152 us -> 151 us (level)
  no operation moved by 1% of the time
where the time goes in v5:
time: 151 us
  Pallas kernels  50.5 us (33%)
  waiting for transfers between devices  40.6 us (27%)
  starting transfers between devices  36.8 us (24%)
  blocking collectives  19.5 us (13%)
  local copies, waits for them, and re-layouts  1.84 us (1%)
    all_to_all x1, blocking collectives, local(): parts = lax.all_to_all(pool_part, HAX, 0, 0, tiled=True)  19.5 us
    ppermute x1, waiting for transfers between devices, local(): rim2 = lax.ppermute(next_, SEQ, NEXT)  19 us
    ppermute x1, waiting for transfers between devices, local(): rim1 = lax.ppermute(near, SEQ, NEAR)  12.7 us
    pallas_call x1, Pallas kernels, conv_adjoint(): pl.pallas_call(adjoint_kernel, grid=(TAPS,), out_shape=(far((ROWS, C), BF...  9.08 us
    pallas_call x1, Pallas kernels, conv_apply(): pl.pallas_call(conv_kernel, out_shape=(far((ROWS, C), F32), sds((ROWS + 1...  8.53 us
    pallas_call x1, Pallas kernels, weight_grads(): pl.pallas_call(weights_kernel, out_shape=far((C, 2304), BF), in_specs=[VM...  7.82 us
    ppermute x1, starting transfers between devices, local(): got2 = lax.ppermute(jnp.where(par[0] == 0, head_rows, tail_rows), SEQ, NEXT)  5.96 us
    all_to_all x1, starting transfers between devices, local(): got = lax.all_to_all(terms.reshape(32, 24, 2304), SEQ, 0, 0, tiled=True)  5.7 us
  transfers between devices with their start and end apart: 17, of which 8 were waited for; matrix products, arithmetic and copies ran while one was open for 0% of the time, Pallas kernels for 20%

profile of v5, /device:TPU:7, one launch (start us, length us, event | category | flops | bytes accessed | tf_op | source)
XLA Modules:
  0.0 150.8 jit_solution(10823272010653657865)
XLA Ops:
  0.6 2.1 %pack_heads.1.after = bf16[8,48,768]{2,1,0:T(8,128)(2,1)} custom-call(bf16[48,1536]{1,0:T(8,128)(2,1)} %bitcast.24, bf16[48,1536]{1,0:T(8,128)(2,1)} %bitcast.25, bf16[48,1536]{1,0:T(8,128)(2,1)} %bitcast.26, bf16[48,1536]{1,0:T(8,128)(2,1)} %bitcast.27), custom_call_target="tpu_custom_call" | custom-call | bytes 1200000 | tf_op jit(solution)/shard_map/pack_heads/pallas_call | solution.py:94
  2.7 0.0 copy-start
  2.7 5.4 %all-to-all-start = ((bf16[8,48,768]{2,1,0:T(8,128)(2,1)}), bf16[8,48,768]{2,1,0:T(8,128)(2,1)S(1)}, u32[]{:S(2)}, u32[]{:S(2)}) async-start(bf16[8,48,768]{2,1,0:T(8,128)(2,1)} %pack_heads.1.after), calls=%async_computation | async-start | bytes 1179648 | tf_op jit(solution)/shard_map/all_to_all | solution.py:723
  8.1 0.7 fusion.1
  8.8 6.0 %collective-permute-start.3 = (bf16[2,768]{1,0:T(2,128)(2,1)S(1)}, bf16[2,768]{1,0:T(2,128)(2,1)S(1)}, u32[]{:S(2)}, u32[]{:S(2)}) collective-permute-start(bf16[2,768]{1,0:T(2,128)(2,1)S(1)} %get-tuple-element.63), channel_id=1, source_target_pairs={{1,2},{2,1},{3,4},{4,3},{5,6},{6,5},{7,8},{8,7},{9,10},{10,9},{11,... | collective-permute-start | bytes 9224 | tf_op jit(solution)/shard_map/ppermute | solution.py:732
  14.8 0.1 collective-permute-start.2
  14.9 3.1 %head_weights.1.after.wh = bf16[576,768]{1,0:T(8,128)(2,1)} custom-call(s32[1]{0:T(128)} %bitcast.7.pair, s32[1]{0:T(128)} %bitcast.8.odd, bf16[768,4608]{1,0:T(8,128)(2,1)} %wv.1, bf16[768,4608]{1,0:T(8,128)(2,1)} %wv.1, bf16[768,4608]{1,0:T(8,128)(2,1)} %wv.1, bf16[8,48,768]{2,1,0:T(8,128)(2,1)S(1)} %copy-done), custom_call_target="tpu_custom_call" | custom-call | bytes 3000000 | tf_op jit(solution)/shard_map/head_weights/pallas_call | solution.py:224
  18.0 0.1 split_own.1
  18.0 1.1 collective-permute-start.1
  19.2 0.5 collective-permute-start
  19.6 8.5 %conv_apply.1 = (f32[768,768]{1,0:T(8,128)}, bf16[784,768]{1,0:T(8,128)(2,1)S(1)}) custom-call(s32[1]{0:T(128)} %bitcast.par, bf16[768,768]{1,0:T(8,128)(2,1)} %bitcast.28, bf16[2,768]{1,0:T(2,128)(2,1)S(1)} %collective-permute-done.2.got1, bf16[2,768]{1,0:T(2,128)(2,1)S(1)} %collective-permute-done.3.got2, bf16[5,768,768]{2,1,0:T(8,128)(2,1)} %w.3, ...), custom_call_target="tpu_custom_call" | custom-call | flops 4529848320 | bytes 9500000 | tf_op jit(solution)/shard_map/conv_apply/pallas_call | solution.py:326
  28.2 1.2 att_stats.1.st
  29.4 1.1 collective-permute-start.4
  30.4 1.7 %collective-permute-done.4.st2 = f32[8,768]{1,0:T(8,128)S(1)} collective-permute-done((f32[8,768]{1,0:T(8,128)S(1)}, f32[8,768]{1,0:T(8,128)S(1)}, u32[]{:S(2)}, u32[]{:S(2)}) %collective-permute-start.4) | collective-permute-done | bytes 24608 | tf_op jit(solution)/shard_map/ppermute | solution.py:736
  32.1 3.3 %att_grads.1 = (f32[384,192]{1,0:T(8,128)}, bf16[192,384]{1,0:T(8,128)(2,1)S(1)}, f32[384,384]{1,0:T(8,128)}, bf16[384,384]{1,0:T(8,128)(2,1)S(1)}) custom-call(bf16[384,768]{1,0:T(8,128)(2,1)S(1)} %bitcast.19, bf16[384,384]{1,0:T(8,128)(2,1)S(1)} %collective-permute-done.qg, bf16[384,384]{1,0:T(8,128)(2,1)S(1)} %collective-permute-done.1.kv, ...), custom_call_target="tpu_custom_call" | custom-call | flops 20000000000 | bytes 3000000 | tf_op jit(solution)/shard_map/att_grads/pallas_call | solution.py:177
  35.4 2.0 %collective-permute-start.6 = (bf16[384,384]{1,0:T(8,128)(2,1)S(1)}, bf16[384,384]{1,0:T(8,128)(2,1)S(1)}, u32[]{:S(2)}, u32[]{:S(2)}) collective-permute-start(bf16[384,384]{1,0:T(8,128)(2,1)S(1)} %get-tuple-element.39), channel_id=1, source_target_pairs={{0,3},{3,0},{1,2},{2,1},{4,7},{7,4},{5,6},{6,5},{8,11},{11,8},{9,1... | collective-permute-start | bytes 884744 | tf_op jit(solution)/shard_map/ppermute | solution.py:739
  37.4 0.0 collective-permute-start.5
  37.4 4.7 %gelu_pool.1 = (bf16[768,768]{1,0:T(8,128)(2,1)}, bf16[48,768]{1,0:T(8,128)(2,1)}) custom-call(f32[768,768]{1,0:T(8,128)} %get-tuple-element.35.after.pre, bf16[768,768]{1,0:T(8,128)(2,1)} %bitcast.29, bf16[192,384]{1,0:T(8,128)(2,1)S(1)} %get-tuple-element.38.after), custom_call_target="tpu_custom_call" | custom-call | flops 3000000000 | bytes 5000000 | tf_op jit(solution)/shard_map/gelu_pool/pallas_call | solution.py:358
  42.1 0.1 collective-permute-done.6.dkv_in
  42.2 3.1 %att_join.1 = (bf16[8,96,768]{2,1,0:T(8,128)(2,1)}, bf16[384,288]{1,0:T(8,128)(2,1)S(1)}, bf16[384,288]{1,0:T(8,128)(2,1)S(1)}) custom-call(s32[1]{0:T(128)} %bitcast.1.core, f32[384,192]{1,0:T(8,128)} %get-tuple-element.36.dq_own, f32[384,384]{1,0:T(8,128)} %get-tuple-element.37.dkv_own, bf16[192,384]{1,0:T(8,128)(2,1)S(1)} %collective-permute-done.5.dq_in, ...), custom_call_target="tpu_custom_call" | custom-call | flops 10000000000 | bytes 3500000 | tf_op jit(solution)/shard_map/att_join/pallas_call | solution.py:272
  45.3 19.5 %all_to_all.15.parts.p0 = bf16[8,96,768]{2,1,0:T(8,128)(2,1)S(1)} all-to-all(bf16[8,96,768]{2,1,0:T(8,128)(2,1)} %get-tuple-element.41), channel_id=1, replica_groups=mesh['yh'=2,'core'=2,'yl'=2,'x'=4,'z'=4] {'yl','x'}, dimensions={0} | all-to-all | bytes 2359296 | tf_op jit(solution)/shard_map/all_to_all | solution.py:742
  64.8 4.3 %collective-permute-start.9 = (bf16[784,768]{1,0:T(8,128)(2,1)S(1)}, bf16[784,768]{1,0:T(8,128)(2,1)S(1)}, u32[]{:S(2)}, u32[]{:S(2)}) collective-permute-start(bf16[784,768]{1,0:T(8,128)(2,1)S(1)} %get-tuple-element.52.xp), channel_id=1, source_target_pairs={{0,32},{32,0},{1,33},{33,1},{2,34},{34,2},{3,35},{35,3},{4,36},{36... | collective-permute-start | bytes 3612680 | tf_op jit(solution)/shard_map/ppermute | solution.py:745
  69.1 0.0 collective-permute-start.11
  69.1 2.6 %pre_grads.1 = (bf16[768,768]{1,0:T(8,128)(2,1)}, bf16[768,384]{1,0:T(8,128)(2,1)S(1)}, bf16[768,384]{1,0:T(8,128)(2,1)S(1)}, f32[48,768]{1,0:T(8,128)}) custom-call(s32[1]{0:T(128)} %bitcast.1.core, bf16[8,96,768]{2,1,0:T(8,128)(2,1)S(1)} %all_to_all.15.parts.p0, bf16[768,768]{1,0:T(8,128)(2,1)} %bitcast.22, bf16[768,768]{1,0:T(8,128)(2,1)} %get-tuple-element.44.slope), custom_call_target="tpu_custom_call" | custom-call | flops 2949120 | bytes 6000000 | tf_op jit(solution)/shard_map/pre_grads/pallas_call | solution.py:446
  71.8 0.6 collective-permute-start.10
  72.3 0.1 collective-permute-start.12
  72.4 0.6 turn_input.2
  73.0 0.6 turn_input.3
  73.6 1.0 collective-permute-done.12.s1
  74.6 7.8 %weight_grads.1 = bf16[768,2304]{1,0:T(8,128)(2,1)} custom-call(bf16[768,768]{1,0:T(8,128)(2,1)S(1)} %get-tuple-element.53.xt0, bf16[768,512]{1,0:T(8,128)(2,1)S(1)} %get-tuple-element.54.al0, bf16[768,768]{1,0:T(8,128)(2,1)S(1)} %get-tuple-element.55.xt1, bf16[768,512]{1,0:T(8,128)(2,1)S(1)} %get-tuple-element.56.al1, ...), custom_call_target="tpu_custom_call" | custom-call | flops 4529848320 | bytes 10000000 | tf_op jit(solution)/shard_map/weight_grads/pallas_call | solution.py:523
  82.4 5.7 %all-to-all-start.2 = ((bf16[32,24,2304]{2,1,0:T(8,128)(2,1)}), bf16[32,24,2304]{2,1,0:T(8,128)(2,1)S(1)}, u32[]{:S(2)}, u32[]{:S(2)}) async-start(bf16[32,24,2304]{2,1,0:T(8,128)(2,1)} %bitcast.21), calls=%async_computation.2 | async-start | bytes 7077888 | tf_op jit(solution)/shard_map/all_to_all | solution.py:753
  88.1 9.1 %conv_adjoint.1 = (bf16[768,768]{1,0:T(8,128)(2,1)}, f32[8,768]{1,0:T(8,128)S(1)}, f32[8,768]{1,0:T(8,128)S(1)}, f32[8,768]{1,0:T(8,128)S(1)}, f32[8,768]{1,0:T(8,128)S(1)}) custom-call(s32[1]{0:T(128)} %bitcast.par, bf16[768,768]{1,0:T(8,128)(2,1)} %get-tuple-element.45.pre, bf16[5,768,768]{2,1,0:T(8,128)(2,1)} %w.3, bf16[768,768]{1,0:T(8,128)(2,1)} %bitcast.23, ...), custom_call_target="tpu_custom_call" | custom-call | flops 4529848320 | bytes 9500000 | tf_op jit(solution)/shard_map/conv_adjoint/pallas_call | solution.py:577
  97.2 0.6 copy-done.3
  97.8 0.6 copy-done.5
  98.4 1.2 collective-permute-start.7
  99.6 4.0 %collective-permute-start.8 = (f32[8,768]{1,0:T(8,128)S(1)}, f32[8,768]{1,0:T(8,128)}, u32[]{:S(2)}, u32[]{:S(2)}) collective-permute-start(f32[8,768]{1,0:T(8,128)S(1)} %get-tuple-element.51), channel_id=1, source_target_pairs={{1,2},{2,1},{3,4},{4,3},{5,6},{6,5},{7,8},{8,7},{9,10},{10,9},{11,... | collective-permute-start | bytes 73736 | tf_op jit(solution)/shard_map/ppermute | solution.py:757
  103.6 12.7 %collective-permute-done.7.got1.after = f32[8,768]{1,0:T(8,128)S(1)} collective-permute-done((f32[8,768]{1,0:T(8,128)S(1)}, f32[8,768]{1,0:T(8,128)S(1)}, u32[]{:S(2)}, u32[]{:S(2)}) %collective-permute-start.7) | collective-permute-done | bytes 24608 | tf_op jit(solution)/shard_map/ppermute | solution.py:756
  116.2 0.6 copy-done.1
  116.8 19.0 %collective-permute-done.8.got2.after2 = f32[8,768]{1,0:T(8,128)} collective-permute-done((f32[8,768]{1,0:T(8,128)S(1)}, f32[8,768]{1,0:T(8,128)}, u32[]{:S(2)}, u32[]{:S(2)}) %collective-permute-start.8) | collective-permute-done | bytes 24608 | tf_op jit(solution)/shard_map/ppermute | solution.py:757
  135.8 2.1 %all-to-all-done.2.parts = bf16[32,24,2304]{2,1,0:T(8,128)(2,1)S(1)} async-done(((bf16[32,24,2304]{2,1,0:T(8,128)(2,1)}), bf16[32,24,2304]{2,1,0:T(8,128)(2,1)S(1)}, u32[]{:S(2)}, u32[]{:S(2)}) %all-to-all-start.2) | async-done | bytes 3538976 | tf_op jit(solution)/shard_map/all_to_all | solution.py:753
  137.9 1.1 sum_partials.1.a
  139.0 2.7 %collective-permute-start.13 = (bf16[24,4224]{1,0:T(8,128)(2,1)S(1)}, bf16[24,4224]{1,0:T(8,128)(2,1)S(1)}, u32[]{:S(2)}, u32[]{:S(2)}) collective-permute-start(bf16[24,4224]{1,0:T(8,128)(2,1)S(1)} %sum_partials.1.a), channel_id=1, source_target_pairs={{0,64},{64,0},{1,65},{65,1},{2,66},{66,2},{3,67},{67,3},{4,68},{68... | collective-permute-start | bytes 608264 | tf_op jit(solution)/shard_map/ppermute | solution.py:760
  141.7 1.4 add_edges.1.after
  143.1 2.8 %collective-permute-done.13.b = bf16[24,4224]{1,0:T(8,128)(2,1)S(1)} collective-permute-done((bf16[24,4224]{1,0:T(8,128)(2,1)S(1)}, bf16[24,4224]{1,0:T(8,128)(2,1)S(1)}, u32[]{:S(2)}, u32[]{:S(2)}) %collective-permute-start.13) | collective-permute-done | bytes 202784 | tf_op jit(solution)/shard_map/ppermute | solution.py:760
  145.9 0.1 add_pair.1.mine
  145.9 2.2 %collective-permute-start.14 = (f32[24,4224]{1,0:T(8,128)S(1)}, f32[24,4224]{1,0:T(8,128)S(1)}, u32[]{:S(2)}, u32[]{:S(2)}) collective-permute-start(f32[24,4224]{1,0:T(8,128)S(1)} %add_pair.1.mine), channel_id=1, source_target_pairs={{0,32},{32,0},{1,33},{33,1},{2,34},{34,2},{3,35},{35,3},{4,36},{36... | collective-permute-start | bytes 1216520 | tf_op jit(solution)/shard_map/ppermute | solution.py:763
  148.2 1.4 collective-permute-done.14.other
  149.5 1.3 place.1
  (19 shorter events, 0.0 us)
Async XLA Ops:
  2.7 12.2 %copy-start = (bf16[8,48,768]{2,1,0:T(8,128)(2,1)S(1)}, bf16[8,48,768]{2,1,0:T(8,128)(2,1)}, u32[]{:S(2)}) copy-start(bf16[8,48,768]{2,1,0:T(8,128)(2,1)} %pack_heads.1.after) | copy-start | bytes 1769476
  2.7 15.3 %all-to-all-start = ((bf16[8,48,768]{2,1,0:T(8,128)(2,1)}), bf16[8,48,768]{2,1,0:T(8,128)(2,1)S(1)}, u32[]{:S(2)}, u32[]{:S(2)}) async-start(bf16[8,48,768]{2,1,0:T(8,128)(2,1)} %pack_heads.1.after), calls=%async_computation | async-start | bytes 1179648 | tf_op jit(solution)/shard_map/all_to_all | solution.py:723
  8.8 10.8 %collective-permute-start.3 = (bf16[2,768]{1,0:T(2,128)(2,1)S(1)}, bf16[2,768]{1,0:T(2,128)(2,1)S(1)}, u32[]{:S(2)}, u32[]{:S(2)}) collective-permute-start(bf16[2,768]{1,0:T(2,128)(2,1)S(1)} %get-tuple-element.63), channel_id=1, source_target_pairs={{1,2},{2,1},{3,4},{4,3},{5,6},{6,5},{7,8},{8,7},{9,10},{10,9},{11,... | collective-permute-start | bytes 9224 | tf_op jit(solution)/shard_map/ppermute | solution.py:732
  14.8 4.8 %collective-permute-start.2 = (bf16[2,768]{1,0:T(2,128)(2,1)S(1)}, bf16[2,768]{1,0:T(2,128)(2,1)S(1)}, u32[]{:S(2)}, u32[]{:S(2)}) collective-permute-start(bf16[2,768]{1,0:T(2,128)(2,1)S(1)} %get-tuple-element.64), channel_id=1, source_target_pairs={{0,1},{1,0},{2,3},{3,2},{4,5},{5,4},{6,7},{7,6},{8,9},{9,8},{10,11... | collective-permute-start | bytes 9224 | tf_op jit(solution)/shard_map/ppermute | solution.py:731
  18.0 10.1 %collective-permute-start.1 = (bf16[384,384]{1,0:T(8,128)(2,1)S(1)}, bf16[384,384]{1,0:T(8,128)(2,1)S(1)}, u32[]{:S(2)}, u32[]{:S(2)}) collective-permute-start(bf16[384,384]{1,0:T(8,128)(2,1)S(1)} %get-tuple-element.34), channel_id=1, source_target_pairs={{0,3},{3,0},{1,2},{2,1},{4,7},{7,4},{5,6},{6,5},{8,11},{11,8},{9,1... | collective-permute-start | bytes 884744 | tf_op jit(solution)/shard_map/ppermute | solution.py:727
  19.2 9.0 %collective-permute-start = (bf16[384,384]{1,0:T(8,128)(2,1)S(1)}, bf16[384,384]{1,0:T(8,128)(2,1)S(1)}, u32[]{:S(2)}, u32[]{:S(2)}) collective-permute-start(bf16[384,384]{1,0:T(8,128)(2,1)S(1)} %get-tuple-element.33.after), channel_id=1, source_target_pairs={{0,1},{1,0},{2,3},{3,2},{4,5},{5,4},{6,7},{7,6},{8,9},{9,8},{10,11... | collective-permute-start | bytes 884744 | tf_op jit(solution)/shard_map/ppermute | solution.py:726
  29.4 2.8 %collective-permute-start.4 = (f32[8,768]{1,0:T(8,128)S(1)}, f32[8,768]{1,0:T(8,128)S(1)}, u32[]{:S(2)}, u32[]{:S(2)}) collective-permute-start(f32[8,768]{1,0:T(8,128)S(1)} %att_stats.1.st), channel_id=1, source_target_pairs={{0,1},{1,0},{2,3},{3,2},{4,5},{5,4},{6,7},{7,6},{8,9},{9,8},{10,11... | collective-permute-start | bytes 73736 | tf_op jit(solution)/shard_map/ppermute | solution.py:736
  35.4 6.8 %collective-permute-start.6 = (bf16[384,384]{1,0:T(8,128)(2,1)S(1)}, bf16[384,384]{1,0:T(8,128)(2,1)S(1)}, u32[]{:S(2)}, u32[]{:S(2)}) collective-permute-start(bf16[384,384]{1,0:T(8,128)(2,1)S(1)} %get-tuple-element.39), channel_id=1, source_target_pairs={{0,3},{3,0},{1,2},{2,1},{4,7},{7,4},{5,6},{6,5},{8,11},{11,8},{9,1... | collective-permute-start | bytes 884744 | tf_op jit(solution)/shard_map/ppermute | solution.py:739
  37.4 4.7 %collective-permute-start.5 = (bf16[192,384]{1,0:T(8,128)(2,1)S(1)}, bf16[192,384]{1,0:T(8,128)(2,1)S(1)}, u32[]{:S(2)}, u32[]{:S(2)}) collective-permute-start(bf16[192,384]{1,0:T(8,128)(2,1)S(1)} %get-tuple-element.38.after), channel_id=1, source_target_pairs={{0,1},{1,0},{2,3},{3,2},{4,5},{5,4},{6,7},{7,6},{8,9},{9,8},{10,11... | collective-permute-start | bytes 442376 | tf_op jit(solution)/shard_map/ppermute | solution.py:738
  64.8 8.2 %collective-permute-start.9 = (bf16[784,768]{1,0:T(8,128)(2,1)S(1)}, bf16[784,768]{1,0:T(8,128)(2,1)S(1)}, u32[]{:S(2)}, u32[]{:S(2)}) collective-permute-start(bf16[784,768]{1,0:T(8,128)(2,1)S(1)} %get-tuple-element.52.xp), channel_id=1, source_target_pairs={{0,32},{32,0},{1,33},{33,1},{2,34},{34,2},{3,35},{35,3},{4,36},{36... | collective-permute-start | bytes 3612680 | tf_op jit(solution)/shard_map/ppermute | solution.py:745
  69.1 5.5 %collective-permute-start.11 = (bf16[8,96,768]{2,1,0:T(8,128)(2,1)S(1)}, bf16[8,96,768]{2,1,0:T(8,128)(2,1)S(1)}, u32[]{:S(2)}, u32[]{:S(2)}) collective-permute-start(bf16[8,96,768]{2,1,0:T(8,128)(2,1)S(1)} %all_to_all.15.parts.p0), channel_id=1, source_target_pairs={{0,32},{32,0},{1,33},{33,1},{2,34},{34,2},{3,35},{35,3},{4,36},{36... | collective-permute-start | bytes 3538952 | tf_op jit(solution)/shard_map/ppermute | solution.py:744
  71.8 2.8 %collective-permute-start.10 = (bf16[768,384]{1,0:T(8,128)(2,1)S(1)}, bf16[768,384]{1,0:T(8,128)(2,1)S(1)}, u32[]{:S(2)}, u32[]{:S(2)}) collective-permute-start(bf16[768,384]{1,0:T(8,128)(2,1)S(1)} %get-tuple-element.58), channel_id=1, source_target_pairs={{0,32},{32,0},{1,33},{33,1},{2,34},{34,2},{3,35},{35,3},{4,36},{36... | collective-permute-start | bytes 1769480 | tf_op jit(solution)/shard_map/ppermute | solution.py:751
  72.3 2.2 %collective-permute-start.12 = (bf16[384,288]{1,0:T(8,128)(2,1)S(1)}, bf16[384,288]{1,0:T(8,128)(2,1)S(1)}, u32[]{:S(2)}, u32[]{:S(2)}) collective-permute-start(bf16[384,288]{1,0:T(8,128)(2,1)S(1)} %get-tuple-element.60), channel_id=1, source_target_pairs={{0,32},{32,0},{1,33},{33,1},{2,34},{34,2},{3,35},{35,3},{4,36},{36... | collective-permute-start | bytes 663560 | tf_op jit(solution)/shard_map/ppermute | solution.py:746
  82.4 55.5 %all-to-all-start.2 = ((bf16[32,24,2304]{2,1,0:T(8,128)(2,1)}), bf16[32,24,2304]{2,1,0:T(8,128)(2,1)S(1)}, u32[]{:S(2)}, u32[]{:S(2)}) async-start(bf16[32,24,2304]{2,1,0:T(8,128)(2,1)} %bitcast.21), calls=%async_computation.2 | async-start | bytes 7077888 | tf_op jit(solution)/shard_map/all_to_all | solution.py:753
  97.2 0.6 copy-start.3
  97.8 0.6 copy-start.5
  98.4 17.8 %collective-permute-start.7 = (f32[8,768]{1,0:T(8,128)S(1)}, f32[8,768]{1,0:T(8,128)S(1)}, u32[]{:S(2)}, u32[]{:S(2)}) collective-permute-start(f32[8,768]{1,0:T(8,128)S(1)} %get-tuple-element.50), channel_id=1, source_target_pairs={{0,1},{1,0},{2,3},{3,2},{4,5},{5,4},{6,7},{7,6},{8,9},{9,8},{10,11... | collective-permute-start | bytes 73736 | tf_op jit(solution)/shard_map/ppermute | solution.py:756
  99.6 36.2 %collective-permute-start.8 = (f32[8,768]{1,0:T(8,128)S(1)}, f32[8,768]{1,0:T(8,128)}, u32[]{:S(2)}, u32[]{:S(2)}) collective-permute-start(f32[8,768]{1,0:T(8,128)S(1)} %get-tuple-element.51), channel_id=1, source_target_pairs={{1,2},{2,1},{3,4},{4,3},{5,6},{6,5},{7,8},{8,7},{9,10},{10,9},{11,... | collective-permute-start | bytes 73736 | tf_op jit(solution)/shard_map/ppermute | solution.py:757
  116.2 0.6 copy-start.1
  137.9 3.8 %copy-start.2 = (f32[8,768]{1,0:T(8,128)S(1)}, f32[8,768]{1,0:T(8,128)}, u32[]{:S(2)}) copy-start(f32[8,768]{1,0:T(8,128)} %copy-done.1) | copy-start | bytes 73732
  137.9 3.8 %copy-start.4 = (f32[8,768]{1,0:T(8,128)S(1)}, f32[8,768]{1,0:T(8,128)}, u32[]{:S(2)}) copy-start(f32[8,768]{1,0:T(8,128)} %copy-done.3) | copy-start | bytes 73732
  137.9 3.8 %copy-start.6 = (f32[8,768]{1,0:T(8,128)S(1)}, f32[8,768]{1,0:T(8,128)}, u32[]{:S(2)}) copy-start(f32[8,768]{1,0:T(8,128)} %copy-done.5) | copy-start | bytes 73732
  139.0 6.9 %collective-permute-start.13 = (bf16[24,4224]{1,0:T(8,128)(2,1)S(1)}, bf16[24,4224]{1,0:T(8,128)(2,1)S(1)}, u32[]{:S(2)}, u32[]{:S(2)}) collective-permute-start(bf16[24,4224]{1,0:T(8,128)(2,1)S(1)} %sum_partials.1.a), channel_id=1, source_target_pairs={{0,64},{64,0},{1,65},{65,1},{2,66},{66,2},{3,67},{67,3},{4,68},{68... | collective-permute-start | bytes 608264 | tf_op jit(solution)/shard_map/ppermute | solution.py:760
  145.9 3.6 %collective-permute-start.14 = (f32[24,4224]{1,0:T(8,128)S(1)}, f32[24,4224]{1,0:T(8,128)S(1)}, u32[]{:S(2)}, u32[]{:S(2)}) collective-permute-start(f32[24,4224]{1,0:T(8,128)S(1)} %add_pair.1.mine), channel_id=1, source_target_pairs={{0,32},{32,0},{1,33},{33,1},{2,34},{34,2},{3,35},{35,3},{4,36},{36... | collective-permute-start | bytes 1216520 | tf_op jit(solution)/shard_map/ppermute | solution.py:763

commit v6 on v5

--- a/solution.py
+++ b/solution.py
@@ -254,15 +254,17 @@
             stores.append(pltpu.make_async_copy(made.at[rows], pool.at[h, pl.ds(0, ATT)], sems.at[h]))
             stores[-1].start()
 
+    send[:, QH:] = jnp.zeros((BLK, HALF - QH), BF)
+
     @pl.when(core[0] == 0)
     def _():
         keep[...] = qkv[:, 0:QH]
-        send[...] = qkv[:, QH : 2 * QH]
+        send[:, 0:QH] = qkv[:, QH : 2 * QH]
 
     @pl.when(core[0] != 0)
     def _():
         keep[...] = qkv[:, QH : 2 * QH]
-        send[...] = qkv[:, 0:QH]
+        send[:, 0:QH] = qkv[:, 0:QH]
 
     for copy in others + stores:
         copy.wait()
@@ -271,7 +273,7 @@
 def att_join(core, dq_own, dkv_own, dq_in, dkv_in, wh, pooled):
     return pl.pallas_call(
         join_kernel,
-        out_shape=(far((HEADS, 2 * ATT, C), BF), sds((BLK, QH), BF), sds((BLK, QH), BF)),
+        out_shape=(far((HEADS, 2 * ATT, C), BF), sds((BLK, QH), BF), far((BLK, HALF), BF)),
         in_specs=[SM] + [VM] * 6,
         out_specs=(pl.BlockSpec(memory_space=pltpu.HBM), VM, VM),
         scratch_shapes=[
@@ -400,7 +402,7 @@
 
 
 def slope_kernel(
-    core, parts, skip, slope, pre, send, keep, pool, skip_v, slope_v, pre_v, pool_v, in_sems, out_sems, pool_sem
+    core, parts, skip, slope, extra, pre, send, keep, pool, skip_v, slope_v, pre_v, pool_v, in_sems, out_sems, pool_sem, extra_sem
 ):
     chunks = range(0, ROWS, 256)
     loads = []
@@ -410,6 +412,8 @@
         loads.append(pltpu.make_async_copy(slope.at[rows], slope_v.at[rows], in_sems.at[1, r // 256]))
     for load in loads:
         load.start()
+    joined = pltpu.make_async_copy(extra, send.at[pl.ds(ROWS, BLK)], extra_sem)
+    joined.start()
     total = jnp.sum(parts[:, 0:ATT, :].astype(F32), axis=0) * (1.0 / FACTOR)
     pool_v[...] = total
     stores = [pltpu.make_async_copy(pool_v, pool, pool_sem)]
@@ -430,28 +434,29 @@
     @pl.when(core[0] == 0)
     def _():
         keep[...] = pre_v[:, 0:HALF]
-        send[...] = pre_v[:, HALF:]
+        send[0:ROWS, :] = pre_v[:, HALF:]
 
     @pl.when(core[0] != 0)
     def _():
         keep[...] = pre_v[:, HALF:]
-        send[...] = pre_v[:, 0:HALF]
-
+        send[0:ROWS, :] = pre_v[:, 0:HALF]
+
+    joined.wait()
     for store in stores:
         store.wait()
 
 
-def pre_grads(core, parts, skip, slope):
+def pre_grads(core, parts, skip, slope, extra):
     near = pl.BlockSpec(memory_space=pltpu.HBM)
     return pl.pallas_call(
         slope_kernel,
         out_shape=(
             far((ROWS, C), BF),
-            sds((ROWS, HALF), BF),
+            sds((ROWS + BLK, HALF), BF),
             sds((ROWS, HALF), BF),
             far((ATT, C), F32),
         ),
-        in_specs=[SM, VM, near, near],
+        in_specs=[SM, VM, near, near, near],
         out_specs=(near, VM, VM, near),
         scratch_shapes=[
             pltpu.VMEM((ROWS, C), BF),
@@ -461,14 +466,15 @@
             pltpu.SemaphoreType.DMA((2, 3)),
             pltpu.SemaphoreType.DMA((3,)),
             pltpu.SemaphoreType.DMA,
+            pltpu.SemaphoreType.DMA,
         ],
         name="pre_grads",
         compiler_params=params(12),
         cost_estimate=cost(5 * 768 * 768, 6000000),
-    )(core, parts, hbm(skip), hbm(slope))
-
-
-def weights_kernel(xt0, al0, xt1, al1, y0, y1, p0, p1, s0, s1, out, yf, wide, rest, made, sems):
+    )(core, parts, hbm(skip), hbm(slope), hbm(extra))
+
+
+def weights_kernel(xt0, al0, xt1, al1, y0, y1, p0, p1, s0, out, yf, wide, rest, made, sems):
     def copy(t):
         cols = pl.ds(t * HALF, HALF)
         return pltpu.make_async_copy(made.at[t], out.at[:, cols], sems.at[t])
@@ -477,11 +483,11 @@
         return jnp.concatenate([ref[h, ATT : 2 * ATT, :] for h in range(HEADS)], axis=0)
 
     part = jnp.concatenate([pooled(p0), pooled(p1)], axis=0)
-    made[TAPS, :, 0:QH] = tn(part, jnp.concatenate([s0[...], s1[...]], axis=0)).astype(BF)
+    made[TAPS, :, 0:QH] = tn(part, jnp.concatenate([s0[...], y1[ROWS:, 0:QH]], axis=0)).astype(BF)
     made[TAPS, :, QH:HALF] = jnp.zeros((C, HALF - QH), BF)
     copy(TAPS).start()
     for i, ref in enumerate((y0, y1)):
-        got = ref[...].astype(F32)
+        got = ref[0:ROWS, :].astype(F32)
         yf[i, 8 : 8 + ROWS, :] = got
         yf[i, 0:8, :] = got[ROWS - 8 :]
         yf[i, 8 + ROWS : 16 + ROWS, :] = got[0:8]
@@ -489,7 +495,7 @@
     for r in chunks:
         rows = slice(r, r + 256)
         left = jnp.concatenate([xt0[rows, :], xt1[rows, :]], axis=1)
-        made[2, rows, :] = mm(left, jnp.concatenate([y0[...], y1[...]], axis=0)).astype(BF)
+        made[2, rows, :] = mm(left, jnp.concatenate([y0[...], y1[0:ROWS, :]], axis=0)).astype(BF)
     copy(2).start()
     for g, taps in enumerate(((0, 1), (3, 4))):
         base, spot = (0, 2 * 256) if g == 0 else (256, 0)
@@ -519,11 +525,11 @@
         copy(t).wait()
 
 
-def weight_grads(xt0, al0, xt1, al1, y0, y1, p0, p1, s0, s1):
+def weight_grads(xt0, al0, xt1, al1, y0, y1, p0, p1, s0):
     return pl.pallas_call(
         weights_kernel,
         out_shape=far((C, 2304), BF),
-        in_specs=[VM] * 10,
+        in_specs=[VM] * 9,
         out_specs=pl.BlockSpec(memory_space=pltpu.HBM),
         scratch_shapes=[
             pltpu.VMEM((2, ROWS + 16, HALF), F32),
@@ -535,7 +541,7 @@
         name="weight_grads",
         compiler_params=params(32),
         cost_estimate=cost(2 * 5 * 768 * 1536 * 384, 10000000),
-    )(xt0, al0, xt1, al1, y0, y1, p0, p1, s0, s1)
+    )(xt0, al0, xt1, al1, y0, y1, p0, p1, s0)
 
 
 def adjoint_kernel(par, pre, w, skip, pool, out, near, far_, first, last, yf, acc):
@@ -743,13 +749,12 @@
     parts, xp = lax.optimization_barrier((parts, xp))
     parts_sib = lax.ppermute(parts, "core", SWAP)
     xp_sib = lax.ppermute(xp, "core", SWAP)
-    s1 = lax.ppermute(s_send, "core", SWAP)
     xt0, al0 = turn_input(xp)
     xt1, al1 = turn_input(xp_sib)
 
-    pre, y_send, y0, pool = pre_grads(core, parts, skip, slope)
+    pre, y_send, y0, pool = pre_grads(core, parts, skip, slope, s_send)
     y1 = lax.ppermute(y_send, "core", SWAP)
-    terms = weight_grads(xt0, al0, xt1, al1, y0, y1, parts, parts_sib, s0, s1)
+    terms = weight_grads(xt0, al0, xt1, al1, y0, y1, parts, parts_sib, s0)
     got = lax.all_to_all(terms.reshape(32, 24, 2304), SEQ, 0, 0, tiled=True)
 
     rows, near, next_, first, last = conv_adjoint(par, pre, conv_weight, skip, pool)

time: 151 us -> 152 us (level)
  transfers between devices with their start and end apart: 17 -> 16, of which waited for: 8 -> 8; matrix products, arithmetic and copies ran while one was open for 0% -> 0% of each run, Pallas kernels for 20% -> 20%
where the time goes in v6:
time: 152 us
  Pallas kernels  51.2 us (34%)
  waiting for transfers between devices  41 us (27%)
  starting transfers between devices  36.5 us (24%)
  blocking collectives  19.5 us (13%)
  local copies, waits for them, and re-layouts  1.83 us (1%)
    all_to_all x1, blocking collectives, local(): parts = lax.all_to_all(pool_part, HAX, 0, 0, tiled=True)  19.5 us
    ppermute x1, waiting for transfers between devices, local(): rim2 = lax.ppermute(next_, SEQ, NEXT)  19.1 us
    ppermute x1, waiting for transfers between devices, local(): rim1 = lax.ppermute(near, SEQ, NEAR)  12.6 us
    pallas_call x1, Pallas kernels, conv_adjoint(): pl.pallas_call(adjoint_kernel, grid=(TAPS,), out_shape=(far((ROWS, C), BF...  9.08 us
    pallas_call x1, Pallas kernels, conv_apply(): pl.pallas_call(conv_kernel, out_shape=(far((ROWS, C), F32), sds((ROWS + 1...  8.53 us
    pallas_call x1, Pallas kernels, weight_grads(): pl.pallas_call(weights_kernel, out_shape=far((C, 2304), BF), in_specs=[VM...  7.84 us
    ppermute x1, starting transfers between devices, local(): got2 = lax.ppermute(jnp.where(par[0] == 0, head_rows, tail_rows), SEQ, NEXT)  5.96 us
    all_to_all x1, starting transfers between devices, local(): got = lax.all_to_all(terms.reshape(32, 24, 2304), SEQ, 0, 0, tiled=True)  5.49 us
  transfers between devices with their start and end apart: 16, of which 8 were waited for; matrix products, arithmetic and copies ran while one was open for 0% of the time, Pallas kernels for 20%

profile of v6, /device:TPU:7, one launch (start us, length us, event | category | flops | bytes accessed | tf_op | source)
XLA Modules:
  0.0 151.7 jit_solution(18232295637303211729)
XLA Ops:
  0.6 2.1 %pack_heads.1.after = bf16[8,48,768]{2,1,0:T(8,128)(2,1)} custom-call(bf16[48,1536]{1,0:T(8,128)(2,1)} %bitcast.24, bf16[48,1536]{1,0:T(8,128)(2,1)} %bitcast.25, bf16[48,1536]{1,0:T(8,128)(2,1)} %bitcast.26, bf16[48,1536]{1,0:T(8,128)(2,1)} %bitcast.27), custom_call_target="tpu_custom_call" | custom-call | bytes 1200000 | tf_op jit(solution)/shard_map/pack_heads/pallas_call | solution.py:94
  2.7 0.0 copy-start
  2.7 5.4 %all-to-all-start = ((bf16[8,48,768]{2,1,0:T(8,128)(2,1)}), bf16[8,48,768]{2,1,0:T(8,128)(2,1)S(1)}, u32[]{:S(2)}, u32[]{:S(2)}) async-start(bf16[8,48,768]{2,1,0:T(8,128)(2,1)} %pack_heads.1.after), calls=%async_computation | async-start | bytes 1179648 | tf_op jit(solution)/shard_map/all_to_all | solution.py:729
  8.1 0.7 fusion.1
  8.8 6.0 %collective-permute-start.3 = (bf16[2,768]{1,0:T(2,128)(2,1)S(1)}, bf16[2,768]{1,0:T(2,128)(2,1)S(1)}, u32[]{:S(2)}, u32[]{:S(2)}) collective-permute-start(bf16[2,768]{1,0:T(2,128)(2,1)S(1)} %get-tuple-element.63), channel_id=1, source_target_pairs={{1,2},{2,1},{3,4},{4,3},{5,6},{6,5},{7,8},{8,7},{9,10},{10,9},{11,... | collective-permute-start | bytes 9224 | tf_op jit(solution)/shard_map/ppermute | solution.py:738
  14.8 0.1 collective-permute-start.2
  14.9 3.1 %head_weights.1.after.wh = bf16[576,768]{1,0:T(8,128)(2,1)} custom-call(s32[1]{0:T(128)} %bitcast.7.pair, s32[1]{0:T(128)} %bitcast.8.odd, bf16[768,4608]{1,0:T(8,128)(2,1)} %wv.1, bf16[768,4608]{1,0:T(8,128)(2,1)} %wv.1, bf16[768,4608]{1,0:T(8,128)(2,1)} %wv.1, bf16[8,48,768]{2,1,0:T(8,128)(2,1)S(1)} %copy-done), custom_call_target="tpu_custom_call" | custom-call | bytes 3000000 | tf_op jit(solution)/shard_map/head_weights/pallas_call | solution.py:224
  18.0 0.0 all-to-all-done
  18.0 0.1 split_own.1
  18.0 1.1 collective-permute-start.1
  19.2 0.5 collective-permute-start
  19.6 8.5 %conv_apply.1 = (f32[768,768]{1,0:T(8,128)}, bf16[784,768]{1,0:T(8,128)(2,1)S(1)}) custom-call(s32[1]{0:T(128)} %bitcast.par, bf16[768,768]{1,0:T(8,128)(2,1)} %bitcast.28, bf16[2,768]{1,0:T(2,128)(2,1)S(1)} %collective-permute-done.2.got1, bf16[2,768]{1,0:T(2,128)(2,1)S(1)} %collective-permute-done.3.got2, bf16[5,768,768]{2,1,0:T(8,128)(2,1)} %w.3, ...), custom_call_target="tpu_custom_call" | custom-call | flops 4529848320 | bytes 9500000 | tf_op jit(solution)/shard_map/conv_apply/pallas_call | solution.py:328
  28.2 1.2 att_stats.1.st
  29.4 1.1 collective-permute-start.4
  30.4 1.7 %collective-permute-done.4.st2 = f32[8,768]{1,0:T(8,128)S(1)} collective-permute-done((f32[8,768]{1,0:T(8,128)S(1)}, f32[8,768]{1,0:T(8,128)S(1)}, u32[]{:S(2)}, u32[]{:S(2)}) %collective-permute-start.4) | collective-permute-done | bytes 24608 | tf_op jit(solution)/shard_map/ppermute | solution.py:742
  32.1 3.3 %att_grads.1 = (f32[384,192]{1,0:T(8,128)}, bf16[192,384]{1,0:T(8,128)(2,1)S(1)}, f32[384,384]{1,0:T(8,128)}, bf16[384,384]{1,0:T(8,128)(2,1)S(1)}) custom-call(bf16[384,768]{1,0:T(8,128)(2,1)S(1)} %bitcast.19, bf16[384,384]{1,0:T(8,128)(2,1)S(1)} %collective-permute-done.qg, bf16[384,384]{1,0:T(8,128)(2,1)S(1)} %collective-permute-done.1.kv, ...), custom_call_target="tpu_custom_call" | custom-call | flops 20000000000 | bytes 3000000 | tf_op jit(solution)/shard_map/att_grads/pallas_call | solution.py:177
  35.4 2.0 %collective-permute-start.6 = (bf16[384,384]{1,0:T(8,128)(2,1)S(1)}, bf16[384,384]{1,0:T(8,128)(2,1)S(1)}, u32[]{:S(2)}, u32[]{:S(2)}) collective-permute-start(bf16[384,384]{1,0:T(8,128)(2,1)S(1)} %get-tuple-element.39), channel_id=1, source_target_pairs={{0,3},{3,0},{1,2},{2,1},{4,7},{7,4},{5,6},{6,5},{8,11},{11,8},{9,1... | collective-permute-start | bytes 884744 | tf_op jit(solution)/shard_map/ppermute | solution.py:745
  37.4 0.1 collective-permute-start.5
  37.4 4.7 %gelu_pool.1 = (bf16[768,768]{1,0:T(8,128)(2,1)}, bf16[48,768]{1,0:T(8,128)(2,1)}) custom-call(f32[768,768]{1,0:T(8,128)} %get-tuple-element.35.after.pre, bf16[768,768]{1,0:T(8,128)(2,1)} %bitcast.29, bf16[192,384]{1,0:T(8,128)(2,1)S(1)} %get-tuple-element.38.after), custom_call_target="tpu_custom_call" | custom-call | flops 3000000000 | bytes 5000000 | tf_op jit(solution)/shard_map/gelu_pool/pallas_call | solution.py:360
  42.1 0.1 collective-permute-done.6.dkv_in
  42.2 3.8 %att_join.1 = (bf16[8,96,768]{2,1,0:T(8,128)(2,1)}, bf16[384,288]{1,0:T(8,128)(2,1)S(1)}, bf16[384,384]{1,0:T(8,128)(2,1)}) custom-call(s32[1]{0:T(128)} %bitcast.1.core, f32[384,192]{1,0:T(8,128)} %get-tuple-element.36.dq_own, f32[384,384]{1,0:T(8,128)} %get-tuple-element.37.dkv_own, bf16[192,384]{1,0:T(8,128)(2,1)S(1)} %collective-permute-done.5.dq_in, ...), custom_call_target="tpu_custom_call" | custom-call | flops 10000000000 | bytes 3500000 | tf_op jit(solution)/shard_map/att_join/pallas_call | solution.py:274
  46.0 19.5 %all_to_all.15.parts.p0 = bf16[8,96,768]{2,1,0:T(8,128)(2,1)S(1)} all-to-all(bf16[8,96,768]{2,1,0:T(8,128)(2,1)} %get-tuple-element.41), channel_id=1, replica_groups=mesh['yh'=2,'core'=2,'yl'=2,'x'=4,'z'=4] {'yl','x'}, dimensions={0} | all-to-all | bytes 2359296 | tf_op jit(solution)/shard_map/all_to_all | solution.py:748
  65.5 4.3 %collective-permute-start.9 = (bf16[784,768]{1,0:T(8,128)(2,1)S(1)}, bf16[784,768]{1,0:T(8,128)(2,1)S(1)}, u32[]{:S(2)}, u32[]{:S(2)}) collective-permute-start(bf16[784,768]{1,0:T(8,128)(2,1)S(1)} %get-tuple-element.53.xp), channel_id=1, source_target_pairs={{0,32},{32,0},{1,33},{33,1},{2,34},{34,2},{3,35},{35,3},{4,36},{36... | collective-permute-start | bytes 3612680 | tf_op jit(solution)/shard_map/ppermute | solution.py:751
  69.8 0.0 collective-permute-start.11
  69.8 2.6 %pre_grads.1 = (bf16[768,768]{1,0:T(8,128)(2,1)}, bf16[1152,384]{1,0:T(8,128)(2,1)S(1)}, bf16[768,384]{1,0:T(8,128)(2,1)S(1)}, f32[48,768]{1,0:T(8,128)}) custom-call(s32[1]{0:T(128)} %bitcast.1.core, bf16[8,96,768]{2,1,0:T(8,128)(2,1)S(1)} %all_to_all.15.parts.p0, bf16[768,768]{1,0:T(8,128)(2,1)} %bitcast.22, bf16[768,768]{1,0:T(8,128)(2,1)} %get-tuple-element.44.slope, ...), custom_call_target="tpu_custom_call" | custom-call | flops 2949120 | bytes 6000000 | tf_op jit(solution)/shard_map/pre_grads/pallas_call | solution.py:451
  72.5 0.6 collective-permute-start.10
  73.0 0.6 turn_input.2
  73.6 0.6 turn_input.3
  74.2 1.0 collective-permute-done.10.y1
  75.3 7.8 %weight_grads.1 = bf16[768,2304]{1,0:T(8,128)(2,1)} custom-call(bf16[768,768]{1,0:T(8,128)(2,1)S(1)} %get-tuple-element.54.xt0, bf16[768,512]{1,0:T(8,128)(2,1)S(1)} %get-tuple-element.55.al0, bf16[768,768]{1,0:T(8,128)(2,1)S(1)} %get-tuple-element.56.xt1, bf16[768,512]{1,0:T(8,128)(2,1)S(1)} %get-tuple-element.57.al1, ...), custom_call_target="tpu_custom_call" | custom-call | flops 4529848320 | bytes 10000000 | tf_op jit(solution)/shard_map/weight_grads/pallas_call | solution.py:529
  83.1 5.5 %all-to-all-start.2 = ((bf16[32,24,2304]{2,1,0:T(8,128)(2,1)}), bf16[32,24,2304]{2,1,0:T(8,128)(2,1)S(1)}, u32[]{:S(2)}, u32[]{:S(2)}) async-start(bf16[32,24,2304]{2,1,0:T(8,128)(2,1)} %bitcast.21), calls=%async_computation.2 | async-start | bytes 7077888 | tf_op jit(solution)/shard_map/all_to_all | solution.py:758
  88.6 9.1 %conv_adjoint.1 = (bf16[768,768]{1,0:T(8,128)(2,1)}, f32[8,768]{1,0:T(8,128)S(1)}, f32[8,768]{1,0:T(8,128)S(1)}, f32[8,768]{1,0:T(8,128)S(1)}, f32[8,768]{1,0:T(8,128)S(1)}) custom-call(s32[1]{0:T(128)} %bitcast.par, bf16[768,768]{1,0:T(8,128)(2,1)} %get-tuple-element.46.pre, bf16[5,768,768]{2,1,0:T(8,128)(2,1)} %w.3, bf16[768,768]{1,0:T(8,128)(2,1)} %bitcast.23, ...), custom_call_target="tpu_custom_call" | custom-call | flops 4529848320 | bytes 9500000 | tf_op jit(solution)/shard_map/conv_adjoint/pallas_call | solution.py:583
  97.7 0.6 copy-done.3
  98.3 0.6 copy-done.5
  98.9 1.2 collective-permute-start.7
  100.1 3.9 %collective-permute-start.8 = (f32[8,768]{1,0:T(8,128)S(1)}, f32[8,768]{1,0:T(8,128)}, u32[]{:S(2)}, u32[]{:S(2)}) collective-permute-start(f32[8,768]{1,0:T(8,128)S(1)} %get-tuple-element.52), channel_id=1, source_target_pairs={{1,2},{2,1},{3,4},{4,3},{5,6},{6,5},{7,8},{8,7},{9,10},{10,9},{11,... | collective-permute-start | bytes 73736 | tf_op jit(solution)/shard_map/ppermute | solution.py:762
  104.1 12.6 %collective-permute-done.7.got1.after = f32[8,768]{1,0:T(8,128)S(1)} collective-permute-done((f32[8,768]{1,0:T(8,128)S(1)}, f32[8,768]{1,0:T(8,128)S(1)}, u32[]{:S(2)}, u32[]{:S(2)}) %collective-permute-start.7) | collective-permute-done | bytes 24608 | tf_op jit(solution)/shard_map/ppermute | solution.py:761
  116.7 0.6 copy-done.1
  117.3 19.1 %collective-permute-done.8.got2.after2 = f32[8,768]{1,0:T(8,128)} collective-permute-done((f32[8,768]{1,0:T(8,128)S(1)}, f32[8,768]{1,0:T(8,128)}, u32[]{:S(2)}, u32[]{:S(2)}) %collective-permute-start.8) | collective-permute-done | bytes 24608 | tf_op jit(solution)/shard_map/ppermute | solution.py:762
  136.4 2.4 %all-to-all-done.2.parts = bf16[32,24,2304]{2,1,0:T(8,128)(2,1)S(1)} async-done(((bf16[32,24,2304]{2,1,0:T(8,128)(2,1)}), bf16[32,24,2304]{2,1,0:T(8,128)(2,1)S(1)}, u32[]{:S(2)}, u32[]{:S(2)}) %all-to-all-start.2) | async-done | bytes 3538976 | tf_op jit(solution)/shard_map/all_to_all | solution.py:758
  138.8 1.1 sum_partials.1.a
  139.8 2.7 %collective-permute-start.12 = (bf16[24,4224]{1,0:T(8,128)(2,1)S(1)}, bf16[24,4224]{1,0:T(8,128)(2,1)S(1)}, u32[]{:S(2)}, u32[]{:S(2)}) collective-permute-start(bf16[24,4224]{1,0:T(8,128)(2,1)S(1)} %sum_partials.1.a), channel_id=1, source_target_pairs={{0,64},{64,0},{1,65},{65,1},{2,66},{66,2},{3,67},{67,3},{4,68},{68... | collective-permute-start | bytes 608264 | tf_op jit(solution)/shard_map/ppermute | solution.py:765
  142.5 1.4 add_edges.1.after
  144.0 2.8 %collective-permute-done.12.b = bf16[24,4224]{1,0:T(8,128)(2,1)S(1)} collective-permute-done((bf16[24,4224]{1,0:T(8,128)(2,1)S(1)}, bf16[24,4224]{1,0:T(8,128)(2,1)S(1)}, u32[]{:S(2)}, u32[]{:S(2)}) %collective-permute-start.12) | collective-permute-done | bytes 202784 | tf_op jit(solution)/shard_map/ppermute | solution.py:765
  146.8 0.1 add_pair.1.mine
  146.8 2.2 %collective-permute-start.13 = (f32[24,4224]{1,0:T(8,128)S(1)}, f32[24,4224]{1,0:T(8,128)S(1)}, u32[]{:S(2)}, u32[]{:S(2)}) collective-permute-start(f32[24,4224]{1,0:T(8,128)S(1)} %add_pair.1.mine), channel_id=1, source_target_pairs={{0,32},{32,0},{1,33},{33,1},{2,34},{34,2},{3,35},{35,3},{4,36},{36... | collective-permute-start | bytes 1216520 | tf_op jit(solution)/shard_map/ppermute | solution.py:768
  149.0 1.4 collective-permute-done.13.other
  150.4 1.3 place.1
  (17 shorter events, 0.0 us)
Async XLA Ops:
  2.7 12.2 %copy-start = (bf16[8,48,768]{2,1,0:T(8,128)(2,1)S(1)}, bf16[8,48,768]{2,1,0:T(8,128)(2,1)}, u32[]{:S(2)}) copy-start(bf16[8,48,768]{2,1,0:T(8,128)(2,1)} %pack_heads.1.after) | copy-start | bytes 1769476
  2.7 15.3 %all-to-all-start = ((bf16[8,48,768]{2,1,0:T(8,128)(2,1)}), bf16[8,48,768]{2,1,0:T(8,128)(2,1)S(1)}, u32[]{:S(2)}, u32[]{:S(2)}) async-start(bf16[8,48,768]{2,1,0:T(8,128)(2,1)} %pack_heads.1.after), calls=%async_computation | async-start | bytes 1179648 | tf_op jit(solution)/shard_map/all_to_all | solution.py:729
  8.8 10.8 %collective-permute-start.3 = (bf16[2,768]{1,0:T(2,128)(2,1)S(1)}, bf16[2,768]{1,0:T(2,128)(2,1)S(1)}, u32[]{:S(2)}, u32[]{:S(2)}) collective-permute-start(bf16[2,768]{1,0:T(2,128)(2,1)S(1)} %get-tuple-element.63), channel_id=1, source_target_pairs={{1,2},{2,1},{3,4},{4,3},{5,6},{6,5},{7,8},{8,7},{9,10},{10,9},{11,... | collective-permute-start | bytes 9224 | tf_op jit(solution)/shard_map/ppermute | solution.py:738
  14.8 4.8 %collective-permute-start.2 = (bf16[2,768]{1,0:T(2,128)(2,1)S(1)}, bf16[2,768]{1,0:T(2,128)(2,1)S(1)}, u32[]{:S(2)}, u32[]{:S(2)}) collective-permute-start(bf16[2,768]{1,0:T(2,128)(2,1)S(1)} %get-tuple-element.64), channel_id=1, source_target_pairs={{0,1},{1,0},{2,3},{3,2},{4,5},{5,4},{6,7},{7,6},{8,9},{9,8},{10,11... | collective-permute-start | bytes 9224 | tf_op jit(solution)/shard_map/ppermute | solution.py:737
  18.0 10.1 %collective-permute-start.1 = (bf16[384,384]{1,0:T(8,128)(2,1)S(1)}, bf16[384,384]{1,0:T(8,128)(2,1)S(1)}, u32[]{:S(2)}, u32[]{:S(2)}) collective-permute-start(bf16[384,384]{1,0:T(8,128)(2,1)S(1)} %get-tuple-element.34), channel_id=1, source_target_pairs={{0,3},{3,0},{1,2},{2,1},{4,7},{7,4},{5,6},{6,5},{8,11},{11,8},{9,1... | collective-permute-start | bytes 884744 | tf_op jit(solution)/shard_map/ppermute | solution.py:733
  19.2 9.0 %collective-permute-start = (bf16[384,384]{1,0:T(8,128)(2,1)S(1)}, bf16[384,384]{1,0:T(8,128)(2,1)S(1)}, u32[]{:S(2)}, u32[]{:S(2)}) collective-permute-start(bf16[384,384]{1,0:T(8,128)(2,1)S(1)} %get-tuple-element.33.after), channel_id=1, source_target_pairs={{0,1},{1,0},{2,3},{3,2},{4,5},{5,4},{6,7},{7,6},{8,9},{9,8},{10,11... | collective-permute-start | bytes 884744 | tf_op jit(solution)/shard_map/ppermute | solution.py:732
  29.4 2.8 %collective-permute-start.4 = (f32[8,768]{1,0:T(8,128)S(1)}, f32[8,768]{1,0:T(8,128)S(1)}, u32[]{:S(2)}, u32[]{:S(2)}) collective-permute-start(f32[8,768]{1,0:T(8,128)S(1)} %att_stats.1.st), channel_id=1, source_target_pairs={{0,1},{1,0},{2,3},{3,2},{4,5},{5,4},{6,7},{7,6},{8,9},{9,8},{10,11... | collective-permute-start | bytes 73736 | tf_op jit(solution)/shard_map/ppermute | solution.py:742
  35.4 6.8 %collective-permute-start.6 = (bf16[384,384]{1,0:T(8,128)(2,1)S(1)}, bf16[384,384]{1,0:T(8,128)(2,1)S(1)}, u32[]{:S(2)}, u32[]{:S(2)}) collective-permute-start(bf16[384,384]{1,0:T(8,128)(2,1)S(1)} %get-tuple-element.39), channel_id=1, source_target_pairs={{0,3},{3,0},{1,2},{2,1},{4,7},{7,4},{5,6},{6,5},{8,11},{11,8},{9,1... | collective-permute-start | bytes 884744 | tf_op jit(solution)/shard_map/ppermute | solution.py:745
  37.4 4.7 %collective-permute-start.5 = (bf16[192,384]{1,0:T(8,128)(2,1)S(1)}, bf16[192,384]{1,0:T(8,128)(2,1)S(1)}, u32[]{:S(2)}, u32[]{:S(2)}) collective-permute-start(bf16[192,384]{1,0:T(8,128)(2,1)S(1)} %get-tuple-element.38.after), channel_id=1, source_target_pairs={{0,1},{1,0},{2,3},{3,2},{4,5},{5,4},{6,7},{7,6},{8,9},{9,8},{10,11... | collective-permute-start | bytes 442376 | tf_op jit(solution)/shard_map/ppermute | solution.py:744
  65.5 8.1 %collective-permute-start.9 = (bf16[784,768]{1,0:T(8,128)(2,1)S(1)}, bf16[784,768]{1,0:T(8,128)(2,1)S(1)}, u32[]{:S(2)}, u32[]{:S(2)}) collective-permute-start(bf16[784,768]{1,0:T(8,128)(2,1)S(1)} %get-tuple-element.53.xp), channel_id=1, source_target_pairs={{0,32},{32,0},{1,33},{33,1},{2,34},{34,2},{3,35},{35,3},{4,36},{36... | collective-permute-start | bytes 3612680 | tf_op jit(solution)/shard_map/ppermute | solution.py:751
  69.8 5.5 %collective-permute-start.11 = (bf16[8,96,768]{2,1,0:T(8,128)(2,1)S(1)}, bf16[8,96,768]{2,1,0:T(8,128)(2,1)S(1)}, u32[]{:S(2)}, u32[]{:S(2)}) collective-permute-start(bf16[8,96,768]{2,1,0:T(8,128)(2,1)S(1)} %all_to_all.15.parts.p0), channel_id=1, source_target_pairs={{0,32},{32,0},{1,33},{33,1},{2,34},{34,2},{3,35},{35,3},{4,36},{36... | collective-permute-start | bytes 3538952 | tf_op jit(solution)/shard_map/ppermute | solution.py:750
  72.5 2.8 %collective-permute-start.10 = (bf16[1152,384]{1,0:T(8,128)(2,1)S(1)}, bf16[1152,384]{1,0:T(8,128)(2,1)S(1)}, u32[]{:S(2)}, u32[]{:S(2)}) collective-permute-start(bf16[1152,384]{1,0:T(8,128)(2,1)S(1)} %get-tuple-element.59), channel_id=1, source_target_pairs={{0,32},{32,0},{1,33},{33,1},{2,34},{34,2},{3,35},{35,3},{4,36},{36... | collective-permute-start | bytes 2654216 | tf_op jit(solution)/shard_map/ppermute | solution.py:756
  83.1 55.6 %all-to-all-start.2 = ((bf16[32,24,2304]{2,1,0:T(8,128)(2,1)}), bf16[32,24,2304]{2,1,0:T(8,128)(2,1)S(1)}, u32[]{:S(2)}, u32[]{:S(2)}) async-start(bf16[32,24,2304]{2,1,0:T(8,128)(2,1)} %bitcast.21), calls=%async_computation.2 | async-start | bytes 7077888 | tf_op jit(solution)/shard_map/all_to_all | solution.py:758
  97.7 0.6 copy-start.3
  98.3 0.6 copy-start.5
  98.9 17.8 %collective-permute-start.7 = (f32[8,768]{1,0:T(8,128)S(1)}, f32[8,768]{1,0:T(8,128)S(1)}, u32[]{:S(2)}, u32[]{:S(2)}) collective-permute-start(f32[8,768]{1,0:T(8,128)S(1)} %get-tuple-element.51), channel_id=1, source_target_pairs={{0,1},{1,0},{2,3},{3,2},{4,5},{5,4},{6,7},{7,6},{8,9},{9,8},{10,11... | collective-permute-start | bytes 73736 | tf_op jit(solution)/shard_map/ppermute | solution.py:761
  100.1 36.3 %collective-permute-start.8 = (f32[8,768]{1,0:T(8,128)S(1)}, f32[8,768]{1,0:T(8,128)}, u32[]{:S(2)}, u32[]{:S(2)}) collective-permute-start(f32[8,768]{1,0:T(8,128)S(1)} %get-tuple-element.52), channel_id=1, source_target_pairs={{1,2},{2,1},{3,4},{4,3},{5,6},{6,5},{7,8},{8,7},{9,10},{10,9},{11,... | collective-permute-start | bytes 73736 | tf_op jit(solution)/shard_map/ppermute | solution.py:762
  116.7 0.6 copy-start.1
  138.8 3.8 %copy-start.2 = (f32[8,768]{1,0:T(8,128)S(1)}, f32[8,768]{1,0:T(8,128)}, u32[]{:S(2)}) copy-start(f32[8,768]{1,0:T(8,128)} %copy-done.1) | copy-start | bytes 73732
  138.8 3.8 %copy-start.4 = (f32[8,768]{1,0:T(8,128)S(1)}, f32[8,768]{1,0:T(8,128)}, u32[]{:S(2)}) copy-start(f32[8,768]{1,0:T(8,128)} %copy-done.3) | copy-start | bytes 73732
  138.8 3.8 %copy-start.6 = (f32[8,768]{1,0:T(8,128)S(1)}, f32[8,768]{1,0:T(8,128)}, u32[]{:S(2)}) copy-start(f32[8,768]{1,0:T(8,128)} %copy-done.5) | copy-start | bytes 73732
  139.8 6.9 %collective-permute-start.12 = (bf16[24,4224]{1,0:T(8,128)(2,1)S(1)}, bf16[24,4224]{1,0:T(8,128)(2,1)S(1)}, u32[]{:S(2)}, u32[]{:S(2)}) collective-permute-start(bf16[24,4224]{1,0:T(8,128)(2,1)S(1)} %sum_partials.1.a), channel_id=1, source_target_pairs={{0,64},{64,0},{1,65},{65,1},{2,66},{66,2},{3,67},{67,3},{4,68},{68... | collective-permute-start | bytes 608264 | tf_op jit(solution)/shard_map/ppermute | solution.py:765
  146.8 3.6 %collective-permute-start.13 = (f32[24,4224]{1,0:T(8,128)S(1)}, f32[24,4224]{1,0:T(8,128)S(1)}, u32[]{:S(2)}, u32[]{:S(2)}) collective-permute-start(f32[24,4224]{1,0:T(8,128)S(1)} %add_pair.1.mine), channel_id=1, source_target_pairs={{0,32},{32,0},{1,33},{33,1},{2,34},{34,2},{3,35},{35,3},{4,36},{36... | collective-permute-start | bytes 1216520 | tf_op jit(solution)/shard_map/ppermute | solution.py:768

commit v7 on v5

--- a/solution.py
+++ b/solution.py
@@ -162,13 +162,13 @@
         dk = dk + mm(sgrad, query[rows])
         dv = dv + mm(probs.astype(BF), grads[rows])
         if i == 0:
-            dq_own[...] = dq
+            dq_own[...] = dq.astype(BF)
         else:
             dq_send[:, 0:HD] = dq[0 : BLK // 2].astype(BF)
             dq_send[:, HD : 2 * HD] = dq[BLK // 2 : BLK].astype(BF)
     dk = dk * SCALE
-    dkv_own[:, 0:HD] = dk[0:BLK]
-    dkv_own[:, HD : 2 * HD] = dv[0:BLK]
+    dkv_own[:, 0:HD] = dk[0:BLK].astype(BF)
+    dkv_own[:, HD : 2 * HD] = dv[0:BLK].astype(BF)
     dkv_send[:, 0:HD] = dk[BLK:].astype(BF)
     dkv_send[:, HD : 2 * HD] = dv[BLK:].astype(BF)
 
@@ -177,9 +177,9 @@
     return pl.pallas_call(
         grads_kernel,
         out_shape=(
-            far((BLK, HD), F32),
+            far((BLK, HD), BF),
             sds((BLK // 2, 2 * HD), BF),
-            far((BLK, 2 * HD), F32),
+            far((BLK, 2 * HD), BF),
             sds((BLK, 2 * HD), BF),
         ),
         in_specs=[VM] * 5 + [ANY],
@@ -243,8 +243,8 @@
     for other in others:
         other.start()
     dq_got = jnp.concatenate([dq_in[:, 0:HD], dq_in[:, HD : 2 * HD]], axis=0).astype(F32)
-    dq = (dq_own[...] + dq_got).astype(BF)
-    dkv = (dkv_own[...] + dkv_in[...].astype(F32)).astype(BF)
+    dq = (dq_own[...].astype(F32) + dq_got).astype(BF)
+    dkv = (dkv_own[...].astype(F32) + dkv_in[...].astype(F32)).astype(BF)
     qkv = jnp.concatenate([dq, dkv], axis=1)
     stores = []
     for r in range(0, BLK, 2 * ATT):

time: 151 us -> 151 us (level)
  no operation moved by 1% of the time
where the time goes in v7:
time: 151 us
  Pallas kernels  50.2 us (33%)
  waiting for transfers between devices  40.6 us (27%)
  starting transfers between devices  36.8 us (24%)
  blocking collectives  19.5 us (13%)
  local copies, waits for them, and re-layouts  1.84 us (1%)
    all_to_all x1, blocking collectives, local(): parts = lax.all_to_all(pool_part, HAX, 0, 0, tiled=True)  19.5 us
    ppermute x1, waiting for transfers between devices, local(): rim2 = lax.ppermute(next_, SEQ, NEXT)  19 us
    ppermute x1, waiting for transfers between devices, local(): rim1 = lax.ppermute(near, SEQ, NEAR)  12.7 us
    pallas_call x1, Pallas kernels, conv_adjoint(): pl.pallas_call(adjoint_kernel, grid=(TAPS,), out_shape=(far((ROWS, C), BF...  9.08 us
    pallas_call x1, Pallas kernels, conv_apply(): pl.pallas_call(conv_kernel, out_shape=(far((ROWS, C), F32), sds((ROWS + 1...  8.53 us
    pallas_call x1, Pallas kernels, weight_grads(): pl.pallas_call(weights_kernel, out_shape=far((C, 2304), BF), in_specs=[VM...  7.82 us
    ppermute x1, starting transfers between devices, local(): got2 = lax.ppermute(jnp.where(par[0] == 0, head_rows, tail_rows), SEQ, NEXT)  5.96 us
    all_to_all x1, starting transfers between devices, local(): got = lax.all_to_all(terms.reshape(32, 24, 2304), SEQ, 0, 0, tiled=True)  5.7 us
  transfers between devices with their start and end apart: 17, of which 8 were waited for; matrix products, arithmetic and copies ran while one was open for 0% of the time, Pallas kernels for 20%

profile of v7, /device:TPU:7, one launch (start us, length us, event | category | flops | bytes accessed | tf_op | source)
XLA Modules:
  0.0 150.5 jit_solution(14099652633452323456)
XLA Ops:
  0.6 2.1 %pack_heads.1.after = bf16[8,48,768]{2,1,0:T(8,128)(2,1)} custom-call(bf16[48,1536]{1,0:T(8,128)(2,1)} %bitcast.24, bf16[48,1536]{1,0:T(8,128)(2,1)} %bitcast.25, bf16[48,1536]{1,0:T(8,128)(2,1)} %bitcast.26, bf16[48,1536]{1,0:T(8,128)(2,1)} %bitcast.27), custom_call_target="tpu_custom_call" | custom-call | bytes 1200000 | tf_op jit(solution)/shard_map/pack_heads/pallas_call | solution.py:94
  2.7 0.0 copy-start
  2.7 5.4 %all-to-all-start = ((bf16[8,48,768]{2,1,0:T(8,128)(2,1)}), bf16[8,48,768]{2,1,0:T(8,128)(2,1)S(1)}, u32[]{:S(2)}, u32[]{:S(2)}) async-start(bf16[8,48,768]{2,1,0:T(8,128)(2,1)} %pack_heads.1.after), calls=%async_computation | async-start | bytes 1179648 | tf_op jit(solution)/shard_map/all_to_all | solution.py:723
  8.1 0.7 fusion.1
  8.8 6.0 %collective-permute-start.3 = (bf16[2,768]{1,0:T(2,128)(2,1)S(1)}, bf16[2,768]{1,0:T(2,128)(2,1)S(1)}, u32[]{:S(2)}, u32[]{:S(2)}) collective-permute-start(bf16[2,768]{1,0:T(2,128)(2,1)S(1)} %get-tuple-element.63), channel_id=1, source_target_pairs={{1,2},{2,1},{3,4},{4,3},{5,6},{6,5},{7,8},{8,7},{9,10},{10,9},{11,... | collective-permute-start | bytes 9224 | tf_op jit(solution)/shard_map/ppermute | solution.py:732
  14.8 0.1 collective-permute-start.2
  14.9 3.1 %head_weights.1.after.wh = bf16[576,768]{1,0:T(8,128)(2,1)} custom-call(s32[1]{0:T(128)} %bitcast.7.pair, s32[1]{0:T(128)} %bitcast.8.odd, bf16[768,4608]{1,0:T(8,128)(2,1)} %wv.1, bf16[768,4608]{1,0:T(8,128)(2,1)} %wv.1, bf16[768,4608]{1,0:T(8,128)(2,1)} %wv.1, bf16[8,48,768]{2,1,0:T(8,128)(2,1)S(1)} %copy-done), custom_call_target="tpu_custom_call" | custom-call | bytes 3000000 | tf_op jit(solution)/shard_map/head_weights/pallas_call | solution.py:224
  18.0 0.1 split_own.1
  18.0 1.1 collective-permute-start.1
  19.2 0.5 collective-permute-start
  19.6 8.5 %conv_apply.1 = (f32[768,768]{1,0:T(8,128)}, bf16[784,768]{1,0:T(8,128)(2,1)S(1)}) custom-call(s32[1]{0:T(128)} %bitcast.par, bf16[768,768]{1,0:T(8,128)(2,1)} %bitcast.28, bf16[2,768]{1,0:T(2,128)(2,1)S(1)} %collective-permute-done.2.got1, bf16[2,768]{1,0:T(2,128)(2,1)S(1)} %collective-permute-done.3.got2, bf16[5,768,768]{2,1,0:T(8,128)(2,1)} %w.3, ...), custom_call_target="tpu_custom_call" | custom-call | flops 4529848320 | bytes 9500000 | tf_op jit(solution)/shard_map/conv_apply/pallas_call | solution.py:326
  28.2 1.2 att_stats.1.st
  29.4 1.1 collective-permute-start.4
  30.4 1.7 %collective-permute-done.4.st2 = f32[8,768]{1,0:T(8,128)S(1)} collective-permute-done((f32[8,768]{1,0:T(8,128)S(1)}, f32[8,768]{1,0:T(8,128)S(1)}, u32[]{:S(2)}, u32[]{:S(2)}) %collective-permute-start.4) | collective-permute-done | bytes 24608 | tf_op jit(solution)/shard_map/ppermute | solution.py:736
  32.1 3.1 %att_grads.1 = (bf16[384,192]{1,0:T(8,128)(2,1)}, bf16[192,384]{1,0:T(8,128)(2,1)S(1)}, bf16[384,384]{1,0:T(8,128)(2,1)}, bf16[384,384]{1,0:T(8,128)(2,1)S(1)}) custom-call(bf16[384,768]{1,0:T(8,128)(2,1)S(1)} %bitcast.19, bf16[384,384]{1,0:T(8,128)(2,1)S(1)} %collective-permute-done.qg, bf16[384,384]{1,0:T(8,128)(2,1)S(1)} %collective-permute-done.1.kv, ...), custom_call_target="tpu_custom_call" | custom-call | flops 20000000000 | bytes 3000000 | tf_op jit(solution)/shard_map/att_grads/pallas_call | solution.py:177
  35.3 2.0 %collective-permute-start.6 = (bf16[384,384]{1,0:T(8,128)(2,1)S(1)}, bf16[384,384]{1,0:T(8,128)(2,1)S(1)}, u32[]{:S(2)}, u32[]{:S(2)}) collective-permute-start(bf16[384,384]{1,0:T(8,128)(2,1)S(1)} %get-tuple-element.39), channel_id=1, source_target_pairs={{0,3},{3,0},{1,2},{2,1},{4,7},{7,4},{5,6},{6,5},{8,11},{11,8},{9,1... | collective-permute-start | bytes 884744 | tf_op jit(solution)/shard_map/ppermute | solution.py:739
  37.2 0.0 collective-permute-start.5
  37.3 4.7 %gelu_pool.1 = (bf16[768,768]{1,0:T(8,128)(2,1)}, bf16[48,768]{1,0:T(8,128)(2,1)}) custom-call(f32[768,768]{1,0:T(8,128)} %get-tuple-element.35.after.pre, bf16[768,768]{1,0:T(8,128)(2,1)} %bitcast.29, bf16[192,384]{1,0:T(8,128)(2,1)S(1)} %get-tuple-element.38.after), custom_call_target="tpu_custom_call" | custom-call | flops 3000000000 | bytes 5000000 | tf_op jit(solution)/shard_map/gelu_pool/pallas_call | solution.py:358
  42.0 0.1 collective-permute-done.6.dkv_in
  42.0 3.0 %att_join.1 = (bf16[8,96,768]{2,1,0:T(8,128)(2,1)}, bf16[384,288]{1,0:T(8,128)(2,1)S(1)}, bf16[384,288]{1,0:T(8,128)(2,1)S(1)}) custom-call(s32[1]{0:T(128)} %bitcast.1.core, bf16[384,192]{1,0:T(8,128)(2,1)} %get-tuple-element.36.dq_own, bf16[384,384]{1,0:T(8,128)(2,1)} %get-tuple-element.37.dkv_own, bf16[192,384]{1,0:T(8,128)(2,1)S(1)} %collective-permute-done.5.dq_in, ...), custom_call_target="tpu_custom_call" | custom-call | flops 10000000000 | bytes 3500000 | tf_op jit(solution)/shard_map/att_join/pallas_call | solution.py:272
  45.1 19.5 %all_to_all.15.parts.p0 = bf16[8,96,768]{2,1,0:T(8,128)(2,1)S(1)} all-to-all(bf16[8,96,768]{2,1,0:T(8,128)(2,1)} %get-tuple-element.41), channel_id=1, replica_groups=mesh['yh'=2,'core'=2,'yl'=2,'x'=4,'z'=4] {'yl','x'}, dimensions={0} | all-to-all | bytes 2359296 | tf_op jit(solution)/shard_map/all_to_all | solution.py:742
  64.6 4.3 %collective-permute-start.9 = (bf16[784,768]{1,0:T(8,128)(2,1)S(1)}, bf16[784,768]{1,0:T(8,128)(2,1)S(1)}, u32[]{:S(2)}, u32[]{:S(2)}) collective-permute-start(bf16[784,768]{1,0:T(8,128)(2,1)S(1)} %get-tuple-element.52.xp), channel_id=1, source_target_pairs={{0,32},{32,0},{1,33},{33,1},{2,34},{34,2},{3,35},{35,3},{4,36},{36... | collective-permute-start | bytes 3612680 | tf_op jit(solution)/shard_map/ppermute | solution.py:745
  68.9 0.0 collective-permute-start.11
  68.9 2.6 %pre_grads.1 = (bf16[768,768]{1,0:T(8,128)(2,1)}, bf16[768,384]{1,0:T(8,128)(2,1)S(1)}, bf16[768,384]{1,0:T(8,128)(2,1)S(1)}, f32[48,768]{1,0:T(8,128)}) custom-call(s32[1]{0:T(128)} %bitcast.1.core, bf16[8,96,768]{2,1,0:T(8,128)(2,1)S(1)} %all_to_all.15.parts.p0, bf16[768,768]{1,0:T(8,128)(2,1)} %bitcast.22, bf16[768,768]{1,0:T(8,128)(2,1)} %get-tuple-element.44.slope), custom_call_target="tpu_custom_call" | custom-call | flops 2949120 | bytes 6000000 | tf_op jit(solution)/shard_map/pre_grads/pallas_call | solution.py:446
  71.5 0.6 collective-permute-start.10
  72.1 0.1 collective-permute-start.12
  72.2 0.6 turn_input.2
  72.8 0.6 turn_input.3
  73.4 1.0 collective-permute-done.12.s1
  74.3 7.8 %weight_grads.1 = bf16[768,2304]{1,0:T(8,128)(2,1)} custom-call(bf16[768,768]{1,0:T(8,128)(2,1)S(1)} %get-tuple-element.53.xt0, bf16[768,512]{1,0:T(8,128)(2,1)S(1)} %get-tuple-element.54.al0, bf16[768,768]{1,0:T(8,128)(2,1)S(1)} %get-tuple-element.55.xt1, bf16[768,512]{1,0:T(8,128)(2,1)S(1)} %get-tuple-element.56.al1, ...), custom_call_target="tpu_custom_call" | custom-call | flops 4529848320 | bytes 10000000 | tf_op jit(solution)/shard_map/weight_grads/pallas_call | solution.py:523
  82.2 5.7 %all-to-all-start.2 = ((bf16[32,24,2304]{2,1,0:T(8,128)(2,1)}), bf16[32,24,2304]{2,1,0:T(8,128)(2,1)S(1)}, u32[]{:S(2)}, u32[]{:S(2)}) async-start(bf16[32,24,2304]{2,1,0:T(8,128)(2,1)} %bitcast.21), calls=%async_computation.2 | async-start | bytes 7077888 | tf_op jit(solution)/shard_map/all_to_all | solution.py:753
  87.9 9.1 %conv_adjoint.1 = (bf16[768,768]{1,0:T(8,128)(2,1)}, f32[8,768]{1,0:T(8,128)S(1)}, f32[8,768]{1,0:T(8,128)S(1)}, f32[8,768]{1,0:T(8,128)S(1)}, f32[8,768]{1,0:T(8,128)S(1)}) custom-call(s32[1]{0:T(128)} %bitcast.par, bf16[768,768]{1,0:T(8,128)(2,1)} %get-tuple-element.45.pre, bf16[5,768,768]{2,1,0:T(8,128)(2,1)} %w.3, bf16[768,768]{1,0:T(8,128)(2,1)} %bitcast.23, ...), custom_call_target="tpu_custom_call" | custom-call | flops 4529848320 | bytes 9500000 | tf_op jit(solution)/shard_map/conv_adjoint/pallas_call | solution.py:577
  97.0 0.6 copy-done.3
  97.6 0.6 copy-done.5
  98.2 1.2 collective-permute-start.7
  99.4 4.0 %collective-permute-start.8 = (f32[8,768]{1,0:T(8,128)S(1)}, f32[8,768]{1,0:T(8,128)}, u32[]{:S(2)}, u32[]{:S(2)}) collective-permute-start(f32[8,768]{1,0:T(8,128)S(1)} %get-tuple-element.51), channel_id=1, source_target_pairs={{1,2},{2,1},{3,4},{4,3},{5,6},{6,5},{7,8},{8,7},{9,10},{10,9},{11,... | collective-permute-start | bytes 73736 | tf_op jit(solution)/shard_map/ppermute | solution.py:757
  103.3 12.7 %collective-permute-done.7.got1.after = f32[8,768]{1,0:T(8,128)S(1)} collective-permute-done((f32[8,768]{1,0:T(8,128)S(1)}, f32[8,768]{1,0:T(8,128)S(1)}, u32[]{:S(2)}, u32[]{:S(2)}) %collective-permute-start.7) | collective-permute-done | bytes 24608 | tf_op jit(solution)/shard_map/ppermute | solution.py:756
  116.0 0.6 copy-done.1
  116.6 19.0 %collective-permute-done.8.got2.after2 = f32[8,768]{1,0:T(8,128)} collective-permute-done((f32[8,768]{1,0:T(8,128)S(1)}, f32[8,768]{1,0:T(8,128)}, u32[]{:S(2)}, u32[]{:S(2)}) %collective-permute-start.8) | collective-permute-done | bytes 24608 | tf_op jit(solution)/shard_map/ppermute | solution.py:757
  135.6 2.1 %all-to-all-done.2.parts = bf16[32,24,2304]{2,1,0:T(8,128)(2,1)S(1)} async-done(((bf16[32,24,2304]{2,1,0:T(8,128)(2,1)}), bf16[32,24,2304]{2,1,0:T(8,128)(2,1)S(1)}, u32[]{:S(2)}, u32[]{:S(2)}) %all-to-all-start.2) | async-done | bytes 3538976 | tf_op jit(solution)/shard_map/all_to_all | solution.py:753
  137.7 1.1 sum_partials.1.a
  138.7 2.7 %collective-permute-start.13 = (bf16[24,4224]{1,0:T(8,128)(2,1)S(1)}, bf16[24,4224]{1,0:T(8,128)(2,1)S(1)}, u32[]{:S(2)}, u32[]{:S(2)}) collective-permute-start(bf16[24,4224]{1,0:T(8,128)(2,1)S(1)} %sum_partials.1.a), channel_id=1, source_target_pairs={{0,64},{64,0},{1,65},{65,1},{2,66},{66,2},{3,67},{67,3},{4,68},{68... | collective-permute-start | bytes 608264 | tf_op jit(solution)/shard_map/ppermute | solution.py:760
  141.4 1.4 add_edges.1.after
  142.8 2.8 %collective-permute-done.13.b = bf16[24,4224]{1,0:T(8,128)(2,1)S(1)} collective-permute-done((bf16[24,4224]{1,0:T(8,128)(2,1)S(1)}, bf16[24,4224]{1,0:T(8,128)(2,1)S(1)}, u32[]{:S(2)}, u32[]{:S(2)}) %collective-permute-start.13) | collective-permute-done | bytes 202784 | tf_op jit(solution)/shard_map/ppermute | solution.py:760
  145.6 0.1 add_pair.1.mine
  145.7 2.2 %collective-permute-start.14 = (f32[24,4224]{1,0:T(8,128)S(1)}, f32[24,4224]{1,0:T(8,128)S(1)}, u32[]{:S(2)}, u32[]{:S(2)}) collective-permute-start(f32[24,4224]{1,0:T(8,128)S(1)} %add_pair.1.mine), channel_id=1, source_target_pairs={{0,32},{32,0},{1,33},{33,1},{2,34},{34,2},{3,35},{35,3},{4,36},{36... | collective-permute-start | bytes 1216520 | tf_op jit(solution)/shard_map/ppermute | solution.py:763
  147.9 1.4 collective-permute-done.14.other
  149.3 1.3 place.1
  (19 shorter events, 0.0 us)
Async XLA Ops:
  2.7 12.2 %copy-start = (bf16[8,48,768]{2,1,0:T(8,128)(2,1)S(1)}, bf16[8,48,768]{2,1,0:T(8,128)(2,1)}, u32[]{:S(2)}) copy-start(bf16[8,48,768]{2,1,0:T(8,128)(2,1)} %pack_heads.1.after) | copy-start | bytes 1769476
  2.7 15.3 %all-to-all-start = ((bf16[8,48,768]{2,1,0:T(8,128)(2,1)}), bf16[8,48,768]{2,1,0:T(8,128)(2,1)S(1)}, u32[]{:S(2)}, u32[]{:S(2)}) async-start(bf16[8,48,768]{2,1,0:T(8,128)(2,1)} %pack_heads.1.after), calls=%async_computation | async-start | bytes 1179648 | tf_op jit(solution)/shard_map/all_to_all | solution.py:723
  8.8 10.8 %collective-permute-start.3 = (bf16[2,768]{1,0:T(2,128)(2,1)S(1)}, bf16[2,768]{1,0:T(2,128)(2,1)S(1)}, u32[]{:S(2)}, u32[]{:S(2)}) collective-permute-start(bf16[2,768]{1,0:T(2,128)(2,1)S(1)} %get-tuple-element.63), channel_id=1, source_target_pairs={{1,2},{2,1},{3,4},{4,3},{5,6},{6,5},{7,8},{8,7},{9,10},{10,9},{11,... | collective-permute-start | bytes 9224 | tf_op jit(solution)/shard_map/ppermute | solution.py:732
  14.8 4.8 %collective-permute-start.2 = (bf16[2,768]{1,0:T(2,128)(2,1)S(1)}, bf16[2,768]{1,0:T(2,128)(2,1)S(1)}, u32[]{:S(2)}, u32[]{:S(2)}) collective-permute-start(bf16[2,768]{1,0:T(2,128)(2,1)S(1)} %get-tuple-element.64), channel_id=1, source_target_pairs={{0,1},{1,0},{2,3},{3,2},{4,5},{5,4},{6,7},{7,6},{8,9},{9,8},{10,11... | collective-permute-start | bytes 9224 | tf_op jit(solution)/shard_map/ppermute | solution.py:731
  18.0 10.1 %collective-permute-start.1 = (bf16[384,384]{1,0:T(8,128)(2,1)S(1)}, bf16[384,384]{1,0:T(8,128)(2,1)S(1)}, u32[]{:S(2)}, u32[]{:S(2)}) collective-permute-start(bf16[384,384]{1,0:T(8,128)(2,1)S(1)} %get-tuple-element.34), channel_id=1, source_target_pairs={{0,3},{3,0},{1,2},{2,1},{4,7},{7,4},{5,6},{6,5},{8,11},{11,8},{9,1... | collective-permute-start | bytes 884744 | tf_op jit(solution)/shard_map/ppermute | solution.py:727
  19.2 9.0 %collective-permute-start = (bf16[384,384]{1,0:T(8,128)(2,1)S(1)}, bf16[384,384]{1,0:T(8,128)(2,1)S(1)}, u32[]{:S(2)}, u32[]{:S(2)}) collective-permute-start(bf16[384,384]{1,0:T(8,128)(2,1)S(1)} %get-tuple-element.33.after), channel_id=1, source_target_pairs={{0,1},{1,0},{2,3},{3,2},{4,5},{5,4},{6,7},{7,6},{8,9},{9,8},{10,11... | collective-permute-start | bytes 884744 | tf_op jit(solution)/shard_map/ppermute | solution.py:726
  29.4 2.8 %collective-permute-start.4 = (f32[8,768]{1,0:T(8,128)S(1)}, f32[8,768]{1,0:T(8,128)S(1)}, u32[]{:S(2)}, u32[]{:S(2)}) collective-permute-start(f32[8,768]{1,0:T(8,128)S(1)} %att_stats.1.st), channel_id=1, source_target_pairs={{0,1},{1,0},{2,3},{3,2},{4,5},{5,4},{6,7},{7,6},{8,9},{9,8},{10,11... | collective-permute-start | bytes 73736 | tf_op jit(solution)/shard_map/ppermute | solution.py:736
  35.3 6.8 %collective-permute-start.6 = (bf16[384,384]{1,0:T(8,128)(2,1)S(1)}, bf16[384,384]{1,0:T(8,128)(2,1)S(1)}, u32[]{:S(2)}, u32[]{:S(2)}) collective-permute-start(bf16[384,384]{1,0:T(8,128)(2,1)S(1)} %get-tuple-element.39), channel_id=1, source_target_pairs={{0,3},{3,0},{1,2},{2,1},{4,7},{7,4},{5,6},{6,5},{8,11},{11,8},{9,1... | collective-permute-start | bytes 884744 | tf_op jit(solution)/shard_map/ppermute | solution.py:739
  37.2 4.7 %collective-permute-start.5 = (bf16[192,384]{1,0:T(8,128)(2,1)S(1)}, bf16[192,384]{1,0:T(8,128)(2,1)S(1)}, u32[]{:S(2)}, u32[]{:S(2)}) collective-permute-start(bf16[192,384]{1,0:T(8,128)(2,1)S(1)} %get-tuple-element.38.after), channel_id=1, source_target_pairs={{0,1},{1,0},{2,3},{3,2},{4,5},{5,4},{6,7},{7,6},{8,9},{9,8},{10,11... | collective-permute-start | bytes 442376 | tf_op jit(solution)/shard_map/ppermute | solution.py:738
  64.6 8.2 %collective-permute-start.9 = (bf16[784,768]{1,0:T(8,128)(2,1)S(1)}, bf16[784,768]{1,0:T(8,128)(2,1)S(1)}, u32[]{:S(2)}, u32[]{:S(2)}) collective-permute-start(bf16[784,768]{1,0:T(8,128)(2,1)S(1)} %get-tuple-element.52.xp), channel_id=1, source_target_pairs={{0,32},{32,0},{1,33},{33,1},{2,34},{34,2},{3,35},{35,3},{4,36},{36... | collective-permute-start | bytes 3612680 | tf_op jit(solution)/shard_map/ppermute | solution.py:745
  68.9 5.5 %collective-permute-start.11 = (bf16[8,96,768]{2,1,0:T(8,128)(2,1)S(1)}, bf16[8,96,768]{2,1,0:T(8,128)(2,1)S(1)}, u32[]{:S(2)}, u32[]{:S(2)}) collective-permute-start(bf16[8,96,768]{2,1,0:T(8,128)(2,1)S(1)} %all_to_all.15.parts.p0), channel_id=1, source_target_pairs={{0,32},{32,0},{1,33},{33,1},{2,34},{34,2},{3,35},{35,3},{4,36},{36... | collective-permute-start | bytes 3538952 | tf_op jit(solution)/shard_map/ppermute | solution.py:744
  71.5 2.8 %collective-permute-start.10 = (bf16[768,384]{1,0:T(8,128)(2,1)S(1)}, bf16[768,384]{1,0:T(8,128)(2,1)S(1)}, u32[]{:S(2)}, u32[]{:S(2)}) collective-permute-start(bf16[768,384]{1,0:T(8,128)(2,1)S(1)} %get-tuple-element.58), channel_id=1, source_target_pairs={{0,32},{32,0},{1,33},{33,1},{2,34},{34,2},{3,35},{35,3},{4,36},{36... | collective-permute-start | bytes 1769480 | tf_op jit(solution)/shard_map/ppermute | solution.py:751
  72.1 2.2 %collective-permute-start.12 = (bf16[384,288]{1,0:T(8,128)(2,1)S(1)}, bf16[384,288]{1,0:T(8,128)(2,1)S(1)}, u32[]{:S(2)}, u32[]{:S(2)}) collective-permute-start(bf16[384,288]{1,0:T(8,128)(2,1)S(1)} %get-tuple-element.60), channel_id=1, source_target_pairs={{0,32},{32,0},{1,33},{33,1},{2,34},{34,2},{3,35},{35,3},{4,36},{36... | collective-permute-start | bytes 663560 | tf_op jit(solution)/shard_map/ppermute | solution.py:746
  82.2 55.5 %all-to-all-start.2 = ((bf16[32,24,2304]{2,1,0:T(8,128)(2,1)}), bf16[32,24,2304]{2,1,0:T(8,128)(2,1)S(1)}, u32[]{:S(2)}, u32[]{:S(2)}) async-start(bf16[32,24,2304]{2,1,0:T(8,128)(2,1)} %bitcast.21), calls=%async_computation.2 | async-start | bytes 7077888 | tf_op jit(solution)/shard_map/all_to_all | solution.py:753
  96.9 0.6 copy-start.3
  97.6 0.6 copy-start.5
  98.2 17.8 %collective-permute-start.7 = (f32[8,768]{1,0:T(8,128)S(1)}, f32[8,768]{1,0:T(8,128)S(1)}, u32[]{:S(2)}, u32[]{:S(2)}) collective-permute-start(f32[8,768]{1,0:T(8,128)S(1)} %get-tuple-element.50), channel_id=1, source_target_pairs={{0,1},{1,0},{2,3},{3,2},{4,5},{5,4},{6,7},{7,6},{8,9},{9,8},{10,11... | collective-permute-start | bytes 73736 | tf_op jit(solution)/shard_map/ppermute | solution.py:756
  99.4 36.2 %collective-permute-start.8 = (f32[8,768]{1,0:T(8,128)S(1)}, f32[8,768]{1,0:T(8,128)}, u32[]{:S(2)}, u32[]{:S(2)}) collective-permute-start(f32[8,768]{1,0:T(8,128)S(1)} %get-tuple-element.51), channel_id=1, source_target_pairs={{1,2},{2,1},{3,4},{4,3},{5,6},{6,5},{7,8},{8,7},{9,10},{10,9},{11,... | collective-permute-start | bytes 73736 | tf_op jit(solution)/shard_map/ppermute | solution.py:757
  116.0 0.6 copy-start.1
  137.7 3.8 %copy-start.2 = (f32[8,768]{1,0:T(8,128)S(1)}, f32[8,768]{1,0:T(8,128)}, u32[]{:S(2)}) copy-start(f32[8,768]{1,0:T(8,128)} %copy-done.1) | copy-start | bytes 73732
  137.7 3.8 %copy-start.4 = (f32[8,768]{1,0:T(8,128)S(1)}, f32[8,768]{1,0:T(8,128)}, u32[]{:S(2)}) copy-start(f32[8,768]{1,0:T(8,128)} %copy-done.3) | copy-start | bytes 73732
  137.7 3.8 %copy-start.6 = (f32[8,768]{1,0:T(8,128)S(1)}, f32[8,768]{1,0:T(8,128)}, u32[]{:S(2)}) copy-start(f32[8,768]{1,0:T(8,128)} %copy-done.5) | copy-start | bytes 73732
  138.7 6.9 %collective-permute-start.13 = (bf16[24,4224]{1,0:T(8,128)(2,1)S(1)}, bf16[24,4224]{1,0:T(8,128)(2,1)S(1)}, u32[]{:S(2)}, u32[]{:S(2)}) collective-permute-start(bf16[24,4224]{1,0:T(8,128)(2,1)S(1)} %sum_partials.1.a), channel_id=1, source_target_pairs={{0,64},{64,0},{1,65},{65,1},{2,66},{66,2},{3,67},{67,3},{4,68},{68... | collective-permute-start | bytes 608264 | tf_op jit(solution)/shard_map/ppermute | solution.py:760
  145.7 3.6 %collective-permute-start.14 = (f32[24,4224]{1,0:T(8,128)S(1)}, f32[24,4224]{1,0:T(8,128)S(1)}, u32[]{:S(2)}, u32[]{:S(2)}) collective-permute-start(f32[24,4224]{1,0:T(8,128)S(1)} %add_pair.1.mine), channel_id=1, source_target_pairs={{0,32},{32,0},{1,33},{33,1},{2,34},{34,2},{3,35},{35,3},{4,36},{36... | collective-permute-start | bytes 1216520 | tf_op jit(solution)/shard_map/ppermute | solution.py:763

commit v8 on v7

--- a/solution.py
+++ b/solution.py
@@ -247,9 +247,9 @@
     dkv = (dkv_own[...].astype(F32) + dkv_in[...].astype(F32)).astype(BF)
     qkv = jnp.concatenate([dq, dkv], axis=1)
     stores = []
-    for r in range(0, BLK, 2 * ATT):
-        made[r : r + 2 * ATT, :] = mm(qkv[r : r + 2 * ATT], wh[...]).astype(BF)
-        for h in (r // ATT, r // ATT + 1):
+    for r in range(0, BLK, 4 * ATT):
+        made[r : r + 4 * ATT, :] = mm(qkv[r : r + 4 * ATT], wh[...]).astype(BF)
+        for h in range(r // ATT, r // ATT + 4):
             rows = pl.ds(h * ATT, ATT)
             stores.append(pltpu.make_async_copy(made.at[rows], pool.at[h, pl.ds(0, ATT)], sems.at[h]))
             stores[-1].start()

time: 151 us -> 151 us (level)
  no operation moved by 1% of the time
where the time goes in v8:
time: 151 us
  Pallas kernels  50.1 us (33%)
  waiting for transfers between devices  40.9 us (27%)
  starting transfers between devices  36.6 us (24%)
  blocking collectives  19.5 us (13%)
  local copies, waits for them, and re-layouts  1.84 us (1%)
    all_to_all x1, blocking collectives, local(): parts = lax.all_to_all(pool_part, HAX, 0, 0, tiled=True)  19.5 us
    ppermute x1, waiting for transfers between devices, local(): rim2 = lax.ppermute(next_, SEQ, NEXT)  19.2 us
    ppermute x1, waiting for transfers between devices, local(): rim1 = lax.ppermute(near, SEQ, NEAR)  12.7 us
    pallas_call x1, Pallas kernels, conv_adjoint(): pl.pallas_call(adjoint_kernel, grid=(TAPS,), out_shape=(far((ROWS, C), BF...  9.08 us
    pallas_call x1, Pallas kernels, conv_apply(): pl.pallas_call(conv_kernel, out_shape=(far((ROWS, C), F32), sds((ROWS + 1...  8.53 us
    pallas_call x1, Pallas kernels, weight_grads(): pl.pallas_call(weights_kernel, out_shape=far((C, 2304), BF), in_specs=[VM...  7.82 us
    ppermute x1, starting transfers between devices, local(): got2 = lax.ppermute(jnp.where(par[0] == 0, head_rows, tail_rows), SEQ, NEXT)  5.96 us
    all_to_all x1, starting transfers between devices, local(): got = lax.all_to_all(terms.reshape(32, 24, 2304), SEQ, 0, 0, tiled=True)  5.49 us
  transfers between devices with their start and end apart: 17, of which 8 were waited for; matrix products, arithmetic and copies ran while one was open for 0% of the time, Pallas kernels for 20%

profile of v8, /device:TPU:7, one launch (start us, length us, event | category | flops | bytes accessed | tf_op | source)
XLA Modules:
  0.0 150.5 jit_solution(7364748063191080226)
XLA Ops:
  0.6 2.1 %pack_heads.1.after = bf16[8,48,768]{2,1,0:T(8,128)(2,1)} custom-call(bf16[48,1536]{1,0:T(8,128)(2,1)} %bitcast.24, bf16[48,1536]{1,0:T(8,128)(2,1)} %bitcast.25, bf16[48,1536]{1,0:T(8,128)(2,1)} %bitcast.26, bf16[48,1536]{1,0:T(8,128)(2,1)} %bitcast.27), custom_call_target="tpu_custom_call" | custom-call | bytes 1200000 | tf_op jit(solution)/shard_map/pack_heads/pallas_call | solution.py:94
  2.7 0.0 copy-start
  2.7 5.4 %all-to-all-start = ((bf16[8,48,768]{2,1,0:T(8,128)(2,1)}), bf16[8,48,768]{2,1,0:T(8,128)(2,1)S(1)}, u32[]{:S(2)}, u32[]{:S(2)}) async-start(bf16[8,48,768]{2,1,0:T(8,128)(2,1)} %pack_heads.1.after), calls=%async_computation | async-start | bytes 1179648 | tf_op jit(solution)/shard_map/all_to_all | solution.py:723
  8.1 0.7 fusion.1
  8.8 6.0 %collective-permute-start.3 = (bf16[2,768]{1,0:T(2,128)(2,1)S(1)}, bf16[2,768]{1,0:T(2,128)(2,1)S(1)}, u32[]{:S(2)}, u32[]{:S(2)}) collective-permute-start(bf16[2,768]{1,0:T(2,128)(2,1)S(1)} %get-tuple-element.63), channel_id=1, source_target_pairs={{1,2},{2,1},{3,4},{4,3},{5,6},{6,5},{7,8},{8,7},{9,10},{10,9},{11,... | collective-permute-start | bytes 9224 | tf_op jit(solution)/shard_map/ppermute | solution.py:732
  14.8 0.1 collective-permute-start.2
  14.9 3.1 %head_weights.1.after.wh = bf16[576,768]{1,0:T(8,128)(2,1)} custom-call(s32[1]{0:T(128)} %bitcast.7.pair, s32[1]{0:T(128)} %bitcast.8.odd, bf16[768,4608]{1,0:T(8,128)(2,1)} %wv.1, bf16[768,4608]{1,0:T(8,128)(2,1)} %wv.1, bf16[768,4608]{1,0:T(8,128)(2,1)} %wv.1, bf16[8,48,768]{2,1,0:T(8,128)(2,1)S(1)} %copy-done), custom_call_target="tpu_custom_call" | custom-call | bytes 3000000 | tf_op jit(solution)/shard_map/head_weights/pallas_call | solution.py:224
  18.0 0.1 split_own.1
  18.0 1.1 collective-permute-start.1
  19.2 0.5 collective-permute-start
  19.6 8.5 %conv_apply.1 = (f32[768,768]{1,0:T(8,128)}, bf16[784,768]{1,0:T(8,128)(2,1)S(1)}) custom-call(s32[1]{0:T(128)} %bitcast.par, bf16[768,768]{1,0:T(8,128)(2,1)} %bitcast.28, bf16[2,768]{1,0:T(2,128)(2,1)S(1)} %collective-permute-done.2.got1, bf16[2,768]{1,0:T(2,128)(2,1)S(1)} %collective-permute-done.3.got2, bf16[5,768,768]{2,1,0:T(8,128)(2,1)} %w.3, ...), custom_call_target="tpu_custom_call" | custom-call | flops 4529848320 | bytes 9500000 | tf_op jit(solution)/shard_map/conv_apply/pallas_call | solution.py:326
  28.2 1.2 att_stats.1.st
  29.4 1.1 collective-permute-start.4
  30.4 1.7 %collective-permute-done.4.st2 = f32[8,768]{1,0:T(8,128)S(1)} collective-permute-done((f32[8,768]{1,0:T(8,128)S(1)}, f32[8,768]{1,0:T(8,128)S(1)}, u32[]{:S(2)}, u32[]{:S(2)}) %collective-permute-start.4) | collective-permute-done | bytes 24608 | tf_op jit(solution)/shard_map/ppermute | solution.py:736
  32.1 3.1 %att_grads.1 = (bf16[384,192]{1,0:T(8,128)(2,1)}, bf16[192,384]{1,0:T(8,128)(2,1)S(1)}, bf16[384,384]{1,0:T(8,128)(2,1)}, bf16[384,384]{1,0:T(8,128)(2,1)S(1)}) custom-call(bf16[384,768]{1,0:T(8,128)(2,1)S(1)} %bitcast.19, bf16[384,384]{1,0:T(8,128)(2,1)S(1)} %collective-permute-done.qg, bf16[384,384]{1,0:T(8,128)(2,1)S(1)} %collective-permute-done.1.kv, ...), custom_call_target="tpu_custom_call" | custom-call | flops 20000000000 | bytes 3000000 | tf_op jit(solution)/shard_map/att_grads/pallas_call | solution.py:177
  35.3 2.0 %collective-permute-start.6 = (bf16[384,384]{1,0:T(8,128)(2,1)S(1)}, bf16[384,384]{1,0:T(8,128)(2,1)S(1)}, u32[]{:S(2)}, u32[]{:S(2)}) collective-permute-start(bf16[384,384]{1,0:T(8,128)(2,1)S(1)} %get-tuple-element.39), channel_id=1, source_target_pairs={{0,3},{3,0},{1,2},{2,1},{4,7},{7,4},{5,6},{6,5},{8,11},{11,8},{9,1... | collective-permute-start | bytes 884744 | tf_op jit(solution)/shard_map/ppermute | solution.py:739
  37.2 0.0 collective-permute-start.5
  37.3 4.7 %gelu_pool.1 = (bf16[768,768]{1,0:T(8,128)(2,1)}, bf16[48,768]{1,0:T(8,128)(2,1)}) custom-call(f32[768,768]{1,0:T(8,128)} %get-tuple-element.35.after.pre, bf16[768,768]{1,0:T(8,128)(2,1)} %bitcast.29, bf16[192,384]{1,0:T(8,128)(2,1)S(1)} %get-tuple-element.38.after), custom_call_target="tpu_custom_call" | custom-call | flops 3000000000 | bytes 5000000 | tf_op jit(solution)/shard_map/gelu_pool/pallas_call | solution.py:358
  42.0 0.1 collective-permute-done.6.dkv_in
  42.0 2.9 %att_join.1 = (bf16[8,96,768]{2,1,0:T(8,128)(2,1)}, bf16[384,288]{1,0:T(8,128)(2,1)S(1)}, bf16[384,288]{1,0:T(8,128)(2,1)S(1)}) custom-call(s32[1]{0:T(128)} %bitcast.1.core, bf16[384,192]{1,0:T(8,128)(2,1)} %get-tuple-element.36.dq_own, bf16[384,384]{1,0:T(8,128)(2,1)} %get-tuple-element.37.dkv_own, bf16[192,384]{1,0:T(8,128)(2,1)S(1)} %collective-permute-done.5.dq_in, ...), custom_call_target="tpu_custom_call" | custom-call | flops 10000000000 | bytes 3500000 | tf_op jit(solution)/shard_map/att_join/pallas_call | solution.py:272
  45.0 19.5 %all_to_all.15.parts.p0 = bf16[8,96,768]{2,1,0:T(8,128)(2,1)S(1)} all-to-all(bf16[8,96,768]{2,1,0:T(8,128)(2,1)} %get-tuple-element.41), channel_id=1, replica_groups=mesh['yh'=2,'core'=2,'yl'=2,'x'=4,'z'=4] {'yl','x'}, dimensions={0} | all-to-all | bytes 2359296 | tf_op jit(solution)/shard_map/all_to_all | solution.py:742
  64.5 4.3 %collective-permute-start.9 = (bf16[784,768]{1,0:T(8,128)(2,1)S(1)}, bf16[784,768]{1,0:T(8,128)(2,1)S(1)}, u32[]{:S(2)}, u32[]{:S(2)}) collective-permute-start(bf16[784,768]{1,0:T(8,128)(2,1)S(1)} %get-tuple-element.52.xp), channel_id=1, source_target_pairs={{0,32},{32,0},{1,33},{33,1},{2,34},{34,2},{3,35},{35,3},{4,36},{36... | collective-permute-start | bytes 3612680 | tf_op jit(solution)/shard_map/ppermute | solution.py:745
  68.8 0.0 collective-permute-start.11
  68.8 2.6 %pre_grads.1 = (bf16[768,768]{1,0:T(8,128)(2,1)}, bf16[768,384]{1,0:T(8,128)(2,1)S(1)}, bf16[768,384]{1,0:T(8,128)(2,1)S(1)}, f32[48,768]{1,0:T(8,128)}) custom-call(s32[1]{0:T(128)} %bitcast.1.core, bf16[8,96,768]{2,1,0:T(8,128)(2,1)S(1)} %all_to_all.15.parts.p0, bf16[768,768]{1,0:T(8,128)(2,1)} %bitcast.22, bf16[768,768]{1,0:T(8,128)(2,1)} %get-tuple-element.44.slope), custom_call_target="tpu_custom_call" | custom-call | flops 2949120 | bytes 6000000 | tf_op jit(solution)/shard_map/pre_grads/pallas_call | solution.py:446
  71.4 0.6 collective-permute-start.10
  72.0 0.1 collective-permute-start.12
  72.1 0.6 turn_input.2
  72.7 0.6 turn_input.3
  73.3 1.0 collective-permute-done.12.s1
  74.2 7.8 %weight_grads.1 = bf16[768,2304]{1,0:T(8,128)(2,1)} custom-call(bf16[768,768]{1,0:T(8,128)(2,1)S(1)} %get-tuple-element.53.xt0, bf16[768,512]{1,0:T(8,128)(2,1)S(1)} %get-tuple-element.54.al0, bf16[768,768]{1,0:T(8,128)(2,1)S(1)} %get-tuple-element.55.xt1, bf16[768,512]{1,0:T(8,128)(2,1)S(1)} %get-tuple-element.56.al1, ...), custom_call_target="tpu_custom_call" | custom-call | flops 4529848320 | bytes 10000000 | tf_op jit(solution)/shard_map/weight_grads/pallas_call | solution.py:523
  82.0 5.5 %all-to-all-start.2 = ((bf16[32,24,2304]{2,1,0:T(8,128)(2,1)}), bf16[32,24,2304]{2,1,0:T(8,128)(2,1)S(1)}, u32[]{:S(2)}, u32[]{:S(2)}) async-start(bf16[32,24,2304]{2,1,0:T(8,128)(2,1)} %bitcast.21), calls=%async_computation.2 | async-start | bytes 7077888 | tf_op jit(solution)/shard_map/all_to_all | solution.py:753
  87.6 9.1 %conv_adjoint.1 = (bf16[768,768]{1,0:T(8,128)(2,1)}, f32[8,768]{1,0:T(8,128)S(1)}, f32[8,768]{1,0:T(8,128)S(1)}, f32[8,768]{1,0:T(8,128)S(1)}, f32[8,768]{1,0:T(8,128)S(1)}) custom-call(s32[1]{0:T(128)} %bitcast.par, bf16[768,768]{1,0:T(8,128)(2,1)} %get-tuple-element.45.pre, bf16[5,768,768]{2,1,0:T(8,128)(2,1)} %w.3, bf16[768,768]{1,0:T(8,128)(2,1)} %bitcast.23, ...), custom_call_target="tpu_custom_call" | custom-call | flops 4529848320 | bytes 9500000 | tf_op jit(solution)/shard_map/conv_adjoint/pallas_call | solution.py:577
  96.6 0.6 copy-done.3
  97.2 0.6 copy-done.5
  97.8 1.2 collective-permute-start.7
  99.0 3.9 %collective-permute-start.8 = (f32[8,768]{1,0:T(8,128)S(1)}, f32[8,768]{1,0:T(8,128)}, u32[]{:S(2)}, u32[]{:S(2)}) collective-permute-start(f32[8,768]{1,0:T(8,128)S(1)} %get-tuple-element.51), channel_id=1, source_target_pairs={{1,2},{2,1},{3,4},{4,3},{5,6},{6,5},{7,8},{8,7},{9,10},{10,9},{11,... | collective-permute-start | bytes 73736 | tf_op jit(solution)/shard_map/ppermute | solution.py:757
  103.0 12.7 %collective-permute-done.7.got1.after = f32[8,768]{1,0:T(8,128)S(1)} collective-permute-done((f32[8,768]{1,0:T(8,128)S(1)}, f32[8,768]{1,0:T(8,128)S(1)}, u32[]{:S(2)}, u32[]{:S(2)}) %collective-permute-start.7) | collective-permute-done | bytes 24608 | tf_op jit(solution)/shard_map/ppermute | solution.py:756
  115.7 0.6 copy-done.1
  116.3 19.2 %collective-permute-done.8.got2.after2 = f32[8,768]{1,0:T(8,128)} collective-permute-done((f32[8,768]{1,0:T(8,128)S(1)}, f32[8,768]{1,0:T(8,128)}, u32[]{:S(2)}, u32[]{:S(2)}) %collective-permute-start.8) | collective-permute-done | bytes 24608 | tf_op jit(solution)/shard_map/ppermute | solution.py:757
  135.4 2.2 %all-to-all-done.2.parts = bf16[32,24,2304]{2,1,0:T(8,128)(2,1)S(1)} async-done(((bf16[32,24,2304]{2,1,0:T(8,128)(2,1)}), bf16[32,24,2304]{2,1,0:T(8,128)(2,1)S(1)}, u32[]{:S(2)}, u32[]{:S(2)}) %all-to-all-start.2) | async-done | bytes 3538976 | tf_op jit(solution)/shard_map/all_to_all | solution.py:753
  137.6 1.1 sum_partials.1.a
  138.7 2.7 %collective-permute-start.13 = (bf16[24,4224]{1,0:T(8,128)(2,1)S(1)}, bf16[24,4224]{1,0:T(8,128)(2,1)S(1)}, u32[]{:S(2)}, u32[]{:S(2)}) collective-permute-start(bf16[24,4224]{1,0:T(8,128)(2,1)S(1)} %sum_partials.1.a), channel_id=1, source_target_pairs={{0,64},{64,0},{1,65},{65,1},{2,66},{66,2},{3,67},{67,3},{4,68},{68... | collective-permute-start | bytes 608264 | tf_op jit(solution)/shard_map/ppermute | solution.py:760
  141.4 1.4 add_edges.1.after
  142.8 2.8 %collective-permute-done.13.b = bf16[24,4224]{1,0:T(8,128)(2,1)S(1)} collective-permute-done((bf16[24,4224]{1,0:T(8,128)(2,1)S(1)}, bf16[24,4224]{1,0:T(8,128)(2,1)S(1)}, u32[]{:S(2)}, u32[]{:S(2)}) %collective-permute-start.13) | collective-permute-done | bytes 202784 | tf_op jit(solution)/shard_map/ppermute | solution.py:760
  145.6 0.1 add_pair.1.mine
  145.7 2.2 %collective-permute-start.14 = (f32[24,4224]{1,0:T(8,128)S(1)}, f32[24,4224]{1,0:T(8,128)S(1)}, u32[]{:S(2)}, u32[]{:S(2)}) collective-permute-start(f32[24,4224]{1,0:T(8,128)S(1)} %add_pair.1.mine), channel_id=1, source_target_pairs={{0,32},{32,0},{1,33},{33,1},{2,34},{34,2},{3,35},{35,3},{4,36},{36... | collective-permute-start | bytes 1216520 | tf_op jit(solution)/shard_map/ppermute | solution.py:763
  147.9 1.4 collective-permute-done.14.other
  149.3 1.3 place.1
  (19 shorter events, 0.0 us)
Async XLA Ops:
  2.7 12.2 %copy-start = (bf16[8,48,768]{2,1,0:T(8,128)(2,1)S(1)}, bf16[8,48,768]{2,1,0:T(8,128)(2,1)}, u32[]{:S(2)}) copy-start(bf16[8,48,768]{2,1,0:T(8,128)(2,1)} %pack_heads.1.after) | copy-start | bytes 1769476
  2.7 15.3 %all-to-all-start = ((bf16[8,48,768]{2,1,0:T(8,128)(2,1)}), bf16[8,48,768]{2,1,0:T(8,128)(2,1)S(1)}, u32[]{:S(2)}, u32[]{:S(2)}) async-start(bf16[8,48,768]{2,1,0:T(8,128)(2,1)} %pack_heads.1.after), calls=%async_computation | async-start | bytes 1179648 | tf_op jit(solution)/shard_map/all_to_all | solution.py:723
  8.8 10.8 %collective-permute-start.3 = (bf16[2,768]{1,0:T(2,128)(2,1)S(1)}, bf16[2,768]{1,0:T(2,128)(2,1)S(1)}, u32[]{:S(2)}, u32[]{:S(2)}) collective-permute-start(bf16[2,768]{1,0:T(2,128)(2,1)S(1)} %get-tuple-element.63), channel_id=1, source_target_pairs={{1,2},{2,1},{3,4},{4,3},{5,6},{6,5},{7,8},{8,7},{9,10},{10,9},{11,... | collective-permute-start | bytes 9224 | tf_op jit(solution)/shard_map/ppermute | solution.py:732
  14.8 4.8 %collective-permute-start.2 = (bf16[2,768]{1,0:T(2,128)(2,1)S(1)}, bf16[2,768]{1,0:T(2,128)(2,1)S(1)}, u32[]{:S(2)}, u32[]{:S(2)}) collective-permute-start(bf16[2,768]{1,0:T(2,128)(2,1)S(1)} %get-tuple-element.64), channel_id=1, source_target_pairs={{0,1},{1,0},{2,3},{3,2},{4,5},{5,4},{6,7},{7,6},{8,9},{9,8},{10,11... | collective-permute-start | bytes 9224 | tf_op jit(solution)/shard_map/ppermute | solution.py:731
  18.0 10.1 %collective-permute-start.1 = (bf16[384,384]{1,0:T(8,128)(2,1)S(1)}, bf16[384,384]{1,0:T(8,128)(2,1)S(1)}, u32[]{:S(2)}, u32[]{:S(2)}) collective-permute-start(bf16[384,384]{1,0:T(8,128)(2,1)S(1)} %get-tuple-element.34), channel_id=1, source_target_pairs={{0,3},{3,0},{1,2},{2,1},{4,7},{7,4},{5,6},{6,5},{8,11},{11,8},{9,1... | collective-permute-start | bytes 884744 | tf_op jit(solution)/shard_map/ppermute | solution.py:727
  19.2 9.0 %collective-permute-start = (bf16[384,384]{1,0:T(8,128)(2,1)S(1)}, bf16[384,384]{1,0:T(8,128)(2,1)S(1)}, u32[]{:S(2)}, u32[]{:S(2)}) collective-permute-start(bf16[384,384]{1,0:T(8,128)(2,1)S(1)} %get-tuple-element.33.after), channel_id=1, source_target_pairs={{0,1},{1,0},{2,3},{3,2},{4,5},{5,4},{6,7},{7,6},{8,9},{9,8},{10,11... | collective-permute-start | bytes 884744 | tf_op jit(solution)/shard_map/ppermute | solution.py:726
  29.4 2.8 %collective-permute-start.4 = (f32[8,768]{1,0:T(8,128)S(1)}, f32[8,768]{1,0:T(8,128)S(1)}, u32[]{:S(2)}, u32[]{:S(2)}) collective-permute-start(f32[8,768]{1,0:T(8,128)S(1)} %att_stats.1.st), channel_id=1, source_target_pairs={{0,1},{1,0},{2,3},{3,2},{4,5},{5,4},{6,7},{7,6},{8,9},{9,8},{10,11... | collective-permute-start | bytes 73736 | tf_op jit(solution)/shard_map/ppermute | solution.py:736
  35.3 6.8 %collective-permute-start.6 = (bf16[384,384]{1,0:T(8,128)(2,1)S(1)}, bf16[384,384]{1,0:T(8,128)(2,1)S(1)}, u32[]{:S(2)}, u32[]{:S(2)}) collective-permute-start(bf16[384,384]{1,0:T(8,128)(2,1)S(1)} %get-tuple-element.39), channel_id=1, source_target_pairs={{0,3},{3,0},{1,2},{2,1},{4,7},{7,4},{5,6},{6,5},{8,11},{11,8},{9,1... | collective-permute-start | bytes 884744 | tf_op jit(solution)/shard_map/ppermute | solution.py:739
  37.2 4.7 %collective-permute-start.5 = (bf16[192,384]{1,0:T(8,128)(2,1)S(1)}, bf16[192,384]{1,0:T(8,128)(2,1)S(1)}, u32[]{:S(2)}, u32[]{:S(2)}) collective-permute-start(bf16[192,384]{1,0:T(8,128)(2,1)S(1)} %get-tuple-element.38.after), channel_id=1, source_target_pairs={{0,1},{1,0},{2,3},{3,2},{4,5},{5,4},{6,7},{7,6},{8,9},{9,8},{10,11... | collective-permute-start | bytes 442376 | tf_op jit(solution)/shard_map/ppermute | solution.py:738
  64.5 8.2 %collective-permute-start.9 = (bf16[784,768]{1,0:T(8,128)(2,1)S(1)}, bf16[784,768]{1,0:T(8,128)(2,1)S(1)}, u32[]{:S(2)}, u32[]{:S(2)}) collective-permute-start(bf16[784,768]{1,0:T(8,128)(2,1)S(1)} %get-tuple-element.52.xp), channel_id=1, source_target_pairs={{0,32},{32,0},{1,33},{33,1},{2,34},{34,2},{3,35},{35,3},{4,36},{36... | collective-permute-start | bytes 3612680 | tf_op jit(solution)/shard_map/ppermute | solution.py:745
  68.8 5.5 %collective-permute-start.11 = (bf16[8,96,768]{2,1,0:T(8,128)(2,1)S(1)}, bf16[8,96,768]{2,1,0:T(8,128)(2,1)S(1)}, u32[]{:S(2)}, u32[]{:S(2)}) collective-permute-start(bf16[8,96,768]{2,1,0:T(8,128)(2,1)S(1)} %all_to_all.15.parts.p0), channel_id=1, source_target_pairs={{0,32},{32,0},{1,33},{33,1},{2,34},{34,2},{3,35},{35,3},{4,36},{36... | collective-permute-start | bytes 3538952 | tf_op jit(solution)/shard_map/ppermute | solution.py:744
  71.4 2.8 %collective-permute-start.10 = (bf16[768,384]{1,0:T(8,128)(2,1)S(1)}, bf16[768,384]{1,0:T(8,128)(2,1)S(1)}, u32[]{:S(2)}, u32[]{:S(2)}) collective-permute-start(bf16[768,384]{1,0:T(8,128)(2,1)S(1)} %get-tuple-element.58), channel_id=1, source_target_pairs={{0,32},{32,0},{1,33},{33,1},{2,34},{34,2},{3,35},{35,3},{4,36},{36... | collective-permute-start | bytes 1769480 | tf_op jit(solution)/shard_map/ppermute | solution.py:751
  72.0 2.2 %collective-permute-start.12 = (bf16[384,288]{1,0:T(8,128)(2,1)S(1)}, bf16[384,288]{1,0:T(8,128)(2,1)S(1)}, u32[]{:S(2)}, u32[]{:S(2)}) collective-permute-start(bf16[384,288]{1,0:T(8,128)(2,1)S(1)} %get-tuple-element.60), channel_id=1, source_target_pairs={{0,32},{32,0},{1,33},{33,1},{2,34},{34,2},{3,35},{35,3},{4,36},{36... | collective-permute-start | bytes 663560 | tf_op jit(solution)/shard_map/ppermute | solution.py:746
  82.0 55.6 %all-to-all-start.2 = ((bf16[32,24,2304]{2,1,0:T(8,128)(2,1)}), bf16[32,24,2304]{2,1,0:T(8,128)(2,1)S(1)}, u32[]{:S(2)}, u32[]{:S(2)}) async-start(bf16[32,24,2304]{2,1,0:T(8,128)(2,1)} %bitcast.21), calls=%async_computation.2 | async-start | bytes 7077888 | tf_op jit(solution)/shard_map/all_to_all | solution.py:753
  96.6 0.6 copy-start.3
  97.2 0.6 copy-start.5
  97.8 17.8 %collective-permute-start.7 = (f32[8,768]{1,0:T(8,128)S(1)}, f32[8,768]{1,0:T(8,128)S(1)}, u32[]{:S(2)}, u32[]{:S(2)}) collective-permute-start(f32[8,768]{1,0:T(8,128)S(1)} %get-tuple-element.50), channel_id=1, source_target_pairs={{0,1},{1,0},{2,3},{3,2},{4,5},{5,4},{6,7},{7,6},{8,9},{9,8},{10,11... | collective-permute-start | bytes 73736 | tf_op jit(solution)/shard_map/ppermute | solution.py:756
  99.0 36.4 %collective-permute-start.8 = (f32[8,768]{1,0:T(8,128)S(1)}, f32[8,768]{1,0:T(8,128)}, u32[]{:S(2)}, u32[]{:S(2)}) collective-permute-start(f32[8,768]{1,0:T(8,128)S(1)} %get-tuple-element.51), channel_id=1, source_target_pairs={{1,2},{2,1},{3,4},{4,3},{5,6},{6,5},{7,8},{8,7},{9,10},{10,9},{11,... | collective-permute-start | bytes 73736 | tf_op jit(solution)/shard_map/ppermute | solution.py:757
  115.7 0.6 copy-start.1
  137.6 3.8 %copy-start.2 = (f32[8,768]{1,0:T(8,128)S(1)}, f32[8,768]{1,0:T(8,128)}, u32[]{:S(2)}) copy-start(f32[8,768]{1,0:T(8,128)} %copy-done.1) | copy-start | bytes 73732
  137.6 3.8 %copy-start.4 = (f32[8,768]{1,0:T(8,128)S(1)}, f32[8,768]{1,0:T(8,128)}, u32[]{:S(2)}) copy-start(f32[8,768]{1,0:T(8,128)} %copy-done.3) | copy-start | bytes 73732
  137.6 3.8 %copy-start.6 = (f32[8,768]{1,0:T(8,128)S(1)}, f32[8,768]{1,0:T(8,128)}, u32[]{:S(2)}) copy-start(f32[8,768]{1,0:T(8,128)} %copy-done.5) | copy-start | bytes 73732
  138.7 6.9 %collective-permute-start.13 = (bf16[24,4224]{1,0:T(8,128)(2,1)S(1)}, bf16[24,4224]{1,0:T(8,128)(2,1)S(1)}, u32[]{:S(2)}, u32[]{:S(2)}) collective-permute-start(bf16[24,4224]{1,0:T(8,128)(2,1)S(1)} %sum_partials.1.a), channel_id=1, source_target_pairs={{0,64},{64,0},{1,65},{65,1},{2,66},{66,2},{3,67},{67,3},{4,68},{68... | collective-permute-start | bytes 608264 | tf_op jit(solution)/shard_map/ppermute | solution.py:760
  145.7 3.6 %collective-permute-start.14 = (f32[24,4224]{1,0:T(8,128)S(1)}, f32[24,4224]{1,0:T(8,128)S(1)}, u32[]{:S(2)}, u32[]{:S(2)}) collective-permute-start(f32[24,4224]{1,0:T(8,128)S(1)} %add_pair.1.mine), channel_id=1, source_target_pairs={{0,32},{32,0},{1,33},{33,1},{2,34},{34,2},{3,35},{35,3},{4,36},{36... | collective-permute-start | bytes 1216520 | tf_op jit(solution)/shard_map/ppermute | solution.py:763
